TPU v7x, 32 devices: a whole 2x2x4 slice. The times are simulated.
32 devices in a mesh: frame: 4 (over y, x), pos: 8 (over z, core).
Axes of the slice: x: 2, y: 2, z: 4, core: 2. Of those that a mesh axis runs over, the one named last changes fastest.
Arguments:
- tokens: bfloat16 [4, 48, 56, 768], P(None, 'frame', 'pos'), may hold values from -6 to 6
- class_tokens: bfloat16 [4, 3, 768], replicated, may hold values from -6 to 6
- clip_frames: int32 [4, 3], replicated, may hold values from 5 to 38, as said below
- cotangent: bfloat16 [4, 48, 56, 768], P(None, 'frame', 'pos'), may hold values from -6 to 6
- temporal_qkv: bfloat16 [768, 2304], P(('frame', 'pos')), may hold values from -0.21875 to 0.21875
- temporal_proj: bfloat16 [768, 768], P(('frame', 'pos')), may hold values from -1.25 to 1.25
- temporal_fc: bfloat16 [768, 768], P(('frame', 'pos')), may hold values from -0.21875 to 0.21875
- spatial_qkv: bfloat16 [768, 2304], P(('frame', 'pos')), may hold values from -0.21875 to 0.21875
- spatial_proj: bfloat16 [768, 768], P(('frame', 'pos')), may hold values from -1.75 to 1.75
- mlp_in: bfloat16 [768, 3072], P(('frame', 'pos')), may hold values from -0.21875 to 0.21875
- mlp_out: bfloat16 [3072, 768], P(('frame', 'pos')), may hold values from -0.109375 to 0.109375
- mlp_in_bias: bfloat16 [3072], P(('frame', 'pos')), may hold values from -2 to 2
- norm_gains: bfloat16 [768, 3], P(('frame', 'pos')), may hold values from 0.5 to 1.5
- norm_shifts: bfloat16 [768, 3], P(('frame', 'pos')), may hold values from -1.1953125 to 1.1953125
- biases: bfloat16 [768, 8], P(('frame', 'pos')), may hold values from -1.1953125 to 1.1953125
Outputs:
- block_out: bfloat16 [4, 48, 56, 768], P(None, 'frame', 'pos')
- tokens_grad: float32 [4, 48, 56, 768], P(None, 'frame', 'pos')
- class_grad: float32 [4, 3, 768], replicated
- grad_temporal_qkv: float32 [768, 2304], P(('frame', 'pos'))
- grad_temporal_proj: float32 [768, 768], P(('frame', 'pos'))
- grad_temporal_fc: float32 [768, 768], P(('frame', 'pos'))
- grad_spatial_qkv: float32 [768, 2304], P(('frame', 'pos'))
- grad_spatial_proj: float32 [768, 768], P(('frame', 'pos'))
- grad_mlp_in: float32 [768, 3072], P(('frame', 'pos'))
- grad_mlp_out: float32 [3072, 768], P(('frame', 'pos'))
- grad_mlp_in_bias: float32 [3072], P(('frame', 'pos'))
- grad_norm_gains: float32 [768, 3], P(('frame', 'pos'))
- grad_norm_shifts: float32 [768, 3], P(('frame', 'pos'))
- grad_biases: float32 [768, 8], P(('frame', 'pos'))
Inputs may be any that keep to these rules, and one draw needn't show every extreme that they name: `clip_frames`: in each micro-batch the 3 counts add up to 48; clips lie end to end from frame 0, and one clip of each micro-batch holds frames among the first 12 and among the last 12.
All inputs are finite; a program needn't handle non-finite values.
Results may differ from a plain program's by a relative error of at most 0.02.
Values may be sent and summed in bfloat16 or wider, within the bound.
No kernel may reach another device: no remote copies, remote signals or barrier semaphores. Data moves between devices by JAX's collectives and lax.ppermute only.
A program may use at most 448 MiB of HBM per device.

v0:
```python
from functools import partial

import jax
import jax.numpy as jnp
from jax import lax
from jax.sharding import PartitionSpec as P

D = 768
HEADS = 12
HEAD = 64
MB = 4
CLIPS = 3


def norm_forward(values, gain_vec, shift_vec):
    centred = values - jnp.mean(values, axis=-1, keepdims=True)
    inv_std = lax.rsqrt(jnp.mean(centred * centred, axis=-1, keepdims=True) + 1e-06)
    normal = centred * inv_std
    return (normal * gain_vec + shift_vec, normal, inv_std)


def norm_backward(upstream, normal, inv_std, gain_vec):
    grad_gain = jnp.sum(upstream * normal, axis=0)
    grad_shift = jnp.sum(upstream, axis=0)
    scaled_grad = upstream * gain_vec
    centred = scaled_grad - jnp.mean(scaled_grad, axis=-1, keepdims=True)
    grad_in = inv_std * (centred - normal * jnp.mean(scaled_grad * normal, axis=-1, keepdims=True))
    return (grad_in, grad_gain, grad_shift)


def matmul(left_mat, right_mat):
    return jnp.dot(left_mat, right_mat, preferred_element_type=jnp.float32)


def outer_sum(left_mat, right_mat):
    return lax.dot_general(
        left_mat, right_mat, (((0,), (0,)), ((), ())), preferred_element_type=jnp.float32
    )


def back_mul(upstream, weight):
    return lax.dot_general(
        upstream, weight, (((1,), (1,)), ((), ())), preferred_element_type=jnp.float32
    )


def column_sum(values):
    return jnp.sum(values.astype(jnp.float32), axis=0)


def on_device(
    tokens,
    class_tokens,
    clip_frames,
    cotangent,
    temporal_qkv,
    temporal_proj,
    temporal_fc,
    spatial_qkv,
    spatial_proj,
    mlp_in,
    mlp_out,
    mlp_in_bias,
    norm_gains,
    norm_shifts,
    biases,
):
    weights = (
        lax.all_gather(temporal_qkv, ("frame", "pos"), axis=0, tiled=True),
        lax.all_gather(temporal_proj, ("frame", "pos"), axis=0, tiled=True),
        lax.all_gather(temporal_fc, ("frame", "pos"), axis=0, tiled=True),
        lax.all_gather(spatial_qkv, ("frame", "pos"), axis=0, tiled=True),
        lax.all_gather(spatial_proj, ("frame", "pos"), axis=0, tiled=True),
        lax.all_gather(mlp_in, ("frame", "pos"), axis=0, tiled=True),
        lax.all_gather(mlp_out, ("frame", "pos"), axis=0, tiled=True),
        lax.all_gather(mlp_in_bias, ("frame", "pos"), axis=0, tiled=True),
        lax.all_gather(norm_gains, ("frame", "pos"), axis=0, tiled=True),
        lax.all_gather(norm_shifts, ("frame", "pos"), axis=0, tiled=True),
        lax.all_gather(biases, ("frame", "pos"), axis=0, tiled=True),
    )
    w_tqkv, w_tproj, w_tfc, w_sqkv, w_sproj, w_in, w_out, in_bias, gains, shifts, bias_cols = (
        weights
    )
    gains = gains.astype(jnp.float32)
    shifts = shifts.astype(jnp.float32)
    bias_cols = bias_cols.astype(jnp.float32)
    in_bias = in_bias.astype(jnp.float32)
    zero_row = jnp.zeros((D,), jnp.float32)
    temporal_bias = jnp.concatenate([bias_cols[:, 0], zero_row, bias_cols[:, 1]])
    spatial_bias = jnp.concatenate([bias_cols[:, 4], zero_row, bias_cols[:, 5]])
    class_bias = jnp.concatenate([zero_row, bias_cols[:, 5]])
    frame_count = tokens.shape[1]
    pos_count = tokens.shape[2]
    rows_count = frame_count * pos_count
    all_frames = frame_count * lax.axis_size("frame")
    frame_start = lax.axis_index("frame") * frame_count
    clip_ends = jnp.cumsum(clip_frames, axis=1)
    frame_ids = jnp.arange(all_frames, dtype=jnp.int32)
    clip_all = jnp.sum(
        (frame_ids[None, :, None] >= clip_ends[:, None, :]).astype(jnp.int32), axis=2
    )
    clip_local = lax.dynamic_slice_in_dim(clip_all, frame_start, frame_count, 1)
    clip_range = jnp.arange(CLIPS, dtype=jnp.int32)
    acc_tqkv = jnp.zeros(w_tqkv.shape, jnp.float32)
    acc_tproj = jnp.zeros(w_tproj.shape, jnp.float32)
    acc_tfc = jnp.zeros(w_tfc.shape, jnp.float32)
    acc_sqkv = jnp.zeros(w_sqkv.shape, jnp.float32)
    acc_sproj = jnp.zeros(w_sproj.shape, jnp.float32)
    acc_in = jnp.zeros(w_in.shape, jnp.float32)
    acc_out = jnp.zeros(w_out.shape, jnp.float32)
    acc_in_bias = jnp.zeros(in_bias.shape, jnp.float32)
    gain_cols = [zero_row, zero_row, zero_row]
    shift_cols = [zero_row, zero_row, zero_row]
    bias_grads = [zero_row] * 8
    outputs = []
    input_grads = []
    class_parts = []
    for micro_index in range(MB):
        rows_in = tokens[micro_index].astype(jnp.float32).reshape(rows_count, D)
        normed_f, normal_t, inv_std_t = norm_forward(rows_in, gains[:, 0], shifts[:, 0])
        normed_t = normed_f.astype(jnp.bfloat16)
        packed_t = (matmul(normed_t, w_tqkv) + temporal_bias).astype(jnp.bfloat16)
        query_t = packed_t[:, :D].reshape(frame_count, pos_count, HEADS, HEAD)
        pairs_t = lax.all_gather(
            packed_t[:, D:].reshape(frame_count, pos_count, 2 * D), "frame", axis=0, tiled=True
        )
        keys_t = pairs_t[:, :, :D].reshape(all_frames, pos_count, HEADS, HEAD)
        values_t = pairs_t[:, :, D:].reshape(all_frames, pos_count, HEADS, HEAD)
        same_clip = clip_local[micro_index][:, None] == clip_all[micro_index][None, :]
        scores = (
            jnp.einsum("fphe,gphe->phfg", query_t, keys_t, preferred_element_type=jnp.float32)
            * 0.125
        )
        scores = jnp.where(same_clip[None, None], scores, -1000000000.0)
        top_score = jnp.max(scores, axis=-1, keepdims=True)
        log_total_t = top_score + jnp.log(
            jnp.sum(jnp.exp(scores - top_score), axis=-1, keepdims=True)
        )
        probs_t = jnp.exp(scores - log_total_t)
        probs_tb = probs_t.astype(jnp.bfloat16)
        mixed_t = jnp.einsum(
            "phfg,gphe->fphe", probs_tb, values_t, preferred_element_type=jnp.float32
        )
        mixed_t = mixed_t.reshape(rows_count, D).astype(jnp.bfloat16)
        projected = (matmul(mixed_t, w_tproj) + bias_cols[:, 2]).astype(jnp.bfloat16)
        temporal = rows_in + matmul(projected, w_tfc) + bias_cols[:, 3]
        normed_f, normal_s, inv_std_s = norm_forward(temporal, gains[:, 1], shifts[:, 1])
        normed_s = normed_f.astype(jnp.bfloat16)
        packed_s = (matmul(normed_s, w_sqkv) + spatial_bias).astype(jnp.bfloat16)
        query_s = packed_s[:, :D].reshape(frame_count, pos_count, HEADS, HEAD)
        pairs_s = lax.all_gather(
            packed_s[:, D:].reshape(frame_count, pos_count, 2 * D), "pos", axis=1, tiled=True
        )
        all_pos = pairs_s.shape[1]
        keys_s = pairs_s[:, :, :D].reshape(frame_count, all_pos, HEADS, HEAD)
        values_s = pairs_s[:, :, D:].reshape(frame_count, all_pos, HEADS, HEAD)
        class_f, class_normal, class_inv = norm_forward(
            class_tokens[micro_index].astype(jnp.float32), gains[:, 1], shifts[:, 1]
        )
        class_pairs = (matmul(class_f.astype(jnp.bfloat16), w_sqkv[:, D:]) + class_bias).astype(
            jnp.bfloat16
        )
        choose = (clip_local[micro_index][:, None] == clip_range[None, :]).astype(jnp.bfloat16)
        frame_pairs = matmul(choose, class_pairs).astype(jnp.bfloat16)
        class_keys = frame_pairs[:, :D].reshape(frame_count, HEADS, HEAD)
        class_values = frame_pairs[:, D:].reshape(frame_count, HEADS, HEAD)
        patch_scores = (
            jnp.einsum("fphe,fqhe->fhpq", query_s, keys_s, preferred_element_type=jnp.float32)
            * 0.125
        )
        class_scores = (
            jnp.einsum("fphe,fhe->fhp", query_s, class_keys, preferred_element_type=jnp.float32)
            * 0.125
        )
        top_spatial = jnp.maximum(jnp.max(patch_scores, axis=-1), class_scores)
        exp_total = jnp.sum(jnp.exp(patch_scores - top_spatial[..., None]), axis=-1) + jnp.exp(
            class_scores - top_spatial
        )
        log_total_s = top_spatial + jnp.log(exp_total)
        probs_patch = jnp.exp(patch_scores - log_total_s[..., None])
        probs_class = jnp.exp(class_scores - log_total_s)
        patch_b = probs_patch.astype(jnp.bfloat16)
        class_b = probs_class.astype(jnp.bfloat16)
        mixed_s = jnp.einsum(
            "fhpq,fqhe->fphe", patch_b, values_s, preferred_element_type=jnp.float32
        )
        mixed_s = mixed_s + jnp.einsum(
            "fhp,fhe->fphe", class_b, class_values, preferred_element_type=jnp.float32
        )
        mixed_s = mixed_s.reshape(rows_count, D).astype(jnp.bfloat16)
        spatial = temporal + matmul(mixed_s, w_sproj) + bias_cols[:, 6]
        normed_f, normal_m, inv_std_m = norm_forward(spatial, gains[:, 2], shifts[:, 2])
        normed_m = normed_f.astype(jnp.bfloat16)
        hidden = matmul(normed_m, w_in) + in_bias
        activated, gelu_back = jax.vjp(partial(jax.nn.gelu, approximate=False), hidden)
        activated_b = activated.astype(jnp.bfloat16)
        result = spatial + matmul(activated_b, w_out) + bias_cols[:, 7]
        outputs.append(result.astype(jnp.bfloat16).reshape(frame_count, pos_count, D))
        grad_out = cotangent[micro_index].astype(jnp.float32).reshape(rows_count, D)
        grad_out_b = cotangent[micro_index].reshape(rows_count, D)
        acc_out = acc_out + outer_sum(activated_b, grad_out_b)
        bias_grads[7] = bias_grads[7] + column_sum(grad_out_b)
        grad_hidden = gelu_back(back_mul(grad_out_b, w_out))[0].astype(jnp.bfloat16)
        acc_in = acc_in + outer_sum(normed_m, grad_hidden)
        acc_in_bias = acc_in_bias + column_sum(grad_hidden)
        grad_ln, gain_part, shift_part = norm_backward(
            back_mul(grad_hidden, w_in), normal_m, inv_std_m, gains[:, 2]
        )
        gain_cols[2] = gain_cols[2] + gain_part
        shift_cols[2] = shift_cols[2] + shift_part
        grad_spatial = grad_out + grad_ln
        grad_spatial_b = grad_spatial.astype(jnp.bfloat16)
        acc_sproj = acc_sproj + outer_sum(mixed_s, grad_spatial_b)
        bias_grads[6] = bias_grads[6] + column_sum(grad_spatial_b)
        grad_mixed = (
            back_mul(grad_spatial_b, w_sproj)
            .astype(jnp.bfloat16)
            .reshape(frame_count, pos_count, HEADS, HEAD)
        )
        dprob_patch = jnp.einsum(
            "fphe,fqhe->fhpq", grad_mixed, values_s, preferred_element_type=jnp.float32
        )
        dprob_class = jnp.einsum(
            "fphe,fhe->fhp", grad_mixed, class_values, preferred_element_type=jnp.float32
        )
        delta_s = jnp.sum(dprob_patch * probs_patch, axis=-1) + dprob_class * probs_class
        dscore_patch = (probs_patch * (dprob_patch - delta_s[..., None])).astype(jnp.bfloat16)
        dscore_class = (probs_class * (dprob_class - delta_s)).astype(jnp.bfloat16)
        grad_query_s = jnp.einsum(
            "fhpq,fqhe->fphe", dscore_patch, keys_s, preferred_element_type=jnp.float32
        )
        grad_query_s = (
            grad_query_s
            + jnp.einsum(
                "fhp,fhe->fphe", dscore_class, class_keys, preferred_element_type=jnp.float32
            )
        ) * 0.125
        grad_class_key = (
            jnp.einsum("fhp,fphe->fhe", dscore_class, query_s, preferred_element_type=jnp.float32)
            * 0.125
        )
        grad_class_value = jnp.einsum(
            "fhp,fphe->fhe", class_b, grad_mixed, preferred_element_type=jnp.float32
        )
        class_frame = jnp.concatenate(
            [grad_class_key.reshape(frame_count, D), grad_class_value.reshape(frame_count, D)],
            axis=1,
        )
        class_parts.append(
            jnp.einsum(
                "fc,fd->cd",
                choose.astype(jnp.float32),
                class_frame,
                precision=lax.Precision.HIGHEST,
            )
        )
        grad_keys_all = (
            jnp.einsum("fhpq,fphe->fqhe", dscore_patch, query_s, preferred_element_type=jnp.float32)
            * 0.125
        )
        grad_values_all = jnp.einsum(
            "fhpq,fphe->fqhe", patch_b, grad_mixed, preferred_element_type=jnp.float32
        )
        stacked = jnp.concatenate(
            [
                grad_keys_all.reshape(frame_count, all_pos, D),
                grad_values_all.reshape(frame_count, all_pos, D),
            ],
            axis=2,
        )
        grad_pairs_s = lax.psum_scatter(
            stacked.astype(jnp.bfloat16), "pos", scatter_dimension=1, tiled=True
        )
        grad_packed_s = jnp.concatenate(
            [
                grad_query_s.reshape(rows_count, D).astype(jnp.bfloat16),
                grad_pairs_s.reshape(rows_count, 2 * D),
            ],
            axis=1,
        )
        acc_sqkv = acc_sqkv + outer_sum(normed_s, grad_packed_s)
        bias_grads[4] = bias_grads[4] + column_sum(grad_packed_s[:, :D])
        bias_grads[5] = bias_grads[5] + column_sum(grad_packed_s[:, 2 * D :])
        grad_ln, gain_part, shift_part = norm_backward(
            back_mul(grad_packed_s, w_sqkv), normal_s, inv_std_s, gains[:, 1]
        )
        gain_cols[1] = gain_cols[1] + gain_part
        shift_cols[1] = shift_cols[1] + shift_part
        grad_temporal = grad_spatial + grad_ln
        grad_temporal_b = grad_temporal.astype(jnp.bfloat16)
        acc_tfc = acc_tfc + outer_sum(projected, grad_temporal_b)
        bias_grads[3] = bias_grads[3] + column_sum(grad_temporal_b)
        grad_proj = back_mul(grad_temporal_b, w_tfc).astype(jnp.bfloat16)
        acc_tproj = acc_tproj + outer_sum(mixed_t, grad_proj)
        bias_grads[2] = bias_grads[2] + column_sum(grad_proj)
        grad_mixed_t = (
            back_mul(grad_proj, w_tproj)
            .astype(jnp.bfloat16)
            .reshape(frame_count, pos_count, HEADS, HEAD)
        )
        dprob_t = jnp.einsum(
            "fphe,gphe->phfg", grad_mixed_t, values_t, preferred_element_type=jnp.float32
        )
        delta_t = jnp.sum(dprob_t * probs_t, axis=-1, keepdims=True)
        dscore_t = (probs_t * (dprob_t - delta_t)).astype(jnp.bfloat16)
        grad_query_t = (
            jnp.einsum("phfg,gphe->fphe", dscore_t, keys_t, preferred_element_type=jnp.float32)
            * 0.125
        )
        grad_keys_t = (
            jnp.einsum("phfg,fphe->gphe", dscore_t, query_t, preferred_element_type=jnp.float32)
            * 0.125
        )
        grad_values_t = jnp.einsum(
            "phfg,fphe->gphe", probs_tb, grad_mixed_t, preferred_element_type=jnp.float32
        )
        stacked_t = jnp.concatenate(
            [
                grad_keys_t.reshape(all_frames, pos_count, D),
                grad_values_t.reshape(all_frames, pos_count, D),
            ],
            axis=2,
        )
        grad_pairs_t = lax.psum_scatter(
            stacked_t.astype(jnp.bfloat16), "frame", scatter_dimension=0, tiled=True
        )
        grad_packed_t = jnp.concatenate(
            [
                grad_query_t.reshape(rows_count, D).astype(jnp.bfloat16),
                grad_pairs_t.reshape(rows_count, 2 * D),
            ],
            axis=1,
        )
        acc_tqkv = acc_tqkv + outer_sum(normed_t, grad_packed_t)
        bias_grads[0] = bias_grads[0] + column_sum(grad_packed_t[:, :D])
        bias_grads[1] = bias_grads[1] + column_sum(grad_packed_t[:, 2 * D :])
        grad_ln, gain_part, shift_part = norm_backward(
            back_mul(grad_packed_t, w_tqkv), normal_t, inv_std_t, gains[:, 0]
        )
        gain_cols[0] = gain_cols[0] + gain_part
        shift_cols[0] = shift_cols[0] + shift_part
        input_grads.append((grad_temporal + grad_ln).reshape(frame_count, pos_count, D))
    class_total = lax.psum(jnp.stack(class_parts), ("frame", "pos"))
    class_grad_b = class_total.reshape(MB * CLIPS, 2 * D).astype(jnp.bfloat16)
    class_in = class_tokens.astype(jnp.float32).reshape(MB * CLIPS, D)
    class_f, class_normal, class_inv = norm_forward(class_in, gains[:, 1], shifts[:, 1])
    leader = ((lax.axis_index("frame") == 0) & (lax.axis_index("pos") == 0)).astype(jnp.float32)
    class_weight = outer_sum(class_f.astype(jnp.bfloat16), class_grad_b)
    acc_sqkv = acc_sqkv + leader * jnp.concatenate(
        [jnp.zeros((D, D), jnp.float32), class_weight], axis=1
    )
    bias_grads[5] = bias_grads[5] + leader * column_sum(class_grad_b[:, D:])
    grad_class, gain_part, shift_part = norm_backward(
        back_mul(class_grad_b, w_sqkv[:, D:]), class_normal, class_inv, gains[:, 1]
    )
    gain_cols[1] = gain_cols[1] + leader * gain_part
    shift_cols[1] = shift_cols[1] + leader * shift_part
    reduced = (
        lax.psum_scatter(acc_tqkv, ("frame", "pos"), scatter_dimension=0, tiled=True),
        lax.psum_scatter(acc_tproj, ("frame", "pos"), scatter_dimension=0, tiled=True),
        lax.psum_scatter(acc_tfc, ("frame", "pos"), scatter_dimension=0, tiled=True),
        lax.psum_scatter(acc_sqkv, ("frame", "pos"), scatter_dimension=0, tiled=True),
        lax.psum_scatter(acc_sproj, ("frame", "pos"), scatter_dimension=0, tiled=True),
        lax.psum_scatter(acc_in, ("frame", "pos"), scatter_dimension=0, tiled=True),
        lax.psum_scatter(acc_out, ("frame", "pos"), scatter_dimension=0, tiled=True),
        lax.psum_scatter(acc_in_bias, ("frame", "pos"), scatter_dimension=0, tiled=True),
        lax.psum_scatter(
            jnp.stack(gain_cols, axis=1), ("frame", "pos"), scatter_dimension=0, tiled=True
        ),
        lax.psum_scatter(
            jnp.stack(shift_cols, axis=1), ("frame", "pos"), scatter_dimension=0, tiled=True
        ),
        lax.psum_scatter(
            jnp.stack(bias_grads, axis=1), ("frame", "pos"), scatter_dimension=0, tiled=True
        ),
    )
    return (
        jnp.stack(outputs),
        jnp.stack(input_grads),
        grad_class.reshape(MB, CLIPS, D),
        reduced[0],
        reduced[1],
        reduced[2],
        reduced[3],
        reduced[4],
        reduced[5],
        reduced[6],
        reduced[7],
        reduced[8],
        reduced[9],
        reduced[10],
    )


def solution(mesh):
    placed = (
        P(None, "frame", "pos", None),
        P(),
        P(),
        P(None, "frame", "pos", None),
        P(("frame", "pos"), None),
        P(("frame", "pos"), None),
        P(("frame", "pos"), None),
        P(("frame", "pos"), None),
        P(("frame", "pos"), None),
        P(("frame", "pos"), None),
        P(("frame", "pos"), None),
        P(("frame", "pos")),
        P(("frame", "pos"), None),
        P(("frame", "pos"), None),
        P(("frame", "pos"), None),
    )
    return jax.shard_map(
        on_device,
        mesh=mesh,
        in_specs=placed,
        out_specs=(
            P(None, "frame", "pos", None),
            P(None, "frame", "pos", None),
            P(),
            P(("frame", "pos"), None),
            P(("frame", "pos"), None),
            P(("frame", "pos"), None),
            P(("frame", "pos"), None),
            P(("frame", "pos"), None),
            P(("frame", "pos"), None),
            P(("frame", "pos"), None),
            P(("frame", "pos")),
            P(("frame", "pos"), None),
            P(("frame", "pos"), None),
            P(("frame", "pos"), None),
        ),
        check_vma=False,
    )
```

profile of v0, /device:TPU:0, one launch (start us, length us, event | category | flops | bytes accessed | tf_op | source)
XLA Modules:
  0.0 2020.6 jit_solution(13742663746158687955)
XLA Ops:
  10.0 44.0 %all-gather.2 = bf16[32,24,8]{1,2,0:T(8,128)(2,1)S(1)} all-gather(bf16[1,24,8]{1,2,0:T(8,128)(2,1)} %bitcast.535), channel_id=1, replica_groups=mesh['frame'=4,'pos'=8] {'frame','pos'}, dimensions={0}, use_global_device_ids=true | all-gather | bytes 12672 | tf_op jit(solution)/shard_map/all_gather | solution.py:79
  56.4 5.3 fusion.258
  62.0 36.7 %all-gather.1 = bf16[32,24,3]{1,2,0:T(4,128)(2,1)S(1)} all-gather(bf16[1,24,3]{1,2,0:T(4,128)(2,1)S(1)} %bitcast.536), channel_id=1, replica_groups=mesh['frame'=4,'pos'=8] {'frame','pos'}, dimensions={0}, use_global_device_ids=true | all-gather | bytes 4752 | tf_op jit(solution)/shard_map/all_gather | solution.py:78
  99.0 38.1 %all-gather = bf16[32,24,3]{1,2,0:T(4,128)(2,1)S(1)} all-gather(bf16[1,24,3]{1,2,0:T(4,128)(2,1)S(1)} %bitcast.537), channel_id=1, replica_groups=mesh['frame'=4,'pos'=8] {'frame','pos'}, dimensions={0}, use_global_device_ids=true | all-gather | bytes 4752 | tf_op jit(solution)/shard_map/all_gather | solution.py:77
  144.3 15.0 all_gather.74
  167.8 18.7 all-gather.19.cloned.1.call-done
  189.0 59.5 %all-gather.21.cloned.1.call-done = bf16[768,2304]{1,0:T(8,128)(2,1)} async-done(((bf16[24,2304]{1,0:T(8,128)(2,1)}), bf16[768,2304]{1,0:T(8,128)(2,1)}) %all-gather.21.cloned.1.call-update) | async-done | bytes 3538960 | tf_op jit(solution)/shard_map/all_gather | solution.py:72
  267.8 15.5 all_gather.72
  312.2 12.9 all_gather.70
  360.1 13.4 all_gather.61
  405.9 39.6 %all-reduce.2 = bf16[3072]{0:T(1024)(128)(2,1)} all-reduce(bf16[3072]{0:T(1024)(128)(2,1)} %dynamic-update-slice), channel_id=1, replica_groups=mesh['frame'=4,'pos'=8] {'frame','pos'}, use_global_device_ids=true, to_apply=%add.2 | all-reduce | flops 3072 | bytes 12288
  626.6 7.7 convert_reduce_fusion.2
  639.3 5.1 convert_reduce_fusion.3
  655.5 5.3 convert_reduce_fusion
  673.6 5.1 multiply_reduce_fusion.4
  687.7 5.0 multiply_reduce_fusion.5
  695.8 5.2 multiply_reduce_fusion.6
  711.9 5.1 multiply_reduce_fusion.7
  855.4 128.1 %all-reduce.15.cloned.1.call-done = (bf16[12,56,1536]{2,1,0:T(8,128)(2,1)}, bf16[12,56,1536]{2,1,0:T(8,128)(2,1)}, bf16[12,56,1536]{2,1,0:T(8,128)(2,1)}, bf16[12,56,1536]{2,1,0:T(8,128)(2,1)}) async-done(((bf16[12,56,1536]{2,1,0:T(8,128)(2,1)}, bf16[12,56,1536]{2,1,0:T(8,128)(2,1)}, bf16[12,56,1536]{2,1,0:T(8,128)(2,1)}, bf16[12,56,1536]{2,1,0:T(8,128)(2,1)}), (bf16[12,56,1536]{2,1,0:T(8,128)(2,1)}, ...) | async-done | bytes 8257552
  1139.5 5.1 fusion.503
  1144.7 5.1 fusion.506
  1149.8 12.1 add_add_fusion.1
  1172.4 5.1 fusion.573
  1178.3 12.0 add_add_fusion
  1226.1 41.4 %psum.7 = bf16[4,3,1536]{2,1,0:T(4,128)(2,1)} all-reduce(f32[4,3,1536]{2,1,0:T(4,128)} %pad_maximum_fusion.10), channel_id=1, replica_groups=mesh['frame'=4,'pos'=8] {'frame','pos'}, use_global_device_ids=true, to_apply=%region_92.93 | all-reduce | flops 18432 | bytes 110592 | tf_op jit(solution)/shard_map/psum | solution.py:343
  1278.5 7.5 multiply_add_fusion
  1383.4 40.1 %all-reduce.11 = (f32[3072]{0:T(1024)S(1)}, f32[768,3]{0,1:T(4,128)S(1)}, f32[768,3]{0,1:T(4,128)S(1)}, f32[768,8]{0,1:T(8,128)S(1)}) all-reduce(f32[3072]{0:T(1024)S(1)} %copy-done.293, f32[768,3]{0,1:T(4,128)S(1)} %pad_maximum_fusion.13, ...), channel_id=17, replica_groups=mesh['frame'=4,'pos'=8] {'frame','pos'}, use_global_device_ids=true, to_apply=%region_106.107.clone | all-reduce | flops 13824 | bytes 110592
  1426.1 54.5 %reduce-scatter.31.cloned.1.call-done = f32[24,768]{1,0:T(8,128)} async-done(((f32[768,768]{1,0:T(8,128)}), f32[24,768]{1,0:T(8,128)}) %reduce-scatter.31.cloned.1.call-update) | async-done | bytes 73744 | tf_op jit(solution)/shard_map/reduce_scatter | solution.py:361
  1480.6 141.0 %reduce-scatter.37.cloned.1.call-done = f32[24,3072]{1,0:T(8,128)} async-done(((f32[768,3072]{1,0:T(8,128)}), f32[24,3072]{1,0:T(8,128)}) %reduce-scatter.37.cloned.1.call-update) | async-done | bytes 294928 | tf_op jit(solution)/shard_map/reduce_scatter | solution.py:364
  1621.6 142.1 %reduce-scatter.39.cloned.1.call-done = f32[96,768]{1,0:T(8,128)} async-done(((f32[3072,768]{1,0:T(8,128)}), f32[96,768]{1,0:T(8,128)}) %reduce-scatter.39.cloned.1.call-update) | async-done | bytes 294928 | tf_op jit(solution)/shard_map/reduce_scatter | solution.py:365
  1763.8 124.4 %reduce-scatter.33.cloned.1.call-done = f32[24,2304]{1,0:T(8,128)} async-done(((f32[768,2304]{1,0:T(8,128)}), f32[24,2304]{1,0:T(8,128)}) %reduce-scatter.33.cloned.1.call-update) | async-done | bytes 221200 | tf_op jit(solution)/shard_map/reduce_scatter | solution.py:362
  1888.2 125.7 %reduce-scatter.27.cloned.1.call-done = f32[24,2304]{1,0:T(8,128)} async-done(((f32[768,2304]{1,0:T(8,128)}), f32[24,2304]{1,0:T(8,128)}) %reduce-scatter.27.cloned.1.call-update) | async-done | bytes 221200 | tf_op jit(solution)/shard_map/reduce_scatter | solution.py:359
  (1511 shorter events, 818.7 us)
Async XLA Ops:
  7.2 134.2 %all-gather.15.cloned.1.call-start = ((), (), s32[]{:S(2)}) async-start(), calls=%async_computation.11 | async-start | bytes 3649536 | tf_op jit(solution)/shard_map/all_gather | solution.py:69
  7.9 158.2 %all-gather.17.cloned.1.call-start = ((), (), s32[]{:S(2)}) async-start(), calls=%async_computation.12 | async-start | bytes 1216512 | tf_op jit(solution)/shard_map/all_gather | solution.py:70
  8.7 177.8 %all-gather.19.cloned.1.call-start = ((), (), s32[]{:S(2)}) async-start(), calls=%async_computation.13 | async-start | bytes 1216512 | tf_op jit(solution)/shard_map/all_gather | solution.py:71
  9.4 239.1 %all-gather.21.cloned.1.call-start = ((), (), s32[]{:S(2)}) async-start(), calls=%async_computation.14 | async-start | bytes 3649536 | tf_op jit(solution)/shard_map/all_gather | solution.py:72
  10.0 512.3 %all-gather.35.cloned.1.call-start = ((), (), s32[]{:S(2)}) async-start(), calls=%async_computation.21 | async-start | bytes 3096576 | tf_op jit(solution)/shard_map/all_gather | solution.py:151
  56.3 85.0 %copy-start.370 = (f32[84]{0:T(128)}, f32[84]{0:T(128)S(1)}, u32[]{:S(2)}) copy-start(f32[84]{0:T(128)S(1)} %div.218) | copy-start | bytes 1012
  56.4 80.9 %copy-start.410 = (s32[4,3]{1,0:T(4,128)S(1)}, s32[4,3]{1,0:T(4,128)}, u32[]{:S(2)}) copy-start(s32[4,3]{1,0:T(4,128)} %param.17) | copy-start | bytes 148
  61.8 124.6 %copy-start.75 = (f32[84,768]{1,0:T(8,128)}, f32[84,768]{1,0:T(8,128)S(1)}, u32[]{:S(2)}) copy-start(f32[84,768]{1,0:T(8,128)S(1)} %reshape.1535) | copy-start | bytes 774148
  61.9 82.2 %copy-start.373 = (f32[84]{0:T(128)}, f32[84]{0:T(128)S(1)}, u32[]{:S(2)}) copy-start(f32[84]{0:T(128)S(1)} %rsqrt.168) | copy-start | bytes 1012
  139.6 214.1 %copy-start.175 = (f32[768]{0:T(1024)}, f32[768]{0:T(1024)S(1)}, u32[]{:S(2)}) copy-start(f32[768]{0:T(1024)S(1)} %get-tuple-element.404) | copy-start | bytes 9220
  139.6 351.3 %copy-start.166 = (f32[768]{0:T(1024)}, f32[768]{0:T(1024)S(1)}, u32[]{:S(2)}) copy-start(f32[768]{0:T(1024)S(1)} %get-tuple-element.182) | copy-start | bytes 9220
  167.8 80.8 %copy-start.241 = (bf16[84,768]{1,0:T(8,128)(2,1)}, bf16[84,768]{1,0:T(8,128)(2,1)S(1)}, u32[]{:S(2)}) copy-start(bf16[84,768]{1,0:T(8,128)(2,1)S(1)} %fusion.176) | copy-start | bytes 387076
  188.2 60.4 %copy-start.63 = (f32[84,768]{1,0:T(8,128)}, f32[84,768]{1,0:T(8,128)S(1)}, u32[]{:S(2)}) copy-start(f32[84,768]{1,0:T(8,128)S(1)} %get-tuple-element.324) | copy-start | bytes 774148
  188.2 60.3 %copy-start.346 = (f32[84]{0:T(128)}, f32[84]{0:T(128)S(1)}, u32[]{:S(2)}) copy-start(f32[84]{0:T(128)S(1)} %broadcast_multiply_fusion.36) | copy-start | bytes 1012
  256.6 288.3 %all-gather.33.cloned.1.call-start = ((), (), s32[]{:S(2)}) async-start(), calls=%async_computation.20 | async-start | bytes 3096576 | tf_op jit(solution)/shard_map/all_gather | solution.py:151
  301.7 265.4 %all-gather.31.cloned.1.call-start = ((), (), s32[]{:S(2)}) async-start(), calls=%async_computation.19 | async-start | bytes 3096576 | tf_op jit(solution)/shard_map/all_gather | solution.py:151
  348.0 241.6 %all-gather.23.cloned.1.call-start = ((), (), s32[]{:S(2)}) async-start(), calls=%async_computation.15 | async-start | bytes 3096576 | tf_op jit(solution)/shard_map/all_gather | solution.py:151
  396.8 215.3 %all-gather.25.cloned.1.call-start = ((), (), s32[]{:S(2)}) async-start(), calls=%async_computation.16 | async-start | bytes 1216512 | tf_op jit(solution)/shard_map/all_gather | solution.py:73
  397.6 222.5 %all-gather.27.cloned.1.call-start = ((), (), s32[]{:S(2)}) async-start(), calls=%async_computation.17 | async-start | bytes 4866048 | tf_op jit(solution)/shard_map/all_gather | solution.py:74
  398.2 228.4 %all-gather.29.cloned.1.call-start = ((), (), s32[]{:S(2)}) async-start(), calls=%async_computation.18 | async-start | bytes 4866048 | tf_op jit(solution)/shard_map/all_gather | solution.py:75
  398.9 584.6 %all-reduce.15.cloned.1.call-start = ((), (), s32[]{:S(2)}) async-start(), calls=%async_computation.33 | async-start | bytes 16515072
  808.7 521.9 %reduce-scatter.21.cloned.1.call-start = ((), (), s32[]{:S(2)}) async-start(), calls=%async_computation.23 | async-start | bytes 1474560 | tf_op jit(solution)/shard_map/reduce_scatter | solution.py:324
  1042.8 289.0 %reduce-scatter.23.cloned.1.call-start = ((), (), s32[]{:S(2)}) async-start(), calls=%async_computation.24 | async-start | bytes 1474560 | tf_op jit(solution)/shard_map/reduce_scatter | solution.py:324
  1070.8 262.2 %reduce-scatter.19.cloned.1.call-start = ((), (), s32[]{:S(2)}) async-start(), calls=%async_computation.22 | async-start | bytes 1474560 | tf_op jit(solution)/shard_map/reduce_scatter | solution.py:324
  1095.0 239.1 %reduce-scatter.25.cloned.1.call-start = ((), (), s32[]{:S(2)}) async-start(), calls=%async_computation.25 | async-start | bytes 1474560 | tf_op jit(solution)/shard_map/reduce_scatter | solution.py:324
  1119.4 306.7 %reduce-scatter.35.cloned.1.call-start = ((), (), s32[]{:S(2)}) async-start(), calls=%async_computation.30 | async-start | bytes 2433024 | tf_op jit(solution)/shard_map/reduce_scatter | solution.py:363
  1125.0 301.1 %reduce-scatter.29.cloned.1.call-start = ((), (), s32[]{:S(2)}) async-start(), calls=%async_computation.27 | async-start | bytes 2433024 | tf_op jit(solution)/shard_map/reduce_scatter | solution.py:360
  1130.5 350.1 %reduce-scatter.31.cloned.1.call-start = ((), (), s32[]{:S(2)}) async-start(), calls=%async_computation.28 | async-start | bytes 2433024 | tf_op jit(solution)/shard_map/reduce_scatter | solution.py:361
  1136.1 485.6 %reduce-scatter.37.cloned.1.call-start = ((), (), s32[]{:S(2)}) async-start(), calls=%async_computation.31 | async-start | bytes 9732096 | tf_op jit(solution)/shard_map/reduce_scatter | solution.py:364
  1162.0 601.8 %reduce-scatter.39.cloned.1.call-start = ((), (), s32[]{:S(2)}) async-start(), calls=%async_computation.32 | async-start | bytes 9732096 | tf_op jit(solution)/shard_map/reduce_scatter | solution.py:365
  1190.3 697.8 %reduce-scatter.33.cloned.1.call-start = ((), (), s32[]{:S(2)}) async-start(), calls=%async_computation.29 | async-start | bytes 7299072 | tf_op jit(solution)/shard_map/reduce_scatter | solution.py:362
  1286.1 727.8 %reduce-scatter.27.cloned.1.call-start = ((), (), s32[]{:S(2)}) async-start(), calls=%async_computation.26 | async-start | bytes 7299072 | tf_op jit(solution)/shard_map/reduce_scatter | solution.py:359
  (419 other events, 1591.4 us)
Sparse Core Ops, SparseCore 0:
  11.0 63.0 all-gather.14
  77.2 52.9 all-gather.16
  133.2 53.1 all-gather.18
  189.3 59.1 all-gather.20
  256.7 33.7 all-gather.34
  301.8 33.8 all-gather.32
  348.2 33.8 all-gather.30
  397.0 34.0 all-gather.22
  434.1 53.1 all-gather.24
  490.2 62.5 all-gather.26
  555.8 62.4 all-gather.28
  808.9 174.5 all-reduce.14
  1042.9 28.6 reduce-scatter.20
  1074.6 28.5 reduce-scatter.22
  1106.2 28.5 reduce-scatter.18
  1137.8 28.5 reduce-scatter.24
  1172.9 98.9 reduce-scatter.34
  1277.7 98.0 reduce-scatter.28
  1382.5 98.0 reduce-scatter.30
  1486.9 134.6 reduce-scatter.36
  1629.1 134.5 reduce-scatter.38
  1770.0 118.1 reduce-scatter.32
  1895.4 118.4 reduce-scatter.26
where the time goes:
time: 2040 us; the launch traced here: 2020 us
  waiting for transfers between devices  799 us (39%)
  local copies, waits for them, and re-layouts  424 us (21%)
  matrix products  364 us (18%)
  blocking collectives  297 us (15%)
  other arithmetic  114 us (6%)
    reduce_scatter x1, waiting for transfers between devices, on_device(): lax.psum_scatter(acc_out, ('frame', 'pos'), scatter_dimension=0, tiled=True)  142 us
    reduce_scatter x1, waiting for transfers between devices, on_device(): lax.psum_scatter(acc_in, ('frame', 'pos'), scatter_dimension=0, tiled=True)  141 us
    unnamed x24, waiting for transfers between devices  133 us
    reduce_scatter x1, waiting for transfers between devices, on_device(): lax.psum_scatter(acc_tqkv, ('frame', 'pos'), scatter_dimension=0, tiled=T...  126 us
    reduce_scatter x1, waiting for transfers between devices, on_device(): lax.psum_scatter(acc_sqkv, ('frame', 'pos'), scatter_dimension=0, tiled=T...  124 us
    dot_general x29, matrix products, outer_sum(): lax.dot_general(left_mat, right_mat, (((0,), (0,)), ((), ())), preferred_...  87.9 us
    unnamed x2, blocking collectives  79.7 us
    dot_general x29, matrix products, back_mul(): lax.dot_general(upstream, weight, (((1,), (1,)), ((), ())), preferred_ele...  72.9 us
  transfers between devices with their start and end apart: 23, of which 8 were waited for; matrix products, arithmetic and copies ran while one was open for 31% of the time, Pallas kernels for 0%

commit v1 on v0

v1 whole, which is shorter than its diff:
```python
from functools import partial

import jax
import jax.numpy as jnp
from jax import lax
from jax.sharding import PartitionSpec as P

D = 768
HEADS = 12
HEAD = 64
MB = 4
CLIPS = 3
AXES = ("frame", "pos")


def norm_forward(values, gain_vec, shift_vec):
    centred = values - jnp.mean(values, axis=-1, keepdims=True)
    inv_std = lax.rsqrt(jnp.mean(centred * centred, axis=-1, keepdims=True) + 1e-06)
    normal = centred * inv_std
    return (normal * gain_vec + shift_vec, normal, inv_std)


def norm_backward(upstream, normal, inv_std, gain_vec):
    grad_gain = jnp.sum(upstream * normal, axis=0)
    grad_shift = jnp.sum(upstream, axis=0)
    scaled_grad = upstream * gain_vec
    centred = scaled_grad - jnp.mean(scaled_grad, axis=-1, keepdims=True)
    grad_in = inv_std * (centred - normal * jnp.mean(scaled_grad * normal, axis=-1, keepdims=True))
    return (grad_in, grad_gain, grad_shift)


def matmul(left_mat, right_mat):
    return jnp.dot(left_mat, right_mat, preferred_element_type=jnp.float32)


def outer_sum(left_mat, right_mat):
    return lax.dot_general(
        left_mat, right_mat, (((0,), (0,)), ((), ())), preferred_element_type=jnp.float32
    ).astype(jnp.bfloat16)


def back_mul(upstream, weight):
    return lax.dot_general(
        upstream, weight, (((1,), (1,)), ((), ())), preferred_element_type=jnp.float32
    )


def column_sum(values):
    return jnp.sum(values.astype(jnp.float32), axis=0)


def split_heads(values):
    return values.reshape(values.shape[0], HEADS, HEAD)


def attention_forward(query, keys, values, allowed):
    scores = (
        jnp.einsum(
            "qhe,khe->hqk", split_heads(query), split_heads(keys), preferred_element_type=jnp.float32
        )
        * 0.125
    )
    scores = jnp.where(allowed[None], scores, -1000000000.0)
    top_score = jnp.max(scores, axis=-1, keepdims=True)
    log_total = top_score + jnp.log(jnp.sum(jnp.exp(scores - top_score), axis=-1, keepdims=True))
    probs = jnp.exp(scores - log_total).astype(jnp.bfloat16)
    mixed = jnp.einsum(
        "hqk,khe->qhe", probs, split_heads(values), preferred_element_type=jnp.float32
    )
    return (mixed.reshape(query.shape).astype(jnp.bfloat16), log_total)


def attention_backward(query, keys, values, allowed, log_total, grad_mixed):
    query, keys, values, grad_mixed = (
        split_heads(query),
        split_heads(keys),
        split_heads(values),
        split_heads(grad_mixed),
    )
    scores = jnp.einsum("qhe,khe->hqk", query, keys, preferred_element_type=jnp.float32) * 0.125
    scores = jnp.where(allowed[None], scores, -1000000000.0)
    probs = jnp.exp(scores - log_total)
    dprob = jnp.einsum("qhe,khe->hqk", grad_mixed, values, preferred_element_type=jnp.float32)
    delta = jnp.sum(dprob * probs, axis=-1, keepdims=True)
    dscore = (probs * (dprob - delta)).astype(jnp.bfloat16)
    probs_b = probs.astype(jnp.bfloat16)
    grad_query = jnp.einsum("hqk,khe->qhe", dscore, keys, preferred_element_type=jnp.float32) * 0.125
    grad_keys = jnp.einsum("hqk,qhe->khe", dscore, query, preferred_element_type=jnp.float32) * 0.125
    grad_values = jnp.einsum("hqk,qhe->khe", probs_b, grad_mixed, preferred_element_type=jnp.float32)
    flat = lambda g: g.reshape(g.shape[0], D).astype(jnp.bfloat16)
    return (flat(grad_query), flat(grad_keys), flat(grad_values))


def on_device(
    tokens,
    class_tokens,
    clip_frames,
    cotangent,
    temporal_qkv,
    temporal_proj,
    temporal_fc,
    spatial_qkv,
    spatial_proj,
    mlp_in,
    mlp_out,
    mlp_in_bias,
    norm_gains,
    norm_shifts,
    biases,
):
    bf16, f32 = jnp.bfloat16, jnp.float32
    frame_size, pos_size = lax.axis_size("frame"), lax.axis_size("pos")
    frame_index, pos_index = lax.axis_index("frame"), lax.axis_index("pos")
    frame_count, pos_count = tokens.shape[1], tokens.shape[2]
    shard = norm_gains.shape[0]
    slots = pos_count + 1
    share = frame_size // MB
    my_slots = slots // share
    all_frames = frame_count * frame_size
    my_frames = all_frames // pos_size
    rows_count = all_frames * my_slots
    micro = frame_index // share

    gather = partial(lax.all_gather, axis_name=AXES, axis=0, tiled=True)
    small = jnp.concatenate(
        [mlp_in_bias.reshape(shard, 4), norm_gains, norm_shifts, biases], axis=1
    )
    chunk_t = gather(jnp.concatenate([temporal_qkv, temporal_proj, temporal_fc], axis=1))
    small = gather(small).astype(f32)
    chunk_s = gather(jnp.concatenate([spatial_qkv, spatial_proj], axis=1))
    w_in = gather(mlp_in)
    w_out = gather(mlp_out)
    w_tqkv, w_tproj, w_tfc = chunk_t[:, : 3 * D], chunk_t[:, 3 * D : 4 * D], chunk_t[:, 4 * D :]
    w_sqkv, w_sproj = chunk_s[:, : 3 * D], chunk_s[:, 3 * D :]
    in_bias = small[:, :4].reshape(-1)
    rows_small = small[:, 4:].T
    gains, shifts, bias_rows = rows_small[:3], rows_small[3:6], rows_small[6:]
    zero_row = jnp.zeros((D,), f32)
    temporal_bias = jnp.concatenate([bias_rows[0], zero_row, bias_rows[1]])
    spatial_bias = jnp.concatenate([bias_rows[4], zero_row, bias_rows[5]])

    def frame_hop(values):
        return lax.all_to_all(values, "frame", 0, 0, tiled=True)

    def pos_hop(values):
        parts = values.reshape(pos_size, rows_count // pos_size, D)
        return lax.all_to_all(parts, "pos", 0, 0, tiled=True).reshape(rows_count, D)

    def to_temporal(values):
        padded = jnp.pad(values, ((0, 0), (0, 0), (0, 1), (0, 0)))
        padded = padded.reshape(MB, frame_count, share, my_slots, D).transpose(0, 2, 1, 3, 4)
        return frame_hop(padded.reshape(frame_size, frame_count * my_slots, D)).reshape(
            rows_count, D
        )

    def from_temporal(values):
        parts = frame_hop(values.reshape(frame_size, frame_count * my_slots, D))
        parts = parts.reshape(MB, share, frame_count, my_slots, D).transpose(0, 2, 1, 3, 4)
        return parts.reshape(MB, frame_count, slots, D)[:, :, :pos_count]

    def partners(values, step):
        perm = [
            (f, f // share * share + (f % share + step) % share) for f in range(frame_size)
        ]
        return lax.ppermute(values, "frame", perm)

    row_ids = jnp.arange(rows_count, dtype=jnp.int32)
    row_slot = row_ids % my_slots
    clip_ends = jnp.cumsum(lax.dynamic_index_in_dim(clip_frames, micro, 0, keepdims=False))
    clip_of = lambda frame: jnp.sum(
        (frame[:, None] >= clip_ends[None, :]).astype(jnp.int32), axis=1
    )
    group_t = row_slot * CLIPS + clip_of(row_ids // my_slots)
    allowed_t = group_t[:, None] == group_t[None, :]
    frame_s = row_ids // my_slots % my_frames
    clip_s = clip_of(pos_index * my_frames + frame_s)
    first_source = row_ids < my_frames * my_slots

    def key_masks(share_index):
        padding = row_slot + share_index * my_slots == slots - 1
        is_class = padding & first_source
        return is_class, is_class | ~padding

    allowed_s = []
    for step in range(share):
        _, valid = key_masks((frame_index + share - step) % share)
        allowed_s.append((frame_s[:, None] == frame_s[None, :]) & valid[None, :])
    allowed_s = jnp.concatenate(allowed_s, axis=1)
    is_class, _ = key_masks(frame_index % share)

    rows_in = to_temporal(tokens).astype(f32)
    normed_f, normal_t, inv_std_t = norm_forward(rows_in, gains[0], shifts[0])
    normed_t = normed_f.astype(bf16)
    packed_t = (matmul(normed_t, w_tqkv) + temporal_bias).astype(bf16)
    query_t, keys_t, values_t = packed_t[:, :D], packed_t[:, D : 2 * D], packed_t[:, 2 * D :]
    mixed_t, log_total_t = attention_forward(query_t, keys_t, values_t, allowed_t)
    projected = (matmul(mixed_t, w_tproj) + bias_rows[2]).astype(bf16)
    temporal = (rows_in + matmul(projected, w_tfc) + bias_rows[3]).astype(bf16)
    temporal = pos_hop(temporal).astype(f32)
    class_rows = lax.dynamic_index_in_dim(class_tokens, micro, 0, keepdims=False).astype(f32)
    choose = (clip_s[:, None] == jnp.arange(CLIPS)[None, :]) & is_class[:, None]
    class_rows = jnp.einsum("rc,cd->rd", choose.astype(f32), class_rows, precision="highest")
    temporal = jnp.where(is_class[:, None], class_rows, temporal)
    normed_f, normal_s, inv_std_s = norm_forward(temporal, gains[1], shifts[1])
    normed_s = normed_f.astype(bf16)
    packed_s = (matmul(normed_s, w_sqkv) + spatial_bias).astype(bf16)
    query_s = packed_s[:, :D]
    pairs_s = [packed_s[:, D:]]
    for step in range(1, share):
        pairs_s.append(partners(packed_s[:, D:], step))
    pairs_s = jnp.concatenate(pairs_s, axis=0)
    keys_s, values_s = pairs_s[:, :D], pairs_s[:, D:]
    mixed_s, log_total_s = attention_forward(query_s, keys_s, values_s, allowed_s)
    spatial = temporal + matmul(mixed_s, w_sproj) + bias_rows[6]
    normed_f, normal_m, inv_std_m = norm_forward(spatial, gains[2], shifts[2])
    normed_m = normed_f.astype(bf16)
    hidden = matmul(normed_m, w_in) + in_bias
    activated, gelu_back = jax.vjp(partial(jax.nn.gelu, approximate=False), hidden)
    activated = activated.astype(bf16)
    result = (spatial + matmul(activated, w_out) + bias_rows[7]).astype(bf16)
    block_out = from_temporal(pos_hop(result))
    grad_out = pos_hop(to_temporal(cotangent))
    acc_out = outer_sum(activated, grad_out)
    grad_hidden = gelu_back(back_mul(grad_out, w_out))[0].astype(bf16)
    acc_in = outer_sum(normed_m, grad_hidden)
    grad_ln, gain_m, shift_m = norm_backward(
        back_mul(grad_hidden, w_in), normal_m, inv_std_m, gains[2]
    )
    grad_spatial = grad_out.astype(f32) + grad_ln
    grad_spatial_b = grad_spatial.astype(bf16)
    acc_sproj = outer_sum(mixed_s, grad_spatial_b)
    grad_mixed = back_mul(grad_spatial_b, w_sproj).astype(bf16)
    grad_query, grad_keys, grad_values = attention_backward(
        query_s, keys_s, values_s, allowed_s, log_total_s, grad_mixed
    )
    grad_pairs = jnp.concatenate([grad_keys, grad_values], axis=1)
    own_pairs = grad_pairs[:rows_count]
    for step in range(1, share):
        theirs = grad_pairs[step * rows_count : (step + 1) * rows_count]
        own_pairs = (own_pairs.astype(f32) + partners(theirs, share - step).astype(f32)).astype(bf16)
    grad_packed_s = jnp.concatenate([grad_query, own_pairs], axis=1)
    acc_sqkv = outer_sum(normed_s, grad_packed_s)
    grad_ln, gain_s, shift_s = norm_backward(
        back_mul(grad_packed_s, w_sqkv), normal_s, inv_std_s, gains[1]
    )
    class_part = jnp.einsum("rc,rd->cd", choose.astype(f32), grad_ln, precision="highest")
    grad_temporal = jnp.where(is_class[:, None], 0.0, grad_spatial + grad_ln).astype(bf16)
    grad_temporal = pos_hop(grad_temporal)
    acc_tfc = outer_sum(projected, grad_temporal)
    grad_proj = back_mul(grad_temporal, w_tfc).astype(bf16)
    acc_tproj = outer_sum(mixed_t, grad_proj)
    grad_mixed_t = back_mul(grad_proj, w_tproj).astype(bf16)
    grad_packed_t = jnp.concatenate(
        attention_backward(query_t, keys_t, values_t, allowed_t, log_total_t, grad_mixed_t), axis=1
    )
    acc_tqkv = outer_sum(normed_t, grad_packed_t)
    grad_ln, gain_t, shift_t = norm_backward(
        back_mul(grad_packed_t, w_tqkv), normal_t, inv_std_t, gains[0]
    )
    tokens_grad = from_temporal((grad_temporal.astype(f32) + grad_ln).astype(bf16)).astype(f32)

    class_all = jnp.zeros((MB, CLIPS, D), f32)
    class_all = lax.dynamic_update_index_in_dim(class_all, class_part, micro, 0)
    class_grad = lax.psum(class_all, AXES)
    scatter = partial(lax.psum_scatter, axis_name=AXES, scatter_dimension=0, tiled=True)
    sum_s = column_sum(grad_packed_s)
    sum_t = column_sum(grad_packed_t)
    small_grads = jnp.stack(
        [gain_t, gain_s, gain_m, shift_t, shift_s, shift_m]
        + [sum_t[:D], sum_t[2 * D :], column_sum(grad_proj), column_sum(grad_temporal)]
        + [sum_s[:D], sum_s[2 * D :], column_sum(grad_spatial_b), column_sum(grad_out)],
        axis=1,
    )
    small_grads = jnp.concatenate([column_sum(grad_hidden).reshape(D, 4), small_grads], axis=1)
    small_grads = scatter(small_grads)
    acc_out = scatter(acc_out).astype(f32)
    acc_in = scatter(acc_in).astype(f32)
    acc_s = scatter(jnp.concatenate([acc_sqkv, acc_sproj], axis=1)).astype(f32)
    acc_t = scatter(jnp.concatenate([acc_tqkv, acc_tproj, acc_tfc], axis=1)).astype(f32)
    return (
        block_out,
        tokens_grad,
        class_grad,
        acc_t[:, : 3 * D],
        acc_t[:, 3 * D : 4 * D],
        acc_t[:, 4 * D :],
        acc_s[:, : 3 * D],
        acc_s[:, 3 * D :],
        acc_in,
        acc_out,
        small_grads[:, :4].reshape(-1),
        small_grads[:, 4:7],
        small_grads[:, 7:10],
        small_grads[:, 10:],
    )


def solution(mesh):
    rows = P(AXES, None)
    wide = P(None, "frame", "pos", None)
    placed = (wide, P(), P(), wide) + (rows,) * 7 + (P(AXES),) + (rows,) * 3
    return jax.shard_map(
        on_device,
        mesh=mesh,
        in_specs=placed,
        out_specs=(wide, wide, P()) + (rows,) * 7 + (P(AXES),) + (rows,) * 3,
        check_vma=False,
    )
```

time: 2040 us -> 997 us (0.49)
  local copies, waits for them, and re-layouts: 424 us -> 63.5 us
  matrix products: 364 us -> 118 us
  blocking collectives: 297 us -> 65.1 us
  waiting for transfers between devices: 799 us -> 661 us
  other arithmetic: 114 us -> 38.3 us
  starting transfers between devices: 3.25 us -> 29.4 us
    reshape x94 -> x3, local copies, waits for them, and re-layouts: 207 us -> 1.85 us  [the longest x1 1.14 us: on_device(): column_sum(grad_hidden).reshape(D, 4)]
    reduce_scatter x11 -> x4, waiting for transfers between devices: 588 us -> 442 us  [the longest x1 116 us: on_device(): scatter(jnp.concatenate([acc_tqkv, acc_tproj, acc_tfc], axis=1)).astype(f32)]
    all_gather x7 -> x1, blocking collectives: 176 us -> 43.5 us  [on_device(): small = gather(small).astype(f32)]
    unnamed x24 -> x9, waiting for transfers between devices: 133 us -> 1.35 us
    dot_general x68 -> x14, matrix products: 140 us -> 31.7 us  [the longest x2 11.2 us: attention_backward(): jnp.einsum('hqk,qhe->khe', probs_b, grad_mixed, preferred_element_type=jn...]
    unnamed x2 -> x0, blocking collectives: 79.7 us -> none
    dot_general x29 -> x7, matrix products: 87.9 us -> 25 us  [outer_sum(): lax.dot_general(left_mat, right_mat, (((0,), (0,)), ((), ())), preferred_...]
    all_gather x11 -> x4, waiting for transfers between devices: 78.2 us -> 130 us  [the longest x1 58.8 us: on_device(): w_out = gather(mlp_out)]
  transfers between devices with their start and end apart: 23 -> 16, of which waited for: 8 -> 13; matrix products, arithmetic and copies ran while one was open for 31% -> 12% of each run, Pallas kernels for 0% -> 0%
where the time goes in v1:
time: 997 us; the launch traced here: 991 us
  waiting for transfers between devices  661 us (66%)
  matrix products  118 us (12%)
  blocking collectives  65.1 us (7%)
  local copies, waits for them, and re-layouts  63.5 us (6%)
  other arithmetic  38.3 us (4%)
  starting transfers between devices  29.4 us (3%)
  between operations  15.7 us (2%)
    reduce_scatter x1, waiting for transfers between devices, on_device(): scatter(jnp.concatenate([acc_tqkv, acc_tproj, acc_tfc], axis=1)).astype(f32)  116 us
    reduce_scatter x1, waiting for transfers between devices, on_device(): acc_out = scatter(acc_out).astype(f32)  111 us
    reduce_scatter x1, waiting for transfers between devices, on_device(): acc_in = scatter(acc_in).astype(f32)  109 us
    reduce_scatter x1, waiting for transfers between devices, on_device(): acc_s = scatter(jnp.concatenate([acc_sqkv, acc_sproj], axis=1)).astype(f32)  107 us
    all_gather x1, waiting for transfers between devices, on_device(): w_out = gather(mlp_out)  58.8 us
    psum x1, waiting for transfers between devices, on_device(): class_grad = lax.psum(class_all, AXES)  50.1 us
    all_gather x1, waiting for transfers between devices, on_device(): w_in = gather(mlp_in)  47.6 us
    all_gather x1, blocking collectives, on_device(): small = gather(small).astype(f32)  43.5 us
  transfers between devices with their start and end apart: 16, of which 13 were waited for; matrix products, arithmetic and copies ran while one was open for 12% of the time, Pallas kernels for 0%

profile of v1, /device:TPU:0, one launch (start us, length us, event | category | flops | bytes accessed | tf_op | source)
XLA Modules:
  0.0 991.2 jit_solution(14376389585125031082)
XLA Ops:
  13.5 5.2 all-to-all-start
  20.6 43.5 %all_gather.15 = bf16[768,18]{1,0:T(8,128)(2,1)S(1)} all-gather(bf16[24,18]{1,0:T(8,128)(2,1)S(1)} %pad_maximum_fusion.8), channel_id=1, replica_groups=mesh['frame'=4,'pos'=8] {'frame','pos'}, dimensions={0}, use_global_device_ids=true | all-gather | bytes 28512 | tf_op jit(solution)/shard_map/all_gather | solution.py:129
  68.6 4.2 all-to-all-start.4
  73.4 8.9 all-to-all-done.4
  82.3 3.8 all-to-all-start.5
  108.8 4.4 all-to-all-start.1
  114.8 21.5 %all-to-all-done.1 = bf16[8,48,768]{2,1,0:T(8,128)(2,1)S(1)} async-done(((bf16[8,48,768]{2,1,0:T(8,128)(2,1)}), bf16[8,48,768]{2,1,0:T(8,128)(2,1)S(1)}, u32[]{:S(2)}, u32[]{:S(2)}) %all-to-all-start.1) | async-done | bytes 589856 | tf_op jit(solution)/shard_map/all_to_all | solution.py:147
  139.0 20.4 %all-gather.7.cloned.1.call-done = bf16[768,3072]{1,0:T(8,128)(2,1)} async-done(((bf16[24,3072]{1,0:T(8,128)(2,1)}), bf16[768,3072]{1,0:T(8,128)(2,1)}) %all-gather.7.cloned.1.call-update) | async-done | bytes 4718608 | tf_op jit(solution)/shard_map/all_gather | solution.py:130
  159.4 3.7 fusion.9
  177.3 47.6 %all-gather.9.cloned.1.call-done = bf16[768,3072]{1,0:T(8,128)(2,1)} async-done(((bf16[24,3072]{1,0:T(8,128)(2,1)}), bf16[768,3072]{1,0:T(8,128)(2,1)}) %all-gather.9.cloned.1.call-update) | async-done | bytes 4718608 | tf_op jit(solution)/shard_map/all_gather | solution.py:131
  224.9 6.6 convolution_add_fusion.2
  231.5 58.8 %all-gather.11.cloned.1.call-done = bf16[3072,768]{1,0:T(8,128)(2,1)} async-done(((bf16[96,768]{1,0:T(8,128)(2,1)}), bf16[3072,768]{1,0:T(8,128)(2,1)}) %all-gather.11.cloned.1.call-update) | async-done | bytes 4718608 | tf_op jit(solution)/shard_map/all_gather | solution.py:132
  290.3 16.7 %convert_reduce_fusion = (f32[3072]{0:T(1024)}, bf16[384,3072]{1,0:T(8,128)(2,1)S(1)}, f32[384,3072]{1,0:T(8,128)}) fusion(f32[384,3072]{1,0:T(8,128)} %convolution_add_fusion.2, bf16[384,768]{1,0:T(8,128)(2,1)S(1)} %bitcast.132, bf16[3072,768]{1,0:T(8,128)(2,1)} %all-gather.11.cloned.1.call-done), kind=kOutput, calls=%fused_computation.20 | convolution fusion | flops 1899230208 | bytes 17117184 | tf_op jit(solution)/shard_map/dot_general | solution.py:43
  316.5 6.0 convolution_convert_fusion.10
  335.0 4.6 multiply_reduce_fusion.3
  341.4 4.2 all-to-all-start.6
  356.4 5.6 convolution_convert_fusion.2
  370.6 5.2 convolution_convert_fusion.7
  393.3 4.6 concatenate.39
  397.9 4.8 pad_maximum_fusion.1
  404.1 6.2 convolution_convert_fusion.1
  410.3 4.9 multiply_convert_fusion.2
  416.7 4.3 convolution_convert_fusion
  431.8 5.1 fusion.21
  436.9 21.6 %all_to_all.40 = bf16[8,48,768]{2,1,0:T(8,128)(2,1)} all-to-all(bf16[8,48,768]{2,1,0:T(8,128)(2,1)S(1)} %bitcast.167), channel_id=1, replica_groups=mesh['frame'=4,'pos'=8] {'pos'}, dimensions={0} | all-to-all | bytes 1179648 | tf_op jit(solution)/shard_map/all_to_all | solution.py:147
  464.4 6.6 all-to-all-done.3
  470.9 3.6 all-to-all-start.7
  474.6 50.1 %all-reduce.6.cloned.1.call-done = (f32[4,3,768]{2,0,1:T(4,128)}, f32[768,18]{1,0:T(8,128)}) async-done(((f32[4,3,768]{2,0,1:T(4,128)}, f32[768,18]{1,0:T(8,128)}), (f32[4,3,768]{2,0,1:T(4,128)}, f32[768,18]{1,0:T(8,128)})) %all-reduce.6.cloned.1.call-update) | async-done | bytes 92176 | tf_op jit(solution)/shard_map/psum | solution.py:264
  532.4 106.5 %reduce-scatter.7.cloned.1.call-done = bf16[24,3072]{1,0:T(8,128)(2,1)} async-done(((bf16[768,3072]{1,0:T(8,128)(2,1)}), bf16[24,3072]{1,0:T(8,128)(2,1)}) %reduce-scatter.7.cloned.1.call-update) | async-done | bytes 147472 | tf_op jit(solution)/shard_map/reduce_scatter | solution.py:278
  641.9 108.6 %reduce-scatter.9.cloned.1.call-done = bf16[24,3072]{1,0:T(8,128)(2,1)} async-done(((bf16[768,3072]{1,0:T(8,128)(2,1)}), bf16[24,3072]{1,0:T(8,128)(2,1)}) %reduce-scatter.9.cloned.1.call-update) | async-done | bytes 147472 | tf_op jit(solution)/shard_map/reduce_scatter | solution.py:277
  752.1 110.9 %reduce-scatter.11.cloned.1.call-done = bf16[96,768]{1,0:T(8,128)(2,1)} async-done(((bf16[3072,768]{1,0:T(8,128)(2,1)}), bf16[96,768]{1,0:T(8,128)(2,1)}) %reduce-scatter.11.cloned.1.call-update) | async-done | bytes 147472 | tf_op jit(solution)/shard_map/reduce_scatter | solution.py:276
  864.6 115.9 %reduce-scatter.5.cloned.1.call-done = bf16[24,3840]{1,0:T(8,128)(2,1)} async-done(((bf16[768,3840]{1,0:T(8,128)(2,1)}), bf16[24,3840]{1,0:T(8,128)(2,1)}) %reduce-scatter.5.cloned.1.call-update) | async-done | bytes 184336 | tf_op jit(solution)/shard_map/reduce_scatter | solution.py:279
  (339 shorter events, 151.3 us)
Async XLA Ops:
  7.2 106.4 %copy-start = (bf16[4,3,768]{2,0,1:T(4,128)(2,1)S(1)}, bf16[4,3,768]{2,0,1:T(4,128)(2,1)}, u32[]{:S(2)}) copy-start(bf16[4,3,768]{2,0,1:T(4,128)(2,1)} %param.16) | copy-start | bytes 55300
  7.2 82.7 %all-gather.5.cloned.1.call-start = ((), (), s32[]{:S(2)}) async-start(), calls=%async_computation.12 | async-start | bytes 6082560 | tf_op jit(solution)/shard_map/all_gather | solution.py:128
  8.9 150.4 %all-gather.7.cloned.1.call-start = ((), (), s32[]{:S(2)}) async-start(), calls=%async_computation.13 | async-start | bytes 4866048 | tf_op jit(solution)/shard_map/all_gather | solution.py:130
  10.6 214.3 %all-gather.9.cloned.1.call-start = ((), (), s32[]{:S(2)}) async-start(), calls=%async_computation.14 | async-start | bytes 4866048 | tf_op jit(solution)/shard_map/all_gather | solution.py:131
  13.5 55.0 %all-to-all-start = ((bf16[4,96,768]{2,1,0:T(8,128)(2,1)}), bf16[4,96,768]{2,1,0:T(8,128)(2,1)S(1)}, u32[]{:S(2)}, u32[]{:S(2)}) async-start(bf16[4,96,768]{2,1,0:T(8,128)(2,1)} %copy.199), calls=%async_computation | async-start | bytes 1179648 | tf_op jit(solution)/shard_map/all_to_all | solution.py:143
  18.7 271.6 %all-gather.11.cloned.1.call-start = ((), (), s32[]{:S(2)}) async-start(), calls=%async_computation.15 | async-start | bytes 4866048 | tf_op jit(solution)/shard_map/all_gather | solution.py:132
  20.6 46.5 %copy-start.50 = (bf16[4,12,7,768]{3,0,2,1:T(4,128)(2,1)S(1)}, bf16[4,12,7,768]{3,0,2,1:T(4,128)(2,1)}, u32[]{:S(2)}) copy-start(bf16[4,12,7,768]{3,0,2,1:T(4,128)(2,1)} %param.18) | copy-start | bytes 1548292
  67.2 92.2 %copy-start.73 = (f32[768]{0:T(1024)}, f32[768]{0:T(1024)S(1)}, u32[]{:S(2)}) copy-start(f32[768]{0:T(1024)S(1)} %get-tuple-element.102) | copy-start | bytes 9220
  67.2 157.7 %copy-start.71 = (f32[768]{0:T(1024)}, f32[768]{0:T(1024)S(1)}, u32[]{:S(2)}) copy-start(f32[768]{0:T(1024)S(1)} %get-tuple-element.97) | copy-start | bytes 9220
  67.2 242.7 %copy-start.61 = (f32[768]{0:T(1024)}, f32[768]{0:T(1024)S(1)}, u32[]{:S(2)}) copy-start(f32[768]{0:T(1024)S(1)} %get-tuple-element.98) | copy-start | bytes 9220
  67.2 272.5 %copy-start.59 = (f32[768]{0:T(1024)}, f32[768]{0:T(1024)S(1)}, u32[]{:S(2)}) copy-start(f32[768]{0:T(1024)S(1)} %get-tuple-element.103) | copy-start | bytes 9220
  68.5 31.7 %copy-start.22 = (pred[384,384]{0,1:T(8,128)(4,1)}, pred[384,384]{0,1:T(8,128)(4,1)S(1)}, u32[]{:S(2)}) copy-start(pred[384,384]{0,1:T(8,128)(4,1)S(1)} %broadcast_compare_fusion) | copy-start | bytes 442372
  68.6 13.8 %all-to-all-start.4 = ((bf16[4,96,768]{2,1,0:T(8,128)(2,1)}), bf16[4,96,768]{2,1,0:T(8,128)(2,1)}, u32[]{:S(2)}, u32[]{:S(2)}) async-start(bf16[4,96,768]{2,1,0:T(8,128)(2,1)} %pad_bitcast_fusion), calls=%async_computation.4 | async-start | bytes 1179648 | tf_op jit(solution)/shard_map/all_to_all | solution.py:143
  82.3 26.5 %all-to-all-start.5 = ((bf16[8,48,768]{2,1,0:T(8,128)(2,1)}), bf16[8,48,768]{2,1,0:T(8,128)(2,1)S(1)}, u32[]{:S(2)}, u32[]{:S(2)}) async-start(bf16[8,48,768]{2,1,0:T(8,128)(2,1)} %bitcast.21), calls=%async_computation.5 | async-start | bytes 1179648 | tf_op jit(solution)/shard_map/all_to_all | solution.py:147
  108.8 54.2 %copy-start.18 = (bf16[8,48,768]{2,1,0:T(8,128)(2,1)}, bf16[8,48,768]{2,1,0:T(8,128)(2,1)S(1)}, u32[]{:S(2)}) copy-start(bf16[8,48,768]{2,1,0:T(8,128)(2,1)S(1)} %all-to-all-done.5) | copy-start | bytes 1769476
  108.8 27.4 %all-to-all-start.1 = ((bf16[8,48,768]{2,1,0:T(8,128)(2,1)}), bf16[8,48,768]{2,1,0:T(8,128)(2,1)S(1)}, u32[]{:S(2)}, u32[]{:S(2)}) async-start(bf16[8,48,768]{2,1,0:T(8,128)(2,1)} %bitcast.10), calls=%async_computation.1 | async-start | bytes 1179648 | tf_op jit(solution)/shard_map/all_to_all | solution.py:147
  113.8 57.6 %copy-start.24 = (pred[384,384]{0,1:T(8,128)(4,1)}, pred[384,384]{0,1:T(8,128)(4,1)S(1)}, u32[]{:S(2)}) copy-start(pred[384,384]{0,1:T(8,128)(4,1)S(1)} %compare_and_fusion) | copy-start | bytes 442372
  138.7 36.1 %copy-start.4 = (f32[384,768]{1,0:T(8,128)}, f32[384,768]{1,0:T(8,128)S(1)}, u32[]{:S(2)}) copy-start(f32[384,768]{1,0:T(8,128)S(1)} %get-tuple-element.140) | copy-start | bytes 3538948
  139.0 200.7 %copy-start.66 = (f32[384]{0:T(512)}, f32[384]{0:T(512)S(1)}, u32[]{:S(2)}) copy-start(f32[384]{0:T(512)S(1)} %add_rsqrt_fusion.1) | copy-start | bytes 4612
  177.0 132.8 %copy-start.8 = (f32[384,768]{1,0:T(8,128)}, f32[384,768]{1,0:T(8,128)S(1)}, u32[]{:S(2)}) copy-start(f32[384,768]{1,0:T(8,128)S(1)} %get-tuple-element.144) | copy-start | bytes 3538948
  177.3 132.6 %copy-start.64 = (f32[384]{0:T(512)}, f32[384]{0:T(512)S(1)}, u32[]{:S(2)}) copy-start(f32[384]{0:T(512)S(1)} %add_rsqrt_fusion) | copy-start | bytes 4612
  224.9 65.4 %copy-start.19 = (bf16[8,48,768]{2,1,0:T(8,128)(2,1)S(1)}, bf16[8,48,768]{2,1,0:T(8,128)(2,1)}, u32[]{:S(2)}) copy-start(bf16[8,48,768]{2,1,0:T(8,128)(2,1)} %copy-done.18) | copy-start | bytes 1769476
  341.4 21.0 %all-to-all-start.6 = ((bf16[8,48,768]{2,1,0:T(8,128)(2,1)}), bf16[8,48,768]{2,1,0:T(8,128)(2,1)}, u32[]{:S(2)}, u32[]{:S(2)}) async-start(bf16[8,48,768]{2,1,0:T(8,128)(2,1)} %bitcast.146), calls=%async_computation.6 | async-start | bytes 1179648 | tf_op jit(solution)/shard_map/all_to_all | solution.py:147
  345.6 179.1 %all-reduce.6.cloned.1.call-start = ((), (), s32[]{:S(2)}) async-start(), calls=%async_computation.20 | async-start | bytes 860160 | tf_op jit(solution)/shard_map/psum | solution.py:264
  397.9 241.0 %reduce-scatter.7.cloned.1.call-start = ((), (), s32[]{:S(2)}) async-start(), calls=%async_computation.17 | async-start | bytes 4866048 | tf_op jit(solution)/shard_map/reduce_scatter | solution.py:278
  402.8 347.6 %reduce-scatter.9.cloned.1.call-start = ((), (), s32[]{:S(2)}) async-start(), calls=%async_computation.18 | async-start | bytes 4866048 | tf_op jit(solution)/shard_map/reduce_scatter | solution.py:277
  410.3 452.7 %reduce-scatter.11.cloned.1.call-start = ((), (), s32[]{:S(2)}) async-start(), calls=%async_computation.19 | async-start | bytes 4866048 | tf_op jit(solution)/shard_map/reduce_scatter | solution.py:276
  421.0 559.5 %reduce-scatter.5.cloned.1.call-start = ((), (), s32[]{:S(2)}) async-start(), calls=%async_computation.16 | async-start | bytes 6082560 | tf_op jit(solution)/shard_map/reduce_scatter | solution.py:279
  458.5 12.5 %all-to-all-start.3 = ((bf16[4,96,768]{2,1,0:T(8,128)(2,1)}), bf16[4,96,768]{2,1,0:T(8,128)(2,1)S(1)}, u32[]{:S(2)}, u32[]{:S(2)}) async-start(bf16[4,96,768]{2,1,0:T(8,128)(2,1)} %bitcast.18), calls=%async_computation.3 | async-start | bytes 1179648 | tf_op jit(solution)/shard_map/all_to_all | solution.py:143
  470.9 513.2 %copy-start.1 = (bf16[4,3,768]{2,0,1:T(4,128)(2,1)S(1)}, bf16[4,3,768]{2,0,1:T(4,128)(2,1)}, u32[]{:S(2)}) copy-start(bf16[4,3,768]{2,0,1:T(4,128)(2,1)} %param.16) | copy-start | bytes 55300
  470.9 59.9 %all-to-all-start.7 = ((bf16[4,96,768]{2,1,0:T(8,128)(2,1)}), bf16[4,96,768]{2,1,0:T(8,128)(2,1)S(1)}, u32[]{:S(2)}, u32[]{:S(2)}) async-start(bf16[4,96,768]{2,1,0:T(8,128)(2,1)} %bitcast.39), calls=%async_computation.7 | async-start | bytes 1179648 | tf_op jit(solution)/shard_map/all_to_all | solution.py:143
  524.7 458.9 %copy-start.52 = (f32[4,3,768]{2,0,1:T(4,128)S(1)}, f32[4,3,768]{2,0,1:T(4,128)}, u32[]{:S(2)}) copy-start(f32[4,3,768]{2,0,1:T(4,128)} %get-tuple-element.158) | copy-start | bytes 110596
  (73 other events, 455.9 us)
Sparse Core Ops, SparseCore 0:
  11.7 78.1 all-gather.4
  93.5 65.8 all-gather.6
  162.4 62.4 all-gather.8
  227.8 62.4 all-gather.10
  398.0 126.6 all-reduce.5
  530.9 107.9 reduce-scatter.6
  644.4 106.0 reduce-scatter.8
  756.8 106.0 reduce-scatter.10
  868.6 111.8 reduce-scatter.4

commit v2 on v1

--- a/solution.py
+++ b/solution.py
@@ -3,6 +3,8 @@
 import jax
 import jax.numpy as jnp
 from jax import lax
+from jax.experimental import pallas as pl
+from jax.experimental.pallas import tpu as pltpu
 from jax.sharding import PartitionSpec as P
 
 D = 768
@@ -11,6 +13,188 @@
 MB = 4
 CLIPS = 3
 AXES = ("frame", "pos")
+
+
+def send(values, perm):
+    return lax.ppermute(values, AXES, perm)
+
+
+def tie(value, *before):
+    return lax.optimization_barrier((value,) + before)[0]
+
+
+class Layout:
+    def __init__(self):
+        self.frames, self.chips = lax.axis_size("frame"), lax.axis_size("pos") // 2
+        self.bits = self.frames.bit_length() - 1
+        self.frame, self.chip = lax.axis_index("frame"), lax.axis_index("pos") // 2
+        self.core = lax.axis_index("pos") % 2
+        self.swap = self.perm(lambda f, z, c: (f, z, 1 - c))
+        self.along = [self.perm(lambda f, z, c, i=i: (f, z ^ i, c)) for i in range(1, self.chips)]
+        self.across = [
+            self.perm(lambda f, z, c, k=k: (f ^ (1 << self.bit(k, c)), z, c))
+            for k in range(self.bits)
+        ]
+
+    def bit(self, step, core):
+        return (step + core) % self.bits
+
+    def perm(self, to):
+        pairs = []
+        for f in range(self.frames):
+            for z in range(self.chips):
+                for c in range(2):
+                    g, y, d = to(f, z, c)
+                    pairs.append(
+                        ((f * self.chips + z) * 2 + c, (g * self.chips + y) * 2 + d)
+                    )
+        return pairs
+
+    def table(self):
+        rows = []
+        for core in (self.core, 1 - self.core):
+            blocks = []
+            for b in range(self.frames * self.chips):
+                flags, i = b // self.chips, b % self.chips
+                f = self.frame
+                for k in range(self.bits):
+                    if flags >> k & 1:
+                        f = f ^ (1 << ((k + core) % self.bits))
+                blocks.append(f * self.chips + (self.chip ^ i))
+            rows.append(jnp.stack(blocks))
+        return jnp.concatenate([jnp.stack(rows).reshape(-1), self.core[None]]).astype(jnp.int32)
+
+    def pick(self, low, high):
+        return jnp.where(self.core == 0, low, high), jnp.where(self.core == 0, high, low)
+
+    def chip_rows(self, mats):
+        low = jnp.concatenate([m[:, : m.shape[1] // 2] for m in mats], axis=1)
+        high = jnp.concatenate([m[:, m.shape[1] // 2 :] for m in mats], axis=1)
+        keep, give = self.pick(low, high)
+        got = send(give, self.swap)
+        first, second = self.pick(keep, got)
+        return jnp.concatenate([first, second], axis=0)
+
+    def gather(self, owned):
+        block = jnp.stack([owned] + [send(owned, p) for p in self.along])
+        for p in self.across:
+            block = jnp.concatenate([block, send(block, p)])
+        return block, send(block, self.swap)
+
+    def scatter(self, mine, other):
+        f32, bf16 = jnp.float32, jnp.bfloat16
+        got = send(other, self.swap)
+        for p in reversed(self.across):
+            half = mine.shape[0] // 2
+            far = (mine[half:].astype(f32) + got[half:].astype(f32)).astype(bf16)
+            mine = (mine[:half].astype(f32) + got[:half].astype(f32)).astype(bf16)
+            got = send(far, p)
+        mine = mine.astype(f32) + got.astype(f32)
+        total = mine[0]
+        parts = mine.astype(bf16)
+        for i, p in enumerate(self.along):
+            total = total + send(parts[i + 1], p).astype(f32)
+        rows = total.shape[0] // 2
+        first, second = total[:rows], total[rows:]
+        keep, give = self.pick(first, second)
+        got = send(give, self.swap)
+        return self.pick(keep, got)
+
+    def split(self, low, high, widths):
+        mats, at = [], 0
+        for width in widths:
+            half = width // 2
+            mats.append(jnp.concatenate([low[:, at : at + half], high[:, at : at + half]], axis=1))
+            at += half
+        return mats
+
+
+def join_kernel(blocks, rows, widths, table, mine, other, *refs):
+    outs, sem = refs[: len(widths)], refs[-1]
+    core = table[2 * blocks]
+
+    def body(b, carry):
+        for side, source in ((0, mine), (1, other)):
+            row = pl.multiple_of(table[side * blocks + b] * rows, rows)
+            half = core if side == 0 else 1 - core
+            at = 0
+            for i, width in enumerate(widths):
+                w = width // 2
+                pltpu.make_async_copy(
+                    source.at[b, :, at : at + w],
+                    outs[i].at[pl.ds(row, rows), pl.ds(pl.multiple_of(half * w, 128), w)],
+                    sem.at[i],
+                ).start()
+                at += w
+        return carry
+
+    lax.fori_loop(0, blocks, body, 0)
+    for i in range(len(widths)):
+        pltpu.make_async_copy(outs[i], outs[i], sem.at[i]).wait()
+
+
+def join(layout, table, mine, other, widths):
+    blocks, rows, _ = mine.shape
+    if rows % 16:
+        order = jnp.argsort(table[: 2 * blocks].reshape(2, blocks), axis=1)
+        halves = [a[o].reshape(blocks * rows, -1) for a, o in zip((mine, other), order)]
+        return layout.split(*layout.pick(*halves), widths)
+    anywhere = pl.BlockSpec(memory_space=pl.ANY)
+    return pl.pallas_call(
+        partial(join_kernel, blocks, rows, widths),
+        out_shape=[jax.ShapeDtypeStruct((blocks * rows, w), mine.dtype) for w in widths],
+        in_specs=[pl.BlockSpec(memory_space=pltpu.SMEM), anywhere, anywhere],
+        out_specs=[pl.BlockSpec(memory_space=pltpu.VMEM)] * len(widths),
+        scratch_shapes=[pltpu.SemaphoreType.DMA((len(widths),))],
+        compiler_params=pltpu.CompilerParams(vmem_limit_bytes=48 << 20),
+        name="join",
+    )(table, mine, other)
+
+
+def part_kernel(blocks, rows, widths, table, *refs):
+    mats, mine, other, sem = refs[: len(widths)], refs[-3], refs[-2], refs[-1]
+    core = table[2 * blocks]
+
+    def body(b, carry):
+        for side, target in ((0, mine), (1, other)):
+            row = pl.multiple_of(table[side * blocks + b] * rows, rows)
+            half = core if side == 0 else 1 - core
+            at = 0
+            for i, width in enumerate(widths):
+                w = width // 2
+                pltpu.make_async_copy(
+                    mats[i].at[pl.ds(row, rows), pl.ds(pl.multiple_of(half * w, 128), w)],
+                    target.at[b, :, at : at + w],
+                    sem.at[side],
+                ).start()
+                at += w
+        return carry
+
+    lax.fori_loop(0, blocks, body, 0)
+    pltpu.make_async_copy(mine, mine, sem.at[0]).wait()
+    pltpu.make_async_copy(other, other, sem.at[1]).wait()
+
+
+def part(layout, table, mats, blocks):
+    widths = [m.shape[1] for m in mats]
+    rows = mats[0].shape[0] // blocks
+    if rows % 16:
+        low = jnp.concatenate([m[:, : m.shape[1] // 2] for m in mats], axis=1)
+        high = jnp.concatenate([m[:, m.shape[1] // 2 :] for m in mats], axis=1)
+        order = table[: 2 * blocks].reshape(2, blocks)
+        return [a.reshape(blocks, rows, -1)[o] for a, o in zip(layout.pick(low, high), order)]
+    anywhere = pl.BlockSpec(memory_space=pl.ANY)
+    shape = jax.ShapeDtypeStruct((blocks, rows, sum(widths) // 2), mats[0].dtype)
+    return pl.pallas_call(
+        partial(part_kernel, blocks, rows, widths),
+        out_shape=[shape, shape],
+        in_specs=[pl.BlockSpec(memory_space=pltpu.SMEM)]
+        + [pl.BlockSpec(memory_space=pltpu.VMEM)] * len(mats),
+        out_specs=[anywhere, anywhere],
+        scratch_shapes=[pltpu.SemaphoreType.DMA((2,))],
+        compiler_params=pltpu.CompilerParams(vmem_limit_bytes=48 << 20),
+        name="part",
+    )(table, *mats)
 
 
 def norm_forward(values, gain_vec, shift_vec):
@@ -121,17 +305,27 @@
     rows_count = all_frames * my_slots
     micro = frame_index // share
 
-    gather = partial(lax.all_gather, axis_name=AXES, axis=0, tiled=True)
+    layout = Layout()
+    table = layout.table()
+    blocks = frame_size * pos_size // 2
     small = jnp.concatenate(
         [mlp_in_bias.reshape(shard, 4), norm_gains, norm_shifts, biases], axis=1
     )
-    chunk_t = gather(jnp.concatenate([temporal_qkv, temporal_proj, temporal_fc], axis=1))
-    small = gather(small).astype(f32)
-    chunk_s = gather(jnp.concatenate([spatial_qkv, spatial_proj], axis=1))
-    w_in = gather(mlp_in)
-    w_out = gather(mlp_out)
-    w_tqkv, w_tproj, w_tfc = chunk_t[:, : 3 * D], chunk_t[:, 3 * D : 4 * D], chunk_t[:, 4 * D :]
-    w_sqkv, w_sproj = chunk_s[:, : 3 * D], chunk_s[:, 3 * D :]
+    small = jnp.pad(small, ((0, 0), (0, 256 - small.shape[1])))
+    widths_t, widths_s, widths_in, widths_out = (3 * D, D, D, 256), (3 * D, D), (4 * D,), (D,)
+    gathered, last = [], None
+    for mats in (
+        (temporal_qkv, temporal_proj, temporal_fc, small),
+        (spatial_qkv, spatial_proj),
+        (mlp_in,),
+        (mlp_out,),
+    ):
+        gathered.append(layout.gather(layout.chip_rows(mats)))
+    w_tqkv, w_tproj, w_tfc, small = join(layout, table, *gathered[0], widths_t)
+    w_sqkv, w_sproj = join(layout, table, *gathered[1], widths_s)
+    (w_in,) = join(layout, table, *gathered[2], widths_in)
+    (w_out,) = join(layout, table, *gathered[3], widths_out)
+    small = small[:, :18].astype(f32)
     in_bias = small[:, :4].reshape(-1)
     rows_small = small[:, 4:].T
     gains, shifts, bias_rows = rows_small[:3], rows_small[3:6], rows_small[6:]
@@ -262,7 +456,6 @@
     class_all = jnp.zeros((MB, CLIPS, D), f32)
     class_all = lax.dynamic_update_index_in_dim(class_all, class_part, micro, 0)
     class_grad = lax.psum(class_all, AXES)
-    scatter = partial(lax.psum_scatter, axis_name=AXES, scatter_dimension=0, tiled=True)
     sum_s = column_sum(grad_packed_s)
     sum_t = column_sum(grad_packed_t)
     small_grads = jnp.stack(
@@ -272,26 +465,31 @@
         axis=1,
     )
     small_grads = jnp.concatenate([column_sum(grad_hidden).reshape(D, 4), small_grads], axis=1)
-    small_grads = scatter(small_grads)
-    acc_out = scatter(acc_out).astype(f32)
-    acc_in = scatter(acc_in).astype(f32)
-    acc_s = scatter(jnp.concatenate([acc_sqkv, acc_sproj], axis=1)).astype(f32)
-    acc_t = scatter(jnp.concatenate([acc_tqkv, acc_tproj, acc_tfc], axis=1)).astype(f32)
+    small_grads = jnp.pad(small_grads, ((0, 0), (0, 256 - small_grads.shape[1]))).astype(bf16)
+    scatter = lambda mats, widths: layout.split(
+        *layout.scatter(*part(layout, table, mats, blocks)), widths
+    )
+    (acc_out,) = scatter([acc_out], widths_out)
+    (acc_in,) = scatter([acc_in], widths_in)
+    acc_sqkv, acc_sproj = scatter([acc_sqkv, acc_sproj], widths_s)
+    acc_tqkv, acc_tproj, acc_tfc, small_grads = scatter(
+        [acc_tqkv, acc_tproj, acc_tfc, small_grads], widths_t
+    )
     return (
         block_out,
         tokens_grad,
         class_grad,
-        acc_t[:, : 3 * D],
-        acc_t[:, 3 * D : 4 * D],
-        acc_t[:, 4 * D :],
-        acc_s[:, : 3 * D],
-        acc_s[:, 3 * D :],
+        acc_tqkv,
+        acc_tproj,
+        acc_tfc,
+        acc_sqkv,
+        acc_sproj,
         acc_in,
         acc_out,
         small_grads[:, :4].reshape(-1),
         small_grads[:, 4:7],
         small_grads[:, 7:10],
-        small_grads[:, 10:],
+        small_grads[:, 10:18],
     )
 
 

time: 997 us -> 605 us (0.61)
  waiting for transfers between devices: 661 us -> 146 us
  starting transfers between devices: 29.4 us -> 123 us
  Pallas kernels: 0 us -> 35 us
  blocking collectives: 65.1 us -> 41.6 us
  other arithmetic: 38.3 us -> 61.3 us
  local copies, waits for them, and re-layouts: 63.5 us -> 76.3 us
  between operations: 15.7 us -> 2.93 us
    reduce_scatter x4 -> x0, waiting for transfers between devices: 442 us -> none  [the longest x1 116 us: on_device(): scatter(jnp.concatenate([acc_tqkv, acc_tproj, acc_tfc], axis=1)).astype(f32)]
    all_gather x4 -> x0, waiting for transfers between devices: 130 us -> none  [the longest x1 58.8 us: on_device(): w_out = gather(mlp_out)]
    ppermute x0 -> x56, waiting for transfers between devices: none -> 107 us  [send(): return lax.ppermute(values, AXES, perm)]
    ppermute x0 -> x56, starting transfers between devices: none -> 83.9 us  [send(): return lax.ppermute(values, AXES, perm)]
    psum x1 -> x0, waiting for transfers between devices: 50.1 us -> none  [on_device(): class_grad = lax.psum(class_all, AXES)]
    all_gather x1 -> x0, blocking collectives: 43.5 us -> none  [on_device(): small = gather(small).astype(f32)]
    psum x0 -> x1, blocking collectives: none -> 41.6 us  [on_device(): class_grad = lax.psum(class_all, AXES)]
    pallas_call x0 -> x8, Pallas kernels: none -> 35 us  [the longest x4 19.6 us: join(): pl.pallas_call(partial(join_kernel, blocks, rows, widths), out_shape=[jax...]
  transfers between devices with their start and end apart: 16 -> 64, of which waited for: 13 -> 19; matrix products, arithmetic and copies ran while one was open for 12% -> 27% of each run, Pallas kernels for 0% -> 5%
where the time goes in v2:
time: 605 us; the launch traced here: 597 us
  waiting for transfers between devices  146 us (24%)
  starting transfers between devices  123 us (20%)
  matrix products  111 us (18%)
  local copies, waits for them, and re-layouts  76.3 us (13%)
  other arithmetic  61.3 us (10%)
  blocking collectives  41.6 us (7%)
  Pallas kernels  35 us (6%)
    ppermute x56, waiting for transfers between devices, send(): return lax.ppermute(values, AXES, perm)  107 us
    ppermute x56, starting transfers between devices, send(): return lax.ppermute(values, AXES, perm)  83.9 us
    psum x1, blocking collectives, on_device(): class_grad = lax.psum(class_all, AXES)  41.6 us
    all_to_all x4, waiting for transfers between devices, frame_hop(): return lax.all_to_all(values, 'frame', 0, 0, tiled=True)  38.4 us
    dot_general x7, matrix products, back_mul(): lax.dot_general(upstream, weight, (((1,), (1,)), ((), ())), preferred_ele...  32.9 us
    dot_general x7, matrix products, outer_sum(): lax.dot_general(left_mat, right_mat, (((0,), (0,)), ((), ())), preferred_...  24.6 us
    all_to_all x4, starting transfers between devices, pos_hop(): return lax.all_to_all(parts, 'pos', 0, 0, tiled=True).reshape(rows_count, D)  20.7 us
    unnamed x224, local copies, waits for them, and re-layouts  20.6 us
  transfers between devices with their start and end apart: 64, of which 19 were waited for; matrix products, arithmetic and copies ran while one was open for 27% of the time, Pallas kernels for 5%

profile of v2, /device:TPU:0, one launch (start us, length us, event | category | flops | bytes accessed | tf_op | source)
XLA Modules:
  0.0 596.9 jit_solution(8691691814987441432)
XLA Ops:
  13.2 5.3 all-to-all-start
  32.9 7.4 %collective-permute-done.15 = bf16[48,1536]{1,0:T(8,128)(2,1)S(1)} collective-permute-done((bf16[48,1536]{1,0:T(8,128)(2,1)S(1)}, bf16[48,1536]{1,0:T(8,128)(2,1)S(1)}, u32[]{:S(2)}, u32[]{:S(2)}) %collective-permute-start.15) | collective-permute-done | bytes 147488 | tf_op jit(solution)/shard_map/ppermute | solution.py:19
  42.4 5.0 collective-permute-done.16
  47.4 7.1 %collective-permute-start.22 = (bf16[192,384]{1,0:T(8,128)(2,1)S(1)}, bf16[192,384]{1,0:T(8,128)(2,1)S(1)}, u32[]{:S(2)}, u32[]{:S(2)}) collective-permute-start(bf16[192,384]{1,0:T(8,128)(2,1)S(1)} %get-tuple-element.226), channel_id=1, source_target_pairs={{0,2},{1,3},{2,0},{3,1},{4,6},{5,7},{6,4},{7,5},{8,10},{9,11},{10,... | collective-permute-start | bytes 442376 | tf_op jit(solution)/shard_map/ppermute | solution.py:19
  67.4 6.8 %collective-permute-done.2 = bf16[48,2048]{1,0:T(8,128)(2,1)S(1)} collective-permute-done((bf16[48,2048]{1,0:T(8,128)(2,1)S(1)}, bf16[48,2048]{1,0:T(8,128)(2,1)S(1)}, u32[]{:S(2)}, u32[]{:S(2)}) %collective-permute-start.2) | collective-permute-done | bytes 196640 | tf_op jit(solution)/shard_map/ppermute | solution.py:19
  79.3 14.2 %collective-permute-done.4 = bf16[4,48,2048]{2,1,0:T(8,128)(2,1)S(1)} collective-permute-done((bf16[4,48,2048]{2,1,0:T(8,128)(2,1)S(1)}, bf16[4,48,2048]{2,1,0:T(8,128)(2,1)S(1)}, u32[]{:S(2)}, u32[]{:S(2)}) %collective-permute-start.4) | collective-permute-done | bytes 786464 | tf_op jit(solution)/shard_map/ppermute | solution.py:19
  98.3 15.8 %collective-permute-done.5 = bf16[8,48,2048]{2,1,0:T(8,128)(2,1)S(1)} collective-permute-done((bf16[8,48,2048]{2,1,0:T(8,128)(2,1)S(1)}, bf16[8,48,2048]{2,1,0:T(8,128)(2,1)S(1)}, u32[]{:S(2)}, u32[]{:S(2)}) %collective-permute-start.5) | collective-permute-done | bytes 1572896 | tf_op jit(solution)/shard_map/ppermute | solution.py:19
  131.4 35.2 %all-to-all-done.4 = bf16[4,96,768]{2,1,0:T(8,128)(2,1)} async-done(((bf16[4,96,768]{2,1,0:T(8,128)(2,1)}), bf16[4,96,768]{2,1,0:T(8,128)(2,1)}, u32[]{:S(2)}, u32[]{:S(2)}) %all-to-all-start.4) | async-done | bytes 589856 | tf_op jit(solution)/shard_map/all_to_all | solution.py:337
  166.6 6.3 %all-to-all-start.5 = ((bf16[8,48,768]{2,1,0:T(8,128)(2,1)}), bf16[8,48,768]{2,1,0:T(8,128)(2,1)}, u32[]{:S(2)}, u32[]{:S(2)}) async-start(bf16[8,48,768]{2,1,0:T(8,128)(2,1)} %bitcast.68), calls=%async_computation.5 | async-start | bytes 1179648 | tf_op jit(solution)/shard_map/all_to_all | solution.py:341
  202.0 5.0 all-to-all-start.1
  209.9 5.1 join.7
  215.0 5.1 join.6
  220.2 4.8 join.5
  246.5 16.5 %fusion.88 = (bf16[3072]{0:T(1024)(128)(2,1)}, bf16[384,3072]{1,0:T(8,128)(2,1)S(1)}, f32[384,3072]{1,0:T(8,128)}) fusion(f32[384,3072]{1,0:T(8,128)S(1)} %convolution_add_fusion.2, bf16[384,768]{1,0:T(8,128)(2,1)} %bitcast.69, bf16[3072,768]{1,0:T(8,128)(2,1)S(1)} %bitcast.282), kind=kOutput, calls=%fused_computation.340 | convolution fusion | flops 1898050560 | bytes 17111040 | tf_op jit(solution)/shard_map/dot_general | solution.py:227
  270.3 4.8 convolution_convert_fusion.1.refs_0_
  276.5 5.9 convolution_convert_fusion.10
  282.4 4.6 multiply_reduce_fusion.1
  303.4 5.6 convolution_convert_fusion.refs_0_
  318.1 5.0 all-to-all-start.6
  328.1 5.8 convolution_convert_fusion.2.refs_0_
  339.4 41.6 %psum.7 = f32[4,3,768]{2,0,1:T(4,128)} all-reduce(f32[4,3,768]{2,0,1:T(4,128)S(1)} %dynamic_update_slice.4), channel_id=1, replica_groups=mesh['frame'=4,'pos'=8] {'frame','pos'}, use_global_device_ids=true, to_apply=%region_21.22 | all-reduce | flops 9216 | bytes 73728 | tf_op jit(solution)/shard_map/psum | solution.py:458
  381.0 6.2 %fusion.15 = bf16[384,768]{1,0:T(8,128)(2,1)} fusion(f32[384,768]{1,0:T(8,128)} %copy-done.19, bf16[384,3072]{1,0:T(8,128)(2,1)} %multiply_convert_fusion.2, bf16[3072,768]{1,0:T(8,128)(2,1)} %join.7, f32[768]{0:T(1024)} %get-tuple-element.110), kind=kOutput, calls=%fused_computation.68 | convolution fusion | flops 1812824064 | bytes 8850432 | tf_op jit(solution)/shard_map/dot_general | solution.py:217
  398.0 5.6 multiply_reduce_fusion
  424.9 5.3 multiply_reduce_fusion.4
  488.0 11.6 %collective-permute-done.36 = bf16[8,48,1536]{2,1,0:T(8,128)(2,1)} collective-permute-done((bf16[8,48,1536]{2,1,0:T(8,128)(2,1)}, bf16[8,48,1536]{2,1,0:T(8,128)(2,1)}, u32[]{:S(2)}, u32[]{:S(2)}) %collective-permute-start.36) | collective-permute-done | bytes 1179680 | tf_op jit(solution)/shard_map/ppermute | solution.py:19
  522.9 7.6 %collective-permute-start.40 = (bf16[48,1536]{1,0:T(8,128)(2,1)S(1)}, bf16[48,1536]{1,0:T(8,128)(2,1)S(1)}, u32[]{:S(2)}, u32[]{:S(2)}) collective-permute-start(bf16[48,1536]{1,0:T(8,128)(2,1)S(1)} %get-tuple-element.167), channel_id=1, source_target_pairs={{0,6},{1,7},{2,4},{3,5},{4,2},{5,3},{6,0},{7,1},{8,14},{9,15},{10,... | collective-permute-start | bytes 442376 | tf_op jit(solution)/shard_map/ppermute | solution.py:19
  531.8 6.9 %collective-permute-done.46 = bf16[48,1536]{1,0:T(8,128)(2,1)S(1)} collective-permute-done((bf16[48,1536]{1,0:T(8,128)(2,1)S(1)}, bf16[48,1536]{1,0:T(8,128)(2,1)S(1)}, u32[]{:S(2)}, u32[]{:S(2)}) %collective-permute-start.46) | collective-permute-done | bytes 147488 | tf_op jit(solution)/shard_map/ppermute | solution.py:19
  539.4 5.1 collective-permute-done.39
  544.8 9.0 %collective-permute-done.29 = bf16[8,48,2048]{2,1,0:T(8,128)(2,1)S(1)} collective-permute-done((bf16[8,48,2048]{2,1,0:T(8,128)(2,1)S(1)}, bf16[8,48,2048]{2,1,0:T(8,128)(2,1)S(1)}, u32[]{:S(2)}, u32[]{:S(2)}) %collective-permute-start.29) | collective-permute-done | bytes 1572896 | tf_op jit(solution)/shard_map/ppermute | solution.py:19
  555.6 10.4 %collective-permute-done.30 = bf16[4,48,2048]{2,1,0:T(8,128)(2,1)S(1)} collective-permute-done((bf16[4,48,2048]{2,1,0:T(8,128)(2,1)S(1)}, bf16[4,48,2048]{2,1,0:T(8,128)(2,1)S(1)}, u32[]{:S(2)}, u32[]{:S(2)}) %collective-permute-start.30) | collective-permute-done | bytes 786464 | tf_op jit(solution)/shard_map/ppermute | solution.py:19
  566.5 9.7 %collective-permute-start.31 = (bf16[48,2048]{1,0:T(8,128)(2,1)S(1)}, bf16[48,2048]{1,0:T(8,128)(2,1)S(1)}, u32[]{:S(2)}, u32[]{:S(2)}) collective-permute-start(bf16[48,2048]{1,0:T(8,128)(2,1)S(1)} %get-tuple-element.155), channel_id=1, source_target_pairs={{0,2},{1,3},{2,0},{3,1},{4,6},{5,7},{6,4},{7,5},{8,10},{9,11},{10,... | collective-permute-start | bytes 589832 | tf_op jit(solution)/shard_map/ppermute | solution.py:19
  580.8 5.4 collective-permute-done.33
  (545 shorter events, 298.2 us)
Async XLA Ops:
  1.6 25.8 %collective-permute-start.21 = (bf16[96,384]{1,0:T(8,128)(2,1)S(1)}, bf16[96,384]{1,0:T(8,128)(2,1)S(1)}, u32[]{:S(2)}, u32[]{:S(2)}) collective-permute-start(bf16[96,384]{1,0:T(8,128)(2,1)S(1)} %broadcast_select_fusion.10), channel_id=1, source_target_pairs={{0,1},{1,0},{2,3},{3,2},{4,5},{5,4},{6,7},{7,6},{8,9},{9,8},{10,11... | collective-permute-start | bytes 221192 | tf_op jit(solution)/shard_map/ppermute | solution.py:19
  3.1 23.5 %collective-permute-start.14 = (bf16[24,1536]{1,0:T(8,128)(2,1)S(1)}, bf16[24,1536]{1,0:T(8,128)(2,1)S(1)}, u32[]{:S(2)}, u32[]{:S(2)}) collective-permute-start(bf16[24,1536]{1,0:T(8,128)(2,1)S(1)} %broadcast_select_fusion.18), channel_id=1, source_target_pairs={{0,1},{1,0},{2,3},{3,2},{4,5},{5,4},{6,7},{7,6},{8,9},{9,8},{10,11... | collective-permute-start | bytes 221192 | tf_op jit(solution)/shard_map/ppermute | solution.py:19
  13.2 111.2 %all-to-all-start = ((bf16[4,96,768]{2,1,0:T(8,128)(2,1)}), bf16[4,96,768]{2,1,0:T(8,128)(2,1)}, u32[]{:S(2)}, u32[]{:S(2)}) async-start(bf16[4,96,768]{2,1,0:T(8,128)(2,1)} %copy.134), calls=%async_computation | async-start | bytes 1179648 | tf_op jit(solution)/shard_map/all_to_all | solution.py:337
  21.1 33.5 %collective-permute-start.9 = (bf16[48,1536]{1,0:T(8,128)(2,1)S(1)}, bf16[48,1536]{1,0:T(8,128)(2,1)S(1)}, u32[]{:S(2)}, u32[]{:S(2)}) collective-permute-start(bf16[48,1536]{1,0:T(8,128)(2,1)S(1)} %get-tuple-element.236), channel_id=1, source_target_pairs={{0,4},{1,5},{2,6},{3,7},{4,0},{5,1},{6,2},{7,3},{8,12},{9,13},{10,... | collective-permute-start | bytes 442376 | tf_op jit(solution)/shard_map/ppermute | solution.py:19
  24.3 33.7 %collective-permute-start.8 = (bf16[48,1536]{1,0:T(8,128)(2,1)S(1)}, bf16[48,1536]{1,0:T(8,128)(2,1)S(1)}, u32[]{:S(2)}, u32[]{:S(2)}) collective-permute-start(bf16[48,1536]{1,0:T(8,128)(2,1)S(1)} %get-tuple-element.236), channel_id=1, source_target_pairs={{0,2},{1,3},{2,0},{3,1},{4,6},{5,7},{6,4},{7,5},{8,10},{9,11},{10,... | collective-permute-start | bytes 442376 | tf_op jit(solution)/shard_map/ppermute | solution.py:19
  26.6 31.4 %collective-permute-start.10 = (bf16[48,1536]{1,0:T(8,128)(2,1)S(1)}, bf16[48,1536]{1,0:T(8,128)(2,1)S(1)}, u32[]{:S(2)}, u32[]{:S(2)}) collective-permute-start(bf16[48,1536]{1,0:T(8,128)(2,1)S(1)} %get-tuple-element.236), channel_id=1, source_target_pairs={{0,6},{1,7},{2,4},{3,5},{4,2},{5,3},{6,0},{7,1},{8,14},{9,15},{10,... | collective-permute-start | bytes 442376 | tf_op jit(solution)/shard_map/ppermute | solution.py:19
  62.5 59.1 %collective-permute-start.11 = (bf16[4,48,1536]{2,1,0:T(8,128)(2,1)S(1)}, bf16[4,48,1536]{2,1,0:T(8,128)(2,1)S(1)}, u32[]{:S(2)}, u32[]{:S(2)}) collective-permute-start(bf16[4,48,1536]{2,1,0:T(8,128)(2,1)S(1)} %pad_maximum_fusion.3), channel_id=1, source_target_pairs={{0,8},{1,17},{2,10},{3,19},{4,12},{5,21},{6,14},{7,23},{8,0},{9,25... | collective-permute-start | bytes 1769480 | tf_op jit(solution)/shard_map/ppermute | solution.py:19
  65.7 54.4 %collective-permute-start.18 = (bf16[4,48,1536]{2,1,0:T(8,128)(2,1)S(1)}, bf16[4,48,1536]{2,1,0:T(8,128)(2,1)S(1)}, u32[]{:S(2)}, u32[]{:S(2)}) collective-permute-start(bf16[4,48,1536]{2,1,0:T(8,128)(2,1)S(1)} %pad_maximum_fusion.4), channel_id=1, source_target_pairs={{0,8},{1,17},{2,10},{3,19},{4,12},{5,21},{6,14},{7,23},{8,0},{9,25... | collective-permute-start | bytes 1769480 | tf_op jit(solution)/shard_map/ppermute | solution.py:19
  74.2 43.2 %collective-permute-start.25 = (bf16[4,192,384]{2,1,0:T(8,128)(2,1)S(1)}, bf16[4,192,384]{2,1,0:T(8,128)(2,1)S(1)}, u32[]{:S(2)}, u32[]{:S(2)}) collective-permute-start(bf16[4,192,384]{2,1,0:T(8,128)(2,1)S(1)} %pad_maximum_fusion.5), channel_id=1, source_target_pairs={{0,8},{1,17},{2,10},{3,19},{4,12},{5,21},{6,14},{7,23},{8,0},{9,25... | collective-permute-start | bytes 1769480 | tf_op jit(solution)/shard_map/ppermute | solution.py:19
  114.2 67.0 %collective-permute-start.6 = (bf16[16,48,2048]{2,1,0:T(8,128)(2,1)S(1)}, bf16[16,48,2048]{2,1,0:T(8,128)(2,1)}, u32[]{:S(2)}, u32[]{:S(2)}) collective-permute-start(bf16[16,48,2048]{2,1,0:T(8,128)(2,1)S(1)} %constant_dynamic-update-slice_fusion.5.mine), channel_id=1, source_target_pairs={{0,1},{1,0},{2,3},{3,2},{4,5},{5,4},{6,7},{7,6},{8,9},{9,8},{10,11... | collective-permute-start | bytes 9437192 | tf_op jit(solution)/shard_map/ppermute | solution.py:19
  118.5 54.5 %collective-permute-start.26 = (bf16[8,192,384]{2,1,0:T(8,128)(2,1)}, bf16[8,192,384]{2,1,0:T(8,128)(2,1)}, u32[]{:S(2)}, u32[]{:S(2)}) collective-permute-start(bf16[8,192,384]{2,1,0:T(8,128)(2,1)} %get-tuple-element.173), channel_id=1, source_target_pairs={{0,16},{1,9},{2,18},{3,11},{4,20},{5,13},{6,22},{7,15},{8,24},{9,1... | collective-permute-start | bytes 3538952 | tf_op jit(solution)/shard_map/ppermute | solution.py:19
  121.2 54.7 %collective-permute-start.19 = (bf16[8,48,1536]{2,1,0:T(8,128)(2,1)}, bf16[8,48,1536]{2,1,0:T(8,128)(2,1)}, u32[]{:S(2)}, u32[]{:S(2)}) collective-permute-start(bf16[8,48,1536]{2,1,0:T(8,128)(2,1)} %get-tuple-element.171), channel_id=1, source_target_pairs={{0,16},{1,9},{2,18},{3,11},{4,20},{5,13},{6,22},{7,15},{8,24},{9,1... | collective-permute-start | bytes 3538952 | tf_op jit(solution)/shard_map/ppermute | solution.py:19
  122.8 55.5 %collective-permute-start.12 = (bf16[8,48,1536]{2,1,0:T(8,128)(2,1)}, bf16[8,48,1536]{2,1,0:T(8,128)(2,1)}, u32[]{:S(2)}, u32[]{:S(2)}) collective-permute-start(bf16[8,48,1536]{2,1,0:T(8,128)(2,1)} %get-tuple-element.175), channel_id=1, source_target_pairs={{0,16},{1,9},{2,18},{3,11},{4,20},{5,13},{6,22},{7,15},{8,24},{9,1... | collective-permute-start | bytes 3538952 | tf_op jit(solution)/shard_map/ppermute | solution.py:19
  124.4 42.2 %all-to-all-start.4 = ((bf16[4,96,768]{2,1,0:T(8,128)(2,1)}), bf16[4,96,768]{2,1,0:T(8,128)(2,1)}, u32[]{:S(2)}, u32[]{:S(2)}) async-start(bf16[4,96,768]{2,1,0:T(8,128)(2,1)} %pad_bitcast_fusion), calls=%async_computation.4 | async-start | bytes 1179648 | tf_op jit(solution)/shard_map/all_to_all | solution.py:337
  166.6 35.4 %all-to-all-start.5 = ((bf16[8,48,768]{2,1,0:T(8,128)(2,1)}), bf16[8,48,768]{2,1,0:T(8,128)(2,1)}, u32[]{:S(2)}, u32[]{:S(2)}) async-start(bf16[8,48,768]{2,1,0:T(8,128)(2,1)} %bitcast.68), calls=%async_computation.5 | async-start | bytes 1179648 | tf_op jit(solution)/shard_map/all_to_all | solution.py:341
  175.3 34.6 %collective-permute-start.27 = (bf16[16,192,384]{2,1,0:T(8,128)(2,1)}, bf16[16,192,384]{2,1,0:T(8,128)(2,1)}, u32[]{:S(2)}, u32[]{:S(2)}) collective-permute-start(bf16[16,192,384]{2,1,0:T(8,128)(2,1)} %constant_dynamic-update-slice_fusion.38.mine), channel_id=1, source_target_pairs={{0,1},{1,0},{2,3},{3,2},{4,5},{5,4},{6,7},{7,6},{8,9},{9,8},{10,11... | collective-permute-start | bytes 7077896 | tf_op jit(solution)/shard_map/ppermute | solution.py:19
  178.2 36.8 %collective-permute-start.20 = (bf16[16,48,1536]{2,1,0:T(8,128)(2,1)}, bf16[16,48,1536]{2,1,0:T(8,128)(2,1)}, u32[]{:S(2)}, u32[]{:S(2)}) collective-permute-start(bf16[16,48,1536]{2,1,0:T(8,128)(2,1)} %constant_dynamic-update-slice_fusion.27.mine), channel_id=1, source_target_pairs={{0,1},{1,0},{2,3},{3,2},{4,5},{5,4},{6,7},{7,6},{8,9},{9,8},{10,11... | collective-permute-start | bytes 7077896 | tf_op jit(solution)/shard_map/ppermute | solution.py:19
  180.7 39.5 %collective-permute-start.13 = (bf16[16,48,1536]{2,1,0:T(8,128)(2,1)}, bf16[16,48,1536]{2,1,0:T(8,128)(2,1)}, u32[]{:S(2)}, u32[]{:S(2)}) collective-permute-start(bf16[16,48,1536]{2,1,0:T(8,128)(2,1)} %constant_dynamic-update-slice_fusion.16.mine), channel_id=1, source_target_pairs={{0,1},{1,0},{2,3},{3,2},{4,5},{5,4},{6,7},{7,6},{8,9},{9,8},{10,11... | collective-permute-start | bytes 7077896 | tf_op jit(solution)/shard_map/ppermute | solution.py:19
  202.0 23.9 %all-to-all-start.1 = ((bf16[8,48,768]{2,1,0:T(8,128)(2,1)}), bf16[8,48,768]{2,1,0:T(8,128)(2,1)S(1)}, u32[]{:S(2)}, u32[]{:S(2)}) async-start(bf16[8,48,768]{2,1,0:T(8,128)(2,1)} %bitcast.45), calls=%async_computation.1 | async-start | bytes 1179648 | tf_op jit(solution)/shard_map/all_to_all | solution.py:341
  313.1 128.3 %collective-permute-start.49 = (bf16[16,192,384]{2,1,0:T(8,128)(2,1)}, bf16[16,192,384]{2,1,0:T(8,128)(2,1)}, u32[]{:S(2)}, u32[]{:S(2)}) collective-permute-start(bf16[16,192,384]{2,1,0:T(8,128)(2,1)} %get-tuple-element.41), channel_id=1, source_target_pairs={{0,1},{1,0},{2,3},{3,2},{4,5},{5,4},{6,7},{7,6},{8,9},{9,8},{10,11... | collective-permute-start | bytes 7077896 | tf_op jit(solution)/shard_map/ppermute | solution.py:19
  313.6 133.7 %collective-permute-start.42 = (bf16[16,48,1536]{2,1,0:T(8,128)(2,1)}, bf16[16,48,1536]{2,1,0:T(8,128)(2,1)}, u32[]{:S(2)}, u32[]{:S(2)}) collective-permute-start(bf16[16,48,1536]{2,1,0:T(8,128)(2,1)} %get-tuple-element.39), channel_id=1, source_target_pairs={{0,1},{1,0},{2,3},{3,2},{4,5},{5,4},{6,7},{7,6},{8,9},{9,8},{10,11... | collective-permute-start | bytes 7077896 | tf_op jit(solution)/shard_map/ppermute | solution.py:19
  318.1 69.1 %all-to-all-start.6 = ((bf16[8,48,768]{2,1,0:T(8,128)(2,1)}), bf16[8,48,768]{2,1,0:T(8,128)(2,1)}, u32[]{:S(2)}, u32[]{:S(2)}) async-start(bf16[8,48,768]{2,1,0:T(8,128)(2,1)} %bitcast.290), calls=%async_computation.6 | async-start | bytes 1179648 | tf_op jit(solution)/shard_map/all_to_all | solution.py:341
  338.8 116.6 %collective-permute-start.35 = (bf16[16,48,1536]{2,1,0:T(8,128)(2,1)}, bf16[16,48,1536]{2,1,0:T(8,128)(2,1)}, u32[]{:S(2)}, u32[]{:S(2)}) collective-permute-start(bf16[16,48,1536]{2,1,0:T(8,128)(2,1)} %get-tuple-element.37), channel_id=1, source_target_pairs={{0,1},{1,0},{2,3},{3,2},{4,5},{5,4},{6,7},{7,6},{8,9},{9,8},{10,11... | collective-permute-start | bytes 7077896 | tf_op jit(solution)/shard_map/ppermute | solution.py:19
  387.2 25.2 %all-to-all-start.2 = ((bf16[8,48,768]{2,1,0:T(8,128)(2,1)}), bf16[8,48,768]{2,1,0:T(8,128)(2,1)}, u32[]{:S(2)}, u32[]{:S(2)}) async-start(bf16[8,48,768]{2,1,0:T(8,128)(2,1)} %bitcast.329), calls=%async_computation.2 | async-start | bytes 1179648 | tf_op jit(solution)/shard_map/all_to_all | solution.py:341
  412.4 38.6 %all-to-all-start.3 = ((bf16[4,96,768]{2,1,0:T(8,128)(2,1)}), bf16[4,96,768]{2,1,0:T(8,128)(2,1)}, u32[]{:S(2)}, u32[]{:S(2)}) async-start(bf16[4,96,768]{2,1,0:T(8,128)(2,1)} %bitcast.65), calls=%async_computation.3 | async-start | bytes 1179648 | tf_op jit(solution)/shard_map/all_to_all | solution.py:337
  445.1 38.3 %collective-permute-start.50 = (bf16[8,192,384]{2,1,0:T(8,128)(2,1)}, bf16[8,192,384]{2,1,0:T(8,128)(2,1)}, u32[]{:S(2)}, u32[]{:S(2)}) collective-permute-start(bf16[8,192,384]{2,1,0:T(8,128)(2,1)} %get-tuple-element.144), channel_id=1, source_target_pairs={{0,16},{1,9},{2,18},{3,11},{4,20},{5,13},{6,22},{7,15},{8,24},{9,1... | collective-permute-start | bytes 3538952 | tf_op jit(solution)/shard_map/ppermute | solution.py:19
  451.0 35.6 %collective-permute-start.43 = (bf16[8,48,1536]{2,1,0:T(8,128)(2,1)}, bf16[8,48,1536]{2,1,0:T(8,128)(2,1)}, u32[]{:S(2)}, u32[]{:S(2)}) collective-permute-start(bf16[8,48,1536]{2,1,0:T(8,128)(2,1)} %get-tuple-element.146), channel_id=1, source_target_pairs={{0,16},{1,9},{2,18},{3,11},{4,20},{5,13},{6,22},{7,15},{8,24},{9,1... | collective-permute-start | bytes 3538952 | tf_op jit(solution)/shard_map/ppermute | solution.py:19
  451.0 29.7 %all-to-all-start.7 = ((bf16[4,96,768]{2,1,0:T(8,128)(2,1)}), bf16[4,96,768]{2,1,0:T(8,128)(2,1)}, u32[]{:S(2)}, u32[]{:S(2)}) async-start(bf16[4,96,768]{2,1,0:T(8,128)(2,1)} %bitcast.307), calls=%async_computation.7 | async-start | bytes 1179648 | tf_op jit(solution)/shard_map/all_to_all | solution.py:337
  459.5 40.1 %collective-permute-start.36 = (bf16[8,48,1536]{2,1,0:T(8,128)(2,1)}, bf16[8,48,1536]{2,1,0:T(8,128)(2,1)}, u32[]{:S(2)}, u32[]{:S(2)}) collective-permute-start(bf16[8,48,1536]{2,1,0:T(8,128)(2,1)} %get-tuple-element.148), channel_id=1, source_target_pairs={{0,16},{1,9},{2,18},{3,11},{4,20},{5,13},{6,22},{7,15},{8,24},{9,1... | collective-permute-start | bytes 3538952 | tf_op jit(solution)/shard_map/ppermute | solution.py:19
  475.2 39.8 %collective-permute-start.28 = (bf16[16,48,2048]{2,1,0:T(8,128)(2,1)}, bf16[16,48,2048]{2,1,0:T(8,128)(2,1)}, u32[]{:S(2)}, u32[]{:S(2)}) collective-permute-start(bf16[16,48,2048]{2,1,0:T(8,128)(2,1)} %get-tuple-element.35), channel_id=1, source_target_pairs={{0,1},{1,0},{2,3},{3,2},{4,5},{5,4},{6,7},{7,6},{8,9},{9,8},{10,11... | collective-permute-start | bytes 9437192 | tf_op jit(solution)/shard_map/ppermute | solution.py:19
  530.7 23.1 %collective-permute-start.29 = (bf16[8,48,2048]{2,1,0:T(8,128)(2,1)S(1)}, bf16[8,48,2048]{2,1,0:T(8,128)(2,1)S(1)}, u32[]{:S(2)}, u32[]{:S(2)}) collective-permute-start(bf16[8,48,2048]{2,1,0:T(8,128)(2,1)S(1)} %get-tuple-element.142), channel_id=1, source_target_pairs={{0,16},{1,9},{2,18},{3,11},{4,20},{5,13},{6,22},{7,15},{8,24},{9,1... | collective-permute-start | bytes 4718600 | tf_op jit(solution)/shard_map/ppermute | solution.py:19
  538.7 41.6 %collective-permute-start.55 = (f32[96,384]{1,0:T(8,128)S(1)}, f32[96,384]{1,0:T(8,128)S(1)}, u32[]{:S(2)}, u32[]{:S(2)}) collective-permute-start(f32[96,384]{1,0:T(8,128)S(1)} %slice_select_fusion.2), channel_id=1, source_target_pairs={{0,1},{1,0},{2,3},{3,2},{4,5},{5,4},{6,7},{7,6},{8,9},{9,8},{10,11... | collective-permute-start | bytes 442376 | tf_op jit(solution)/shard_map/ppermute | solution.py:19
  (134 other events, 1722.6 us)

commit v3 on v1

v3 whole, which is shorter than its diff:
```python
from functools import partial

import jax
import jax.numpy as jnp
from jax import lax
from jax.experimental import pallas as pl
from jax.experimental.pallas import tpu as pltpu
from jax.sharding import PartitionSpec as P

D = 768
HEADS = 12
HEAD = 64
FF = 4 * D
MB = 4
CLIPS = 3
AXES = ("frame", "pos")
TILE = 256
SMALL = 256
f32, bf16 = jnp.float32, jnp.bfloat16
GAIN, SHIFT, BIAS = 4, 7, 10


def send(values, perm):
    return lax.ppermute(values, AXES, perm)


def tie(value, *before):
    return lax.optimization_barrier((value,) + before)[0] if before else value


class Layout:
    def __init__(self):
        self.frames, self.chips = lax.axis_size("frame"), lax.axis_size("pos") // 2
        self.bits = self.frames.bit_length() - 1
        self.frame, self.chip = lax.axis_index("frame"), lax.axis_index("pos") // 2
        self.core = lax.axis_index("pos") % 2
        self.swap = self.perm(lambda f, z, c: (f, z, 1 - c))
        self.along = [self.perm(lambda f, z, c, i=i: (f, z ^ i, c)) for i in range(1, self.chips)]
        self.across = [
            self.perm(lambda f, z, c, k=k: (f ^ (1 << self.bit(k, c)), z, c))
            for k in range(self.bits)
        ]

        share = self.frames // MB
        steps = lambda n: [1 << k for k in range(n.bit_length() - 1)]
        self.within = [self.swap]
        self.within += [self.perm(lambda f, z, c, k=k: (f, z ^ k, c)) for k in steps(self.chips)]
        self.within += [self.perm(lambda f, z, c, k=k: (f ^ k, z, c)) for k in steps(share)]
        self.between = [
            self.perm(lambda f, z, c, k=k * share: (f ^ k, z, c)) for k in steps(MB)
        ]

    def bit(self, step, core):
        return (step + core) % self.bits

    def perm(self, to):
        pairs = []
        for f in range(self.frames):
            for z in range(self.chips):
                for c in range(2):
                    g, y, d = to(f, z, c)
                    pairs.append(
                        ((f * self.chips + z) * 2 + c, (g * self.chips + y) * 2 + d)
                    )
        return pairs

    def table(self):
        rows = []
        for core in (self.core, 1 - self.core):
            blocks = []
            for b in range(self.frames * self.chips):
                flags, i = b // self.chips, b % self.chips
                f = self.frame
                for k in range(self.bits):
                    if flags >> k & 1:
                        f = f ^ (1 << ((k + core) % self.bits))
                blocks.append(f * self.chips + (self.chip ^ i))
            rows.append(jnp.stack(blocks))
        return jnp.concatenate([jnp.stack(rows).reshape(-1), self.core[None]]).astype(jnp.int32)

    def pick(self, low, high):
        return jnp.where(self.core == 0, low, high), jnp.where(self.core == 0, high, low)

    def halves(self, mats):
        low = jnp.concatenate([m[:, : m.shape[1] // 2] for m in mats], axis=1)
        high = jnp.concatenate([m[:, m.shape[1] // 2 :] for m in mats], axis=1)
        return self.pick(low, high)

    def chip_rows(self, keep, got):
        return jnp.concatenate(self.pick(keep, got), axis=0)

    def split(self, low, high, widths):
        mats, at = [], 0
        for width in widths:
            half = width // 2
            mats.append(jnp.concatenate([low[:, at : at + half], high[:, at : at + half]], axis=1))
            at += half
        return mats


class Way:
    def __init__(self, layout, *state):
        self.layout, self.state = layout, state


def meet(*things):
    values = tuple(t.state if isinstance(t, Way) else t for t in things)
    values = lax.optimization_barrier(values)
    out = []
    for thing, value in zip(things, values):
        if isinstance(thing, Way):
            thing.state = value
        else:
            out.append(value)
    return out[0] if len(out) == 1 else out


class Gather(Way):
    def along(self):
        (block,) = self.state
        self.state = (block,) + tuple(send(block, p) for p in self.layout.along)

    def across(self, step):
        if step == 0:
            self.state = (jnp.stack(self.state),)
        self.state += tuple(send(piece, self.layout.across[step]) for piece in self.state)

    def swap(self):
        self.state = (self.state, tuple(send(piece, self.layout.swap) for piece in self.state))


class Scatter(Way):
    def __init__(self, layout, mine, other):
        near = [mine[0]], [send(other[0], layout.swap)]
        far = [mine[1]], [send(other[1], layout.swap)]
        super().__init__(layout, tuple(near[0] + near[1]), tuple(far[0] + far[1]))

    def across(self, step):
        near, far = self.state
        if far is None:
            half = near[0].shape[0] // 2
            near, far = tuple(a[:half] for a in near), tuple(a[half:] for a in near)
        far = total(far).astype(bf16)
        self.state = (near + (send(far, self.layout.across[step]),), None)
        return far

    def along(self):
        near, _ = self.state
        parts = total(near)
        away = parts.astype(bf16)
        self.state = (parts[0],) + tuple(
            send(away[i + 1], p) for i, p in enumerate(self.layout.along)
        )

    def swap(self):
        sums = total(self.state)
        rows = sums.shape[0] // 2
        keep, give = self.layout.pick(sums[:rows], sums[rows:])
        self.state = (keep, send(give, self.layout.swap))

    def finish(self, widths):
        return self.layout.split(*self.layout.pick(*self.state), widths)


def total(values):
    out = values[0].astype(f32)
    for value in values[1:]:
        out = out + value.astype(f32)
    return out


class Chunk:
    def __init__(self, layout, widths, rows):
        self.layout, self.widths, self.rows = layout, widths, rows
        self.count = layout.frames * layout.chips
        self.table = layout.table()
        self.half = sum(widths) // 2
        self.whole = bool(rows % 16)
        if self.whole:
            core = layout.core.astype(jnp.int32)
            self.index = jnp.stack([jnp.zeros_like(core)] * 2 + [core])
            self.blocks, self.block_rows = 1, self.count * rows
        else:
            self.index = self.table
            self.blocks, self.block_rows = self.count, rows

    def load(self, way):
        mine, other = way.state
        if self.whole:
            order = jnp.argsort(self.table[: 2 * self.count].reshape(2, -1), axis=1)
            mine, other = [
                (jnp.concatenate(a)[o].reshape(1, self.block_rows, -1),)
                for a, o in zip((mine, other), order)
            ]
        self.mine, self.other = mine, other
        return self

    def operands(self):
        pieces = [[(a, "h") for a in side] for side in (self.mine, self.other)]
        return [[(self.index, "s")] + pieces]

    def grads(self):
        if self.whole:
            piece = [((1, self.block_rows, self.half), bf16, "h")]
        else:
            piece = [((self.count // 2, self.block_rows, self.half), bf16, "h")] * 2
        return [[piece, piece]]

    def at(self, which):
        return sum(self.widths[:which]) // 2

    def fetch(self, which, weights, dst, sem):
        self._copies(which, *weights, dst, sem, True)

    def store(self, which, table, src, grads, sem):
        self._copies(which, table, *grads, src, sem, False)

    def _copies(self, which, table, mine, other, mat, sem, into):
        at, w = self.at(which), self.widths[which] // 2
        core = table[2 * self.blocks]
        for side, pieces in ((0, mine), (1, other)):
            half = core if side == 0 else 1 - core
            first = side * self.blocks
            for piece in pieces:

                def body(b, carry, piece=piece, first=first, half=half):
                    row = pl.multiple_of(table[first + b] * self.block_rows, 16)
                    block = piece.at[b, :, at : at + w]
                    place = mat.at[
                        pl.ds(row, self.block_rows), pl.ds(pl.multiple_of(half * w, 128), w)
                    ]
                    pair = (block, place) if into else (place, block)
                    pltpu.make_async_copy(*pair, sem).start()
                    return carry

                lax.fori_loop(0, piece.shape[0], body, 0)
                first += piece.shape[0]

    def scatter(self, mine, other):
        if self.whole:
            order = self.table[: 2 * self.count].reshape(2, -1)
            mine, other = [
                a[0].reshape(self.count, self.rows, -1)[o] for a, o in zip((mine, other), order)
            ]
            half = self.count // 2
            mine, other = [(a[:half], a[half:]) for a in (mine, other)]
        return Scatter(self.layout, mine, other)


def arrived(mat, sem):
    pltpu.make_async_copy(mat, mat, sem).wait()


SPACE = {"s": pltpu.SMEM, "v": pltpu.VMEM, "h": pltpu.HBM}


def flat(items):
    return [leaf for item in items for leaf in (flat(item) if isinstance(item, list) else [item])]


def nest(items, leaves):
    return [nest(item, leaves) if isinstance(item, list) else next(leaves) for item in items]


def call(name, body, ins, outs, scratch, sems, flops, alias=None):
    operands, results = flat(ins), flat(outs)
    bytes_of = lambda shape, kind: jnp.dtype(kind).itemsize * _size(shape)
    size = sum(bytes_of(a.shape, a.dtype) for a, space in operands if space == "v")
    size += sum(bytes_of(shape, kind) for shape, kind, space in results if space == "v")
    size += sum(bytes_of(shape, kind) for shape, kind in scratch)
    moved = sum(bytes_of(a.shape, a.dtype) for a, _ in operands)
    moved += sum(bytes_of(shape, kind) for shape, kind, _ in results)
    aliases = {}
    for i, o in (alias or {}).items():
        start, end = len(flat(ins[:i])), len(flat(outs[:o]))
        for k in range(len(flat([ins[i]]))):
            aliases[start + k] = end + k

    def kernel(*refs):
        leaves = iter(refs)
        body(*nest(ins, leaves), *nest(outs, leaves), *leaves)

    values = pl.pallas_call(
        kernel,
        out_shape=[jax.ShapeDtypeStruct(shape, kind) for shape, kind, _ in results],
        in_specs=[pl.BlockSpec(memory_space=SPACE[space]) for _, space in operands],
        out_specs=[pl.BlockSpec(memory_space=SPACE[space]) for _, _, space in results],
        scratch_shapes=[pltpu.VMEM(shape, kind) for shape, kind in scratch]
        + [pltpu.SemaphoreType.DMA((sems,))],
        input_output_aliases=aliases,
        compiler_params=pltpu.CompilerParams(
            vmem_limit_bytes=min(int(size * 1.1) + (12 << 20), 60 << 20)
        ),
        cost_estimate=pl.CostEstimate(flops=flops, bytes_accessed=moved, transcendentals=0),
        name=name,
    )(*[a for a, _ in operands])
    return nest(outs, iter(values))


def _size(shape):
    total = 1
    for n in shape:
        total *= n
    return total


def tiles(width, body, size=TILE):
    def step(j, carry):
        body(pl.ds(pl.multiple_of(j * size, size), size))
        return carry

    lax.fori_loop(0, width // size, step, 0)


def dot(a, b):
    return jnp.dot(a, b, preferred_element_type=f32)


def dot_t(a, b):
    return lax.dot_general(a, b, (((1,), (1,)), ((), ())), preferred_element_type=f32)


def normalise(values):
    centred = values - jnp.mean(values, axis=-1, keepdims=True)
    inv_std = lax.rsqrt(jnp.mean(centred * centred, axis=-1, keepdims=True) + 1e-06)
    return centred * inv_std, inv_std


def norm_rows(values, small, which):
    normal, _ = normalise(values)
    return normal * small[GAIN + which : GAIN + which + 1] + small[SHIFT + which : SHIFT + which + 1]


def norm_back(values, upstream, small, which):
    normal, inv_std = normalise(values)
    product = upstream * normal
    grad_gain = jnp.sum(product, axis=0, keepdims=True)
    grad_shift = jnp.sum(upstream, axis=0, keepdims=True)
    gain = small[GAIN + which : GAIN + which + 1]
    scaled = upstream * gain
    mean = jnp.mean(scaled, axis=-1, keepdims=True)
    mean_normal = jnp.mean(product * gain, axis=-1, keepdims=True)
    return inv_std * (scaled - mean - normal * mean_normal), grad_gain, grad_shift


def column_sum(values):
    return jnp.sum(values.astype(f32), axis=0, keepdims=True)


def set_mask(mask, key_ids, query_ids):
    mask[...] = jnp.where(key_ids[...] == query_ids[...], 0.0, -1000000000.0)


def head_lanes(h, value):
    lane = lax.broadcasted_iota(jnp.int32, (1, 2 * HEAD), 1)
    return jnp.where(lane // HEAD == h, value, 0.0)


def only(values, lanes):
    return (values.astype(f32) * lanes).astype(bf16)


def attend(query, q_at, pairs, k_at, v_at, mask, mixed, lse):
    def pair(i, carry):
        cols = lambda at: pl.ds(pl.multiple_of(at + i * 2 * HEAD, 2 * HEAD), 2 * HEAD)
        queries, keys = query[:, cols(q_at)], pairs[:, cols(k_at)]
        values = pairs[:, cols(v_at)].astype(f32).T.astype(bf16)
        outs = []
        for h in range(2):
            score = dot_t(keys, only(queries, head_lanes(h, 0.125))) + mask[...]
            top = jnp.max(score, axis=0, keepdims=True)
            weight = jnp.exp(score - top)
            total = jnp.sum(weight, axis=0, keepdims=True)
            lse[pl.ds(2 * i + h, 1), :] = top + jnp.log(total)
            probs = (weight * (1.0 / total)).astype(bf16)
            outs.append(dot(values[h * HEAD : (h + 1) * HEAD], probs))
        mixed[:, cols(0)] = jnp.concatenate(outs, axis=0).T.astype(bf16)
        return carry

    lax.fori_loop(0, HEADS // 2, pair, 0)


def attend_back(query, q_at, pairs, k_at, v_at, mask, lse, grad, out_q, out_pairs, gk_at, gv_at):
    def pair(i, carry):
        cols = lambda at: pl.ds(pl.multiple_of(at + i * 2 * HEAD, 2 * HEAD), 2 * HEAD)
        queries, keys, values = query[:, cols(q_at)], pairs[:, cols(k_at)], pairs[:, cols(v_at)]
        upstream = grad[:, cols(0)]
        keys_across = keys.astype(f32).T.astype(bf16)
        grad_keys = grad_values = 0.0
        outs = []
        for h in range(2):
            queries_h = only(queries, head_lanes(h, 0.125))
            upstream_h = only(upstream, head_lanes(h, 1.0))
            score = dot_t(keys, queries_h) + mask[...]
            probs = jnp.exp(score - lse[pl.ds(2 * i + h, 1), :])
            dprob = dot_t(values, upstream_h)
            delta = jnp.sum(probs * dprob, axis=0, keepdims=True)
            dscore = (probs * (dprob - delta)).astype(bf16)
            grad_keys += dot(dscore, queries_h)
            grad_values += dot(probs.astype(bf16), upstream_h)
            outs.append(dot(keys_across[h * HEAD : (h + 1) * HEAD], dscore))
        out_q[:, cols(0)] = (jnp.concatenate(outs, axis=0).T * 0.125).astype(bf16)
        out_pairs[:, cols(gk_at)] = grad_keys.astype(bf16)
        out_pairs[:, cols(gv_at)] = grad_values.astype(bf16)
        return carry

    lax.fori_loop(0, HEADS // 2, pair, 0)


def qkv_tiles(x, w, bias, small, which, packed):
    bias[:, :D] = small[BIAS + which : BIAS + which + 1]
    bias[:, D : 2 * D] = jnp.zeros((1, D), f32)
    bias[:, 2 * D :] = small[BIAS + which + 1 : BIAS + which + 2]

    def tile(cols):
        packed[:, cols] = (dot(x[...], w[:, cols]) + bias[:, cols]).astype(bf16)

    tiles(3 * D, tile)


def across(mat, out):
    for at in range(0, mat.shape[1], 128):
        out[at : at + 128, :] = mat[:, at : at + 128].astype(f32).T.astype(bf16)


def temporal_qkv_kernel(chunk, weights, rows, packed, small, w, raw, x, bias, sem):
    chunk.fetch(3, weights, raw, sem.at[0])
    chunk.fetch(0, weights, w, sem.at[1])
    arrived(raw, sem.at[0])
    small[...] = raw[:, :128].astype(f32).T[: small.shape[0]]
    x[...] = norm_rows(rows[...].astype(f32), small, 0).astype(bf16)
    arrived(w, sem.at[1])
    qkv_tiles(x, w, bias, small, 0, packed)


def temporal_mix_kernel(
    chunk, weights, packed, rows, key_ids, query_ids, small,
    mixed, projected, lse, temporal, w_proj, w_fc, mask, sem,
):
    chunk.fetch(1, weights, w_proj, sem.at[0])
    chunk.fetch(2, weights, w_fc, sem.at[1])
    set_mask(mask, key_ids, query_ids)
    attend(packed, 0, packed, D, 2 * D, mask, mixed, lse)
    arrived(w_proj, sem.at[0])

    def project(cols):
        bias = small[BIAS + 2 : BIAS + 3, cols]
        projected[:, cols] = (dot(mixed[...], w_proj[:, cols]) + bias).astype(bf16)

    tiles(D, project)
    arrived(w_fc, sem.at[1])

    def residual(cols):
        added = dot(projected[...], w_fc[:, cols]) + small[BIAS + 3 : BIAS + 4, cols]
        temporal[:, cols] = (rows[:, cols].astype(f32) + added).astype(bf16)

    tiles(D, residual)


def spatial_qkv_kernel(
    chunk, weights, rows, choose, class_rows, is_class, small,
    temporal, packed, w, x, bias, sem,
):
    chunk.fetch(0, weights, w, sem.at[0])
    values = jnp.where(
        is_class[...] > 0, dot(choose[...], class_rows[...]), rows[...].astype(f32)
    )
    temporal[...] = values.astype(bf16)
    x[...] = norm_rows(values, small, 1).astype(bf16)
    arrived(w, sem.at[0])
    qkv_tiles(x, w, bias, small, 4, packed)


def spatial_mix_kernel(
    chunk, k_at, weights, packed, pairs, key_ids, query_ids, temporal, small,
    mixed, lse, spatial, w, mask, sem,
):
    chunk.fetch(1, weights, w, sem.at[0])
    set_mask(mask, key_ids, query_ids)
    attend(packed, 0, pairs, k_at, k_at + D, mask, mixed, lse)
    arrived(w, sem.at[0])

    def residual(cols):
        added = dot(mixed[...], w[:, cols]) + small[BIAS + 6 : BIAS + 7, cols]
        spatial[:, cols] = temporal[:, cols].astype(f32) + added

    tiles(D, residual)


def hidden_kernel(
    chunk, weights, spatial, in_bias, small, normed, activated, slope, w, sem
):
    chunk.fetch(0, weights, w, sem.at[0])
    normed[...] = norm_rows(spatial[...], small, 2).astype(bf16)
    arrived(w, sem.at[0])

    def tile(cols):
        hidden = dot(normed[...], w[:, cols]) + in_bias[:, cols]
        below = 0.5 + 0.5 * lax.erf(hidden * 0.7071067811865476)
        density = jnp.exp(hidden * hidden * -0.5) * 0.3989422804014327
        activated[:, cols] = (hidden * below).astype(bf16)
        slope[:, cols] = (below + hidden * density).astype(bf16)

    tiles(FF, tile)


def out_grad_kernel(chunk, table, activated, grad_out, grads, grad, sem):
    def tile(cols):
        grad[cols, :] = dot(activated[:, cols].astype(f32).T.astype(bf16), grad_out[...]).astype(bf16)

    tiles(FF, tile)
    chunk.store(0, table, grad, grads, sem.at[0])
    arrived(grad, sem.at[0])


def mlp_back_kernel(
    chunk_in, chunk_out, weights_in, weights_out,
    grad_out, slope, spatial, small, grad_hidden, in_bias, grad_spatial, sums,
    w_in, w_out, total, sem,
):
    chunk_out.fetch(0, weights_out, w_out, sem.at[0])
    chunk_in.fetch(0, weights_in, w_in, sem.at[1])
    total[...] = jnp.zeros_like(total)
    arrived(w_out, sem.at[0])
    arrived(w_in, sem.at[1])

    def tile(cols):
        grad = (dot_t(grad_out[...], w_out[cols, :]) * slope[:, cols].astype(f32)).astype(bf16)
        grad_hidden[:, cols] = grad
        in_bias[:, cols] = column_sum(grad)
        total[...] += dot_t(grad, w_in[:, cols])

    tiles(FF, tile)
    back, gain, shift = norm_back(spatial[...], total[...], small, 2)
    upstream = grad_out[...].astype(f32)
    result = upstream + back
    grad_spatial[...] = result
    sums[0:1] = gain
    sums[1:2] = shift
    sums[2:3] = column_sum(upstream)
    sums[3:4] = column_sum(result.astype(bf16))
    sums[4:8] = jnp.zeros((4, D), f32)


def in_grad_kernel(chunk, table, normed, grad_hidden, grads, normed_t, grad, sem):
    across(normed, normed_t)

    def tile(cols):
        grad[:, cols] = dot(normed_t[...], grad_hidden[:, cols]).astype(bf16)

    tiles(FF, tile)
    chunk.store(0, table, grad, grads, sem.at[0])
    arrived(grad, sem.at[0])


def block_out_kernel(
    chunk, weights, activated, spatial, small, result, w, total, sem
):
    chunk.fetch(0, weights, w, sem.at[0])
    total[...] = spatial[...] + small[BIAS + 7 : BIAS + 8]
    arrived(w, sem.at[0])

    def tile(cols):
        total[...] += dot(activated[:, cols], w[cols, :])

    tiles(FF, tile)
    result[...] = total[...].astype(bf16)


def spatial_attention_back_kernel(
    chunk, k_at, weights, grad_spatial, mixed, packed, pairs, key_ids, query_ids, lse,
    grads, grad_query, grad_pairs,
    w, upstream, mixed_t, grad, grad_mixed, mask, sem,
):
    chunk.fetch(1, weights, w, sem.at[0])
    upstream[...] = grad_spatial[...].astype(bf16)
    set_mask(mask, key_ids, query_ids)
    arrived(w, sem.at[0])

    def back(cols):
        grad_mixed[:, cols] = dot_t(upstream[...], w[cols, :]).astype(bf16)

    tiles(D, back)
    across(mixed, mixed_t)

    def tile(cols):
        grad[:, cols] = dot(mixed_t[...], upstream[:, cols]).astype(bf16)

    tiles(D, tile)
    chunk.store(1, weights[0], grad, grads, sem.at[1])
    attend_back(
        packed, 0, pairs, k_at, k_at + D, mask, lse, grad_mixed, grad_query, grad_pairs, 0, D
    )
    arrived(grad, sem.at[1])


def qkv_back(normed_t, grad_packed, w, grad, total):
    total[...] = jnp.zeros_like(total)

    def tile(cols):
        grad[:, cols] = dot(normed_t[...], grad_packed[:, cols]).astype(bf16)
        total[...] += dot_t(grad_packed[:, cols], w[:, cols])

    tiles(3 * D, tile)


def spatial_qkv_back_kernel(
    chunk, weights, grad_query, grad_pairs, temporal, grad_spatial, choose, is_class,
    small, old, grads, grad_temporal, class_part, sums,
    w, packed, normed, normed_t, grad, total, sem,
):
    chunk.fetch(0, weights, w, sem.at[0])
    packed[:, :D] = grad_query[...]
    packed[:, D:] = grad_pairs[...]
    values = temporal[...].astype(f32)
    normed[...] = norm_rows(values, small, 1).astype(bf16)
    across(normed, normed_t)
    arrived(w, sem.at[0])
    qkv_back(normed_t, packed, w, grad, total)
    chunk.store(0, weights[0], grad, grads, sem.at[1])
    back, gain, shift = norm_back(values, total[...], small, 1)
    result = grad_spatial[...] + back
    grad_temporal[...] = jnp.where(is_class[...] > 0, 0.0, result).astype(bf16)
    class_part[...] = jnp.zeros_like(class_part)
    for c in range(CLIPS):
        class_part[c : c + 1] = column_sum(back * choose[:, c : c + 1].astype(f32))
    sums[0:1] = gain
    sums[1:2] = shift
    sums[2:3] = column_sum(packed[:, :D])
    sums[3:4] = column_sum(packed[:, 2 * D :])
    sums[4:8] = jnp.zeros((4, D), f32)
    arrived(grad, sem.at[1])


def temporal_proj_back_kernel(
    chunk, chunk_back, weights, grad_temporal, projected, mixed,
    grads, grad_mixed, sums,
    w_proj, w_fc, grad_proj, proj_t, mixed_t, acc_proj, acc_fc, sem,
):
    chunk.fetch(2, weights, w_fc, sem.at[0])
    chunk.fetch(1, weights, w_proj, sem.at[1])
    across(projected, proj_t)

    def fc_tile(cols):
        acc_fc[:, cols] = dot(proj_t[...], grad_temporal[:, cols]).astype(bf16)

    tiles(D, fc_tile)
    chunk_back.store(1, weights[0], acc_fc, grads, sem.at[2])
    arrived(w_fc, sem.at[0])

    def fc_back(cols):
        grad_proj[:, cols] = dot_t(grad_temporal[...], w_fc[cols, :]).astype(bf16)

    tiles(D, fc_back)
    across(mixed, mixed_t)

    def proj_tile(cols):
        acc_proj[:, cols] = dot(mixed_t[...], grad_proj[:, cols]).astype(bf16)

    tiles(D, proj_tile)
    chunk_back.store(0, weights[0], acc_proj, grads, sem.at[3])
    arrived(w_proj, sem.at[1])

    def proj_back(cols):
        grad_mixed[:, cols] = dot_t(grad_proj[...], w_proj[cols, :]).astype(bf16)

    tiles(D, proj_back)
    sums[0:1] = column_sum(grad_temporal[...])
    sums[1:2] = column_sum(grad_proj[...])
    sums[2:8] = jnp.zeros((6, D), f32)
    arrived(acc_fc, sem.at[2])
    arrived(acc_proj, sem.at[3])


def temporal_attention_back_kernel(
    chunk, chunk_back, weights, packed, key_ids, query_ids, lse, grad_mixed, rows, grad_temporal,
    small, in_bias, sums_m, sums_s, sums_t,
    grads, tokens_grad,
    w, mask, grad_packed, normed, normed_t, grad, total, rows_small, raw, sem,
):
    chunk.fetch(0, weights, w, sem.at[0])
    set_mask(mask, key_ids, query_ids)
    attend_back(
        packed, 0, packed, D, 2 * D, mask, lse, grad_mixed, grad_packed, grad_packed, D, 2 * D
    )
    values = rows[...].astype(f32)
    normed[...] = norm_rows(values, small, 0).astype(bf16)
    across(normed, normed_t)
    arrived(w, sem.at[0])
    qkv_back(normed_t, grad_packed, w, grad, total)
    chunk_back.store(0, weights[0], grad, grads, sem.at[1])
    back, gain, shift = norm_back(values, total[...], small, 0)
    tokens_grad[...] = (grad_temporal[...].astype(f32) + back).astype(bf16)
    rows_small[...] = jnp.zeros_like(rows_small)
    rows_small[0:4] = in_bias[...]
    for i, (gain_row, shift_row) in enumerate(
        ((gain, shift), (sums_s[0:1], sums_s[1:2]), (sums_m[0:1], sums_m[1:2]))
    ):
        rows_small[GAIN + i : GAIN + i + 1] = gain_row
        rows_small[SHIFT + i : SHIFT + i + 1] = shift_row
    for i, row in enumerate(
        (
            column_sum(grad_packed[:, :D]),
            column_sum(grad_packed[:, 2 * D :]),
            sums_t[1:2],
            sums_t[0:1],
            sums_s[2:3],
            sums_s[3:4],
            sums_m[3:4],
            sums_m[2:3],
        )
    ):
        rows_small[BIAS + i : BIAS + i + 1] = row
    raw[:, :128] = rows_small[...].T.astype(bf16)
    raw[:, 128:] = jnp.zeros((D, 128), bf16)
    chunk_back.store(1, weights[0], raw, grads, sem.at[2])
    arrived(grad, sem.at[1])
    arrived(raw, sem.at[2])


def on_device(
    tokens,
    class_tokens,
    clip_frames,
    cotangent,
    temporal_qkv,
    temporal_proj,
    temporal_fc,
    spatial_qkv,
    spatial_proj,
    mlp_in,
    mlp_out,
    mlp_in_bias,
    norm_gains,
    norm_shifts,
    biases,
):
    frame_size, pos_size = lax.axis_size("frame"), lax.axis_size("pos")
    frame_index, pos_index = lax.axis_index("frame"), lax.axis_index("pos")
    frame_count, pos_count = tokens.shape[1], tokens.shape[2]
    shard = norm_gains.shape[0]
    slots = pos_count + 1
    share = frame_size // MB
    my_slots = slots // share
    all_frames = frame_count * frame_size
    my_frames = all_frames // pos_size
    rows_count = all_frames * my_slots
    micro = frame_index // share

    layout = Layout()
    small = jnp.concatenate(
        [mlp_in_bias.reshape(shard, 4), norm_gains, norm_shifts, biases], axis=1
    )
    small = jnp.pad(small, ((0, 0), (0, SMALL - small.shape[1])))
    keep_t, give_t = layout.halves((temporal_qkv, temporal_proj, temporal_fc, small))
    keep_s, give_s = layout.halves((spatial_qkv, spatial_proj))
    keep_in, give_in = layout.halves((mlp_in,))
    keep_out, give_out = layout.halves((mlp_out,))
    got_t = send(give_t, layout.swap)
    got = send(tie(jnp.concatenate([give_s, give_in], axis=1), give_t), layout.swap)
    got_out = send(tie(give_out, give_t), layout.swap)
    cut = keep_s.shape[1]
    way_t = Gather(layout, layout.chip_rows(keep_t, got_t))
    way_s = Gather(layout, layout.chip_rows(keep_s, got[:, :cut]))
    way_in = Gather(layout, layout.chip_rows(keep_in, got[:, cut:]))
    way_out = Gather(layout, layout.chip_rows(keep_out, got_out))
    chunk_t = Chunk(layout, (3 * D, D, D, SMALL), 2 * shard)
    chunk_s = Chunk(layout, (3 * D, D), 2 * shard)
    chunk_in = Chunk(layout, (FF,), 2 * shard)
    chunk_out = Chunk(layout, (D,), 8 * shard)
    chunk_proj = Chunk(layout, (D, D), 2 * shard)
    chunk_qkv = Chunk(layout, (3 * D, SMALL), 2 * shard)
    later = range(1, layout.bits)

    def frame_hop(values):
        return lax.all_to_all(values, "frame", 0, 0, tiled=True)

    def pos_hop(values):
        parts = values.reshape(pos_size, rows_count // pos_size, D)
        return lax.all_to_all(parts, "pos", 0, 0, tiled=True).reshape(rows_count, D)

    def to_temporal(values):
        padded = jnp.pad(values, ((0, 0), (0, 0), (0, 1), (0, 0)))
        padded = padded.reshape(MB, frame_count, share, my_slots, D).transpose(0, 2, 1, 3, 4)
        return frame_hop(padded.reshape(frame_size, frame_count * my_slots, D)).reshape(
            rows_count, D
        )

    def from_temporal(values):
        parts = frame_hop(values.reshape(frame_size, frame_count * my_slots, D))
        parts = parts.reshape(MB, share, frame_count, my_slots, D).transpose(0, 2, 1, 3, 4)
        return parts.reshape(MB, frame_count, slots, D)[:, :, :pos_count]

    def partners(values, step):
        perm = [(f, f // share * share + (f % share + step) % share) for f in range(frame_size)]
        return lax.ppermute(values, "frame", perm)

    row_ids = jnp.arange(rows_count, dtype=jnp.int32)
    row_slot = row_ids % my_slots
    clip_ends = jnp.cumsum(lax.dynamic_index_in_dim(clip_frames, micro, 0, keepdims=False))
    clip_of = lambda frame: jnp.sum(
        (frame[:, None] >= clip_ends[None, :]).astype(jnp.int32), axis=1
    )
    group_t = row_slot * CLIPS + clip_of(row_ids // my_slots)
    ids_t = [(group_t[:, None], "v"), (group_t[None, :], "v")]
    frame_s = row_ids // my_slots % my_frames
    clip_s = clip_of(pos_index * my_frames + frame_s)
    first_source = row_ids < my_frames * my_slots

    def key_masks(share_index):
        padding = row_slot + share_index * my_slots == slots - 1
        is_class = padding & first_source
        return is_class, is_class | ~padding

    keys_s = []
    for step in range(share):
        _, valid = key_masks((frame_index + share - step) % share)
        keys_s.append(jnp.where(valid, frame_s, -1))
    ids_s = [(jnp.concatenate(keys_s)[:, None], "v"), (frame_s[None, :], "v")]
    is_class, _ = key_masks(frame_index % share)
    choose = (clip_s[:, None] == jnp.arange(8)[None, :]) & is_class[:, None]
    choose = (choose.astype(bf16), "v")
    class_rows = lax.dynamic_index_in_dim(class_tokens, micro, 0, keepdims=False)
    class_rows = (jnp.pad(class_rows, ((0, 8 - CLIPS), (0, 0))), "v")
    is_class = (is_class.astype(jnp.int32)[:, None], "v")

    n = rows_count
    narrow, wide, full = (n, D), (n, 3 * D), (n, FF)
    heads = (16, n)
    flops = lambda columns: 2 * n * D * columns

    way_t.along()
    rows = to_temporal(tokens)
    rows = meet(way_t, way_s, way_in, way_out, rows)
    way_t.across(0)
    way_s.along()
    meet(way_t, way_s)
    for step in later:
        way_t.across(step)
    way_in.state = (tie(way_in.state[0], way_s.state[1]),)
    way_in.along()
    meet(way_t, way_in)
    way_t.swap()
    way_s.across(0)
    cotangent = meet(way_t, way_s, cotangent)
    for step in later:
        way_s.across(step)
    way_out.state = (tie(way_out.state[0], way_in.state[1]),)
    way_out.along()
    packed_t, small_t = call(
        "temporal_qkv",
        partial(temporal_qkv_kernel, chunk_t),
        chunk_t.load(way_t).operands() + [(rows, "v")],
        [(wide, bf16, "v"), ((32, D), f32, "v")],
        [((D, 3 * D), bf16), ((D, SMALL), bf16), (narrow, bf16), ((1, 3 * D), f32)],
        2,
        flops(3 * D),
    )
    small = (small_t, "v")
    grad_out = to_temporal(cotangent)
    mixed_t, projected, lse_t, temporal = call(
        "temporal_mix",
        partial(temporal_mix_kernel, chunk_t),
        chunk_t.operands() + [(packed_t, "v"), (rows, "v")] + ids_t + [small],
        [(narrow, bf16, "v"), (narrow, bf16, "v"), (heads, f32, "v"), (narrow, bf16, "v")],
        [((D, D), bf16), ((D, D), bf16), ((n, n), f32)],
        2,
        flops(2 * D + 4 * n),
    )
    temporal = meet(way_s, way_out, temporal)
    temporal = pos_hop(temporal)
    way_s.swap()
    way_in.across(0)
    temporal, grad_out = meet(way_s, way_in, temporal, grad_out)
    for step in later:
        way_in.across(step)
    grad_out = pos_hop(grad_out)
    temporal, packed_s = call(
        "spatial_qkv",
        partial(spatial_qkv_kernel, chunk_s),
        chunk_s.load(way_s).operands() + [(temporal, "v"), choose, class_rows, is_class, small],
        [(narrow, bf16, "v"), (wide, bf16, "v")],
        [((D, 3 * D), bf16), (narrow, bf16), ((1, 3 * D), f32)],
        1,
        flops(3 * D),
    )
    temporal = (temporal, "v")
    pairs, k_at = packed_s, D
    if share > 1:
        pairs = [packed_s[:, D:]]
        for step in range(1, share):
            pairs.append(partners(packed_s[:, D:], step))
        pairs, k_at = jnp.concatenate(pairs, axis=0), 0
    all_keys = share * n
    mixed_s, lse_s, spatial = call(
        "spatial_mix",
        partial(spatial_mix_kernel, chunk_s, k_at),
        chunk_s.operands() + [(packed_s, "v"), (pairs, "v")] + ids_s + [temporal, small],
        [(narrow, bf16, "v"), (heads, f32, "v"), (narrow, f32, "v")],
        [((D, D), bf16), ((all_keys, n), f32)],
        1,
        flops(D + 4 * all_keys),
    )
    spatial, grad_out = meet(way_in, spatial, grad_out)
    spatial, grad_out = (spatial, "v"), (grad_out, "v")
    way_in.swap()
    way_out.across(0)
    meet(way_in, way_out)
    for step in later:
        way_out.across(step)
    in_bias = (small_t[:4].T.reshape(1, FF), "v")
    normed_m, activated, slope = call(
        "hidden",
        partial(hidden_kernel, chunk_in),
        chunk_in.load(way_in).operands() + [spatial, in_bias, small],
        [(narrow, bf16, "v"), (full, bf16, "v"), (full, bf16, "v")],
        [((D, FF), bf16)],
        1,
        flops(FF),
    )
    activated = (activated, "v")
    (acc_out,) = call(
        "mlp_out_grad",
        partial(out_grad_kernel, chunk_out),
        [(chunk_out.index, "s"), activated, grad_out],
        chunk_out.grads(),
        [((FF, D), bf16)],
        1,
        flops(FF),
    )
    acc_out, slope = meet(way_out, acc_out, slope)
    way_out.swap()
    back_out = chunk_out.scatter(*acc_out)
    slope = meet(way_out, back_out, slope)
    for step in reversed(later):
        back_out.across(step)
    grad_hidden, grad_in_bias, grad_spatial, sums_m = call(
        "mlp_back",
        partial(mlp_back_kernel, chunk_in, chunk_out),
        chunk_in.operands()
        + chunk_out.load(way_out).operands()
        + [grad_out, (slope, "v"), spatial, small],
        [(full, bf16, "v"), ((1, FF), f32, "v"), (narrow, f32, "v"), ((8, D), f32, "v")],
        [((D, FF), bf16), ((FF, D), bf16), (narrow, f32)],
        2,
        flops(2 * FF),
    )
    grad_hidden = meet(back_out, grad_hidden)
    back_out.across(0)
    (acc_in,) = call(
        "mlp_in_grad",
        partial(in_grad_kernel, chunk_in),
        [(chunk_in.index, "s"), (normed_m, "v"), (grad_hidden, "v")],
        chunk_in.grads(),
        [((D, n), bf16), ((D, FF), bf16)],
        1,
        flops(FF),
    )
    acc_in, grad_spatial = meet(back_out, acc_in, grad_spatial)
    back_in = chunk_in.scatter(*acc_in)
    grad_spatial = meet(back_in, grad_spatial)
    for step in reversed(later):
        back_in.across(step)
    back_out.along()
    grad_spatial = (grad_spatial, "v")
    acc_s, grad_query, grad_pairs = call(
        "spatial_attention_back",
        partial(spatial_attention_back_kernel, chunk_s, k_at),
        chunk_s.operands()
        + [grad_spatial, (mixed_s, "v"), (packed_s, "v"), (pairs, "v")]
        + ids_s
        + [(lse_s, "v")],
        chunk_s.grads() + [(narrow, bf16, "v"), ((all_keys, 2 * D), bf16, "v")],
        [((D, D), bf16), (narrow, bf16), ((D, n), bf16), ((D, D), bf16), (narrow, bf16)]
        + [((all_keys, n), f32)],
        2,
        flops(2 * D + 10 * all_keys),
    )
    grad_query, grad_pairs = meet(back_in, back_out, grad_query, grad_pairs)
    back_in.across(0)
    back_out.swap()
    own_pairs = grad_pairs[:n]
    for step in range(1, share):
        theirs = partners(grad_pairs[step * n : (step + 1) * n], share - step)
        own_pairs = (own_pairs.astype(f32) + theirs.astype(f32)).astype(bf16)
    acc_s, grad_temporal, class_part, sums_s = call(
        "spatial_qkv_back",
        partial(spatial_qkv_back_kernel, chunk_s),
        chunk_s.operands()
        + [(grad_query, "v"), (own_pairs, "v"), temporal, grad_spatial, choose, is_class, small]
        + [[[(a, "h") for a in side] for side in acc_s]],
        chunk_s.grads() + [(narrow, bf16, "v"), ((8, D), f32, "v"), ((8, D), f32, "v")],
        [((D, 3 * D), bf16), (wide, bf16), (narrow, bf16), ((D, n), bf16)]
        + [((D, 3 * D), bf16), (narrow, f32)],
        2,
        flops(6 * D),
        {8: 0},
    )
    acc_s, grad_temporal, class_part = meet(back_in, back_out, acc_s, grad_temporal, class_part)
    grad_temporal = pos_hop(grad_temporal)
    back_s = chunk_s.scatter(*acc_s)
    activated = meet(back_s, activated[0])
    for step in reversed(later):
        far = back_s.across(step)
    (result,) = call(
        "block_out",
        partial(block_out_kernel, chunk_out),
        chunk_out.operands() + [(tie(activated, far), "v"), spatial, small],
        [(narrow, bf16, "v")],
        [((FF, D), bf16), (narrow, f32)],
        1,
        flops(FF),
    )
    grad_temporal, class_part, result = meet(back_s, back_in, grad_temporal, class_part, result)
    back_s.across(0)
    back_in.along()
    class_sum = class_part[:CLIPS]
    class_sum = class_sum + send(class_sum, layout.within[0])
    grad_temporal = (grad_temporal, "v")
    acc_proj, grad_mixed_t, sums_t = call(
        "temporal_proj_back",
        partial(temporal_proj_back_kernel, chunk_t, chunk_proj),
        chunk_t.operands() + [grad_temporal, (projected, "v"), (mixed_t, "v")],
        chunk_proj.grads() + [(narrow, bf16, "v"), ((8, D), f32, "v")],
        [((D, D), bf16), ((D, D), bf16), (narrow, bf16), ((D, n), bf16), ((D, n), bf16)]
        + [((D, D), bf16), ((D, D), bf16)],
        4,
        flops(4 * D),
    )
    acc_proj, grad_mixed_t, class_sum, result = meet(
        back_s, back_in, acc_proj, grad_mixed_t, class_sum, result
    )
    back_proj = chunk_proj.scatter(*acc_proj)
    grad_mixed_t, result = meet(back_proj, back_in, grad_mixed_t, result)
    for step in reversed(later):
        back_proj.across(step)
    back_s.along()
    back_in.swap()
    result = pos_hop(result)
    class_sum = class_sum + send(class_sum, layout.within[1])
    acc_qkv, tokens_grad = call(
        "temporal_attention_back",
        partial(temporal_attention_back_kernel, chunk_t, chunk_qkv),
        chunk_t.operands()
        + [(packed_t, "v")]
        + ids_t
        + [(lse_t, "v"), (grad_mixed_t, "v"), (rows, "v"), grad_temporal, small]
        + [(grad_in_bias.reshape(D, 4).T, "v"), (sums_m, "v"), (sums_s, "v"), (sums_t, "v")],
        chunk_qkv.grads() + [(narrow, bf16, "v")],
        [((D, 3 * D), bf16), ((n, n), f32), (wide, bf16), (narrow, bf16), ((D, n), bf16)]
        + [((D, 3 * D), bf16), (narrow, f32), ((128, D), f32), ((D, SMALL), bf16)],
        3,
        flops(6 * D + 10 * n),
    )
    acc_qkv, tokens_grad, class_sum, result = meet(
        back_s, back_in, back_proj, acc_qkv, tokens_grad, class_sum, result
    )
    back_qkv = chunk_qkv.scatter(*acc_qkv)
    back_proj.across(0)
    for perm in layout.within[2:]:
        class_sum = class_sum + send(class_sum, perm)
    result, class_sum = meet(back_qkv, back_proj, result, class_sum)
    for step in reversed(later):
        back_qkv.across(step)
    back_s.swap()
    back_proj.along()
    block_out = from_temporal(result)
    class_grad = jnp.zeros((MB, CLIPS, D), f32)
    class_grad = lax.dynamic_update_index_in_dim(class_grad, class_sum, micro, 0)
    class_grad = class_grad + send(class_grad, layout.between[0])
    tokens_grad, class_grad, block_out = meet(
        back_qkv, back_s, back_proj, tokens_grad, class_grad, block_out
    )
    back_qkv.across(0)
    back_proj.swap()
    for perm in layout.between[1:]:
        class_grad = class_grad + send(class_grad, perm)
    tokens_grad, class_grad = meet(back_qkv, back_proj, tokens_grad, class_grad)
    back_qkv.along()
    tokens_grad = from_temporal(tokens_grad).astype(f32)
    tokens_grad = meet(back_qkv, tokens_grad)
    back_qkv.swap()

    (acc_out,) = back_out.finish(chunk_out.widths)
    (acc_in,) = back_in.finish(chunk_in.widths)
    acc_sqkv, acc_sproj = back_s.finish(chunk_s.widths)
    acc_tproj, acc_tfc = back_proj.finish(chunk_proj.widths)
    acc_tqkv, small_grads = back_qkv.finish(chunk_qkv.widths)
    return (
        block_out,
        tokens_grad,
        class_grad,
        acc_tqkv,
        acc_tproj,
        acc_tfc,
        acc_sqkv,
        acc_sproj,
        acc_in,
        acc_out,
        small_grads[:, :4].reshape(-1),
        small_grads[:, 4:7],
        small_grads[:, 7:10],
        small_grads[:, 10:18],
    )


def solution(mesh):
    rows = P(AXES, None)
    wide = P(None, "frame", "pos", None)
    placed = (wide, P(), P(), wide) + (rows,) * 7 + (P(AXES),) + (rows,) * 3
    return jax.shard_map(
        on_device,
        mesh=mesh,
        in_specs=placed,
        out_specs=(wide, wide, P()) + (rows,) * 7 + (P(AXES),) + (rows,) * 3,
        check_vma=False,
    )
```

time: 997 us -> 450 us (0.45)
  waiting for transfers between devices: 661 us -> 101 us
  Pallas kernels: 0 us -> 123 us
  matrix products: 118 us -> 0 us
  starting transfers between devices: 29.4 us -> 120 us
  blocking collectives: 65.1 us -> 0 us
  between operations: 15.7 us -> 3.09 us
    reduce_scatter x4 -> x0, waiting for transfers between devices: 442 us -> none  [the longest x1 116 us: on_device(): scatter(jnp.concatenate([acc_tqkv, acc_tproj, acc_tfc], axis=1)).astype(f32)]
    all_gather x4 -> x0, waiting for transfers between devices: 130 us -> none  [the longest x1 58.8 us: on_device(): w_out = gather(mlp_out)]
    pallas_call x0 -> x13, Pallas kernels: none -> 123 us  [call(): pl.pallas_call(kernel, out_shape=[jax.ShapeDtypeStruct(shape, kind) for s...]
    dot_general x35 -> x0, matrix products: 118 us -> none  [the longest x7 35.2 us: back_mul(): lax.dot_general(upstream, weight, (((1,), (1,)), ((), ())), preferred_ele...]
    ppermute x0 -> x88, starting transfers between devices: none -> 85.9 us  [send(): return lax.ppermute(values, AXES, perm)]
    ppermute x0 -> x88, waiting for transfers between devices: none -> 83.8 us  [send(): return lax.ppermute(values, AXES, perm)]
    psum x1 -> x0, waiting for transfers between devices: 50.1 us -> none  [on_device(): class_grad = lax.psum(class_all, AXES)]
    all_gather x1 -> x0, blocking collectives: 43.5 us -> none  [on_device(): small = gather(small).astype(f32)]
  transfers between devices with their start and end apart: 16 -> 96, of which waited for: 13 -> 28; matrix products, arithmetic and copies ran while one was open for 12% -> 10% of each run, Pallas kernels for 0% -> 28%
where the time goes in v3:
time: 450 us; the launch traced here: 442 us
  Pallas kernels  123 us (27%)
  starting transfers between devices  120 us (27%)
  waiting for transfers between devices  101 us (22%)
  local copies, waits for them, and re-layouts  65.7 us (15%)
  other arithmetic  30.1 us (7%)
    pallas_call x13, Pallas kernels, call(): pl.pallas_call(kernel, out_shape=[jax.ShapeDtypeStruct(shape, kind) for s...  123 us
    ppermute x88, starting transfers between devices, send(): return lax.ppermute(values, AXES, perm)  85.9 us
    ppermute x88, waiting for transfers between devices, send(): return lax.ppermute(values, AXES, perm)  83.8 us
    unnamed x263, local copies, waits for them, and re-layouts  43.2 us
    all_to_all x4, starting transfers between devices, pos_hop(): return lax.all_to_all(parts, 'pos', 0, 0, tiled=True).reshape(rows_count, D)  18 us
    all_to_all x4, starting transfers between devices, frame_hop(): return lax.all_to_all(values, 'frame', 0, 0, tiled=True)  15.8 us
    all_to_all x4, waiting for transfers between devices, frame_hop(): return lax.all_to_all(values, 'frame', 0, 0, tiled=True)  13.4 us
  transfers between devices with their start and end apart: 96, of which 28 were waited for; matrix products, arithmetic and copies ran while one was open for 10% of the time, Pallas kernels for 28%

profile of v3, /device:TPU:0, one launch (start us, length us, event | category | flops | bytes accessed | tf_op | source)
XLA Modules:
  0.0 442.0 jit_solution(2212670627109551513)
XLA Ops:
  10.5 4.7 %all-to-all-start = ((bf16[4,96,768]{2,1,0:T(8,128)(2,1)}), bf16[4,96,768]{2,1,0:T(8,128)(2,1)S(1)}, u32[]{:S(2)}, u32[]{:S(2)}) async-start(bf16[4,96,768]{2,1,0:T(8,128)(2,1)} %copy.60), calls=%async_computation | async-start | bytes 1179648 | tf_op jit(solution)/shard_map/all_to_all | solution.py:776
  20.0 6.2 %collective-permute-done.1 = bf16[48,2048]{1,0:T(8,128)(2,1)S(1)} collective-permute-done((bf16[48,2048]{1,0:T(8,128)(2,1)S(1)}, bf16[48,2048]{1,0:T(8,128)(2,1)S(1)}, u32[]{:S(2)}, u32[]{:S(2)}) %collective-permute-start.1) | collective-permute-done | bytes 196640 | tf_op jit(solution)/shard_map/ppermute | solution.py:24
  26.2 8.0 %collective-permute-done.2 = bf16[48,2048]{1,0:T(8,128)(2,1)S(1)} collective-permute-done((bf16[48,2048]{1,0:T(8,128)(2,1)S(1)}, bf16[48,2048]{1,0:T(8,128)(2,1)S(1)}, u32[]{:S(2)}, u32[]{:S(2)}) %collective-permute-start.2) | collective-permute-done | bytes 196640 | tf_op jit(solution)/shard_map/ppermute | solution.py:24
  45.5 8.1 %collective-permute-done.8 = bf16[48,1536]{1,0:T(8,128)(2,1)S(1)} collective-permute-done((bf16[48,1536]{1,0:T(8,128)(2,1)S(1)}, bf16[48,1536]{1,0:T(8,128)(2,1)S(1)}, u32[]{:S(2)}, u32[]{:S(2)}) %collective-permute-start.8) | collective-permute-done | bytes 147488 | tf_op jit(solution)/shard_map/ppermute | solution.py:24
  62.1 8.1 %collective-permute-done.13 = bf16[48,1536]{1,0:T(8,128)(2,1)S(1)} collective-permute-done((bf16[48,1536]{1,0:T(8,128)(2,1)S(1)}, bf16[48,1536]{1,0:T(8,128)(2,1)S(1)}, u32[]{:S(2)}, u32[]{:S(2)}) %collective-permute-start.13) | collective-permute-done | bytes 147488 | tf_op jit(solution)/shard_map/ppermute | solution.py:24
  70.2 4.0 collective-permute-done.11.refs_4_
  79.0 7.4 %collective-permute-done.19.refs_2_ = bf16[4,48,1536]{2,1,0:T(8,128)(2,1)} collective-permute-done((bf16[4,48,1536]{2,1,0:T(8,128)(2,1)S(1)}, bf16[4,48,1536]{2,1,0:T(8,128)(2,1)}, u32[]{:S(2)}, u32[]{:S(2)}) %collective-permute-start.19) | collective-permute-done | bytes 589856 | tf_op jit(solution)/shard_map/ppermute | solution.py:24
  90.5 4.2 all-to-all-start.2
  100.6 5.9 %temporal_qkv.1 = (bf16[384,2304]{1,0:T(8,128)(2,1)S(1)}, f32[32,768]{1,0:T(8,128)S(1)}) custom-call(s32[33]{0:T(128)S(1)} %pad_add_fusion.1.refs_0_.refs_9_, bf16[4,48,2048]{2,1,0:T(8,128)(2,1)S(1)} %pad_maximum_fusion.refs_1_, bf16[4,48,2048]{2,1,0:T(8,128)(2,1)S(1)} %collective-permute-done.6.refs_2_, ...), custom_call_target="tpu_custom_call" | custom-call | flops 1358954496 | bytes 8749188 | tf_op jit(solution)/shard_map/temporal_qkv/pallas_call | solution.py:283
  106.6 10.0 %temporal_mix.1 = (bf16[384,768]{1,0:T(8,128)(2,1)S(1)}, bf16[384,768]{1,0:T(8,128)(2,1)S(1)}, f32[16,384]{1,0:T(8,128)S(1)}, bf16[384,768]{1,0:T(8,128)(2,1)S(1)}) custom-call(s32[33]{0:T(128)S(1)} %pad_add_fusion.1.refs_0_.refs_9_, bf16[4,48,2048]{2,1,0:T(8,128)(2,1)S(1)} %pad_maximum_fusion.refs_1_, ...), custom_call_target="tpu_custom_call" | custom-call | flops 1811939328 | bytes 10546308 | tf_op jit(solution)/shard_map/temporal_mix/pallas_call | solution.py:283
  119.3 3.7 all-to-all-start.1
  127.0 7.2 %collective-permute-done.29.refs_2_ = bf16[4,48,1536]{2,1,0:T(8,128)(2,1)} collective-permute-done((bf16[4,48,1536]{2,1,0:T(8,128)(2,1)}, bf16[4,48,1536]{2,1,0:T(8,128)(2,1)}, u32[]{:S(2)}, u32[]{:S(2)}) %collective-permute-start.29) | collective-permute-done | bytes 589856 | tf_op jit(solution)/shard_map/ppermute | solution.py:24
  139.7 4.4 all-to-all-start.3
  152.8 5.0 %spatial_qkv.1 = (bf16[384,768]{1,0:T(8,128)(2,1)S(1)}, bf16[384,2304]{1,0:T(8,128)(2,1)S(1)}) custom-call(s32[33]{0:T(128)S(1)} %pad_add_fusion.1.refs_0_.refs_9_, bf16[4,48,1536]{2,1,0:T(8,128)(2,1)S(1)} %pad_maximum_fusion.1.refs_1_, bf16[4,48,1536]{2,1,0:T(8,128)(2,1)} %collective-permute-done.19.refs_2_, ...), custom_call_target="tpu_custom_call" | custom-call | flops 1358954496 | bytes 7786116 | tf_op jit(solution)/shard_map/spatial_qkv/pallas_call | solution.py:283
  157.9 8.7 %spatial_mix.1 = (bf16[384,768]{1,0:T(8,128)(2,1)S(1)}, f32[16,384]{1,0:T(8,128)S(1)}, f32[384,768]{1,0:T(8,128)S(1)}) custom-call(s32[33]{0:T(128)S(1)} %pad_add_fusion.1.refs_0_.refs_9_, bf16[4,48,1536]{2,1,0:T(8,128)(2,1)S(1)} %pad_maximum_fusion.1.refs_1_, bf16[4,48,1536]{2,1,0:T(8,128)(2,1)} %collective-permute-done.19.refs_2_, ...), custom_call_target="tpu_custom_call" | custom-call | flops 1358954496 | bytes 10742916 | tf_op jit(solution)/shard_map/spatial_mix/pallas_call | solution.py:283
  184.6 7.4 %hidden.1 = (bf16[384,768]{1,0:T(8,128)(2,1)S(1)}, bf16[384,3072]{1,0:T(8,128)(2,1)S(1)}, bf16[384,3072]{1,0:T(8,128)(2,1)S(1)}) custom-call(s32[33]{0:T(128)S(1)} %pad_add_fusion.1.refs_0_.refs_9_, bf16[4,48,1536]{2,1,0:T(8,128)(2,1)} %pad_maximum_fusion.2.refs_1_, bf16[4,48,1536]{2,1,0:T(8,128)(2,1)} %collective-permute-done.29.refs_2_, ...), custom_call_target="tpu_custom_call" | custom-call | flops 1811939328 | bytes 11317380 | tf_op jit(solution)/shard_map/hidden/pallas_call | solution.py:283
  192.0 7.6 %mlp_out_grad.1 = (bf16[8,192,384]{2,1,0:T(8,128)(2,1)S(1)}, bf16[8,192,384]{2,1,0:T(8,128)(2,1)S(1)}, bf16[8,192,384]{2,1,0:T(8,128)(2,1)S(1)}, bf16[8,192,384]{2,1,0:T(8,128)(2,1)S(1)}) custom-call(s32[33]{0:T(128)S(1)} %pad_add_fusion.1.refs_0_.refs_9_, bf16[384,3072]{1,0:T(8,128)(2,1)S(1)} %get-tuple-element.462.refs_1_.refs_9_, ...), custom_call_target="tpu_custom_call" | custom-call | flops 1811939328 | bytes 7667844 | tf_op jit(solution)/shard_map/mlp_out_grad/pallas_call | solution.py:283
  209.6 14.4 %mlp_back.1 = (bf16[384,3072]{1,0:T(8,128)(2,1)S(1)}, f32[1,3072]{1,0:T(1,128)S(1)}, f32[384,768]{1,0:T(8,128)S(1)}, f32[8,768]{1,0:T(8,128)S(1)}) custom-call(s32[33]{0:T(128)S(1)} %pad_add_fusion.1.refs_0_.refs_9_, bf16[4,48,1536]{2,1,0:T(8,128)(2,1)} %pad_maximum_fusion.2.refs_1_, bf16[4,48,1536]{2,1,0:T(8,128)(2,1)} %collective-permute-done.29.refs_2_, ...), custom_call_target="tpu_custom_call" | custom-call | flops 3623878656 | bytes 17240328 | tf_op jit(solution)/shard_map/mlp_back/pallas_call | solution.py:283
  225.3 6.6 %mlp_in_grad.1 = (bf16[8,48,1536]{2,1,0:T(8,128)(2,1)S(1)}, bf16[8,48,1536]{2,1,0:T(8,128)(2,1)S(1)}, bf16[8,48,1536]{2,1,0:T(8,128)(2,1)S(1)}, bf16[8,48,1536]{2,1,0:T(8,128)(2,1)S(1)}) custom-call(s32[33]{0:T(128)S(1)} %pad_add_fusion.1.refs_0_.refs_9_, bf16[384,768]{1,0:T(8,128)(2,1)S(1)} %get-tuple-element.403.refs_1_, ...), custom_call_target="tpu_custom_call" | custom-call | flops 1811939328 | bytes 7667844 | tf_op jit(solution)/shard_map/mlp_in_grad/pallas_call | solution.py:283
  245.9 13.0 %spatial_attention_back.1 = (bf16[8,48,1536]{2,1,0:T(8,128)(2,1)S(1)}, bf16[8,48,1536]{2,1,0:T(8,128)(2,1)S(1)}, bf16[8,48,1536]{2,1,0:T(8,128)(2,1)S(1)}, bf16[...) custom-call(s32[33]{0:T(128)S(1)} %pad_add_fusion.1.refs_0_.refs_9_, ...), custom_call_target="tpu_custom_call" | custom-call | flops 3170893824 | bytes 16542852 | tf_op jit(solution)/shard_map/spatial_attention_back/pallas_call | solution.py:283
  261.8 10.4 %spatial_qkv_back.1 = (bf16[8,48,1536]{2,1,0:T(8,128)(2,1)S(1)}, bf16[8,48,1536]{2,1,0:T(8,128)(2,1)S(1)}, bf16[8,48,1536]{2,1,0:T(8,128)(2,1)S(1)}, bf16[8,48,1...) custom-call(s32[33]{0:T(128)S(1)} %pad_add_fusion.1.refs_0_.refs_9_,, ...), custom_call_target="tpu_custom_call", output_to_operand_aliasing={{0}: (16, {}), {1}: (17, {}), {2}: (18, {}), {3}: (19, {})} | custom-call | flops 2717908992 | bytes 18439812 | tf_op jit(solution)/shard_map/spatial_qkv_back/pallas_call | solution.py:283
  279.0 5.4 %all-to-all-start.4 = ((bf16[8,48,768]{2,1,0:T(8,128)(2,1)}), bf16[8,48,768]{2,1,0:T(8,128)(2,1)}, u32[]{:S(2)}, u32[]{:S(2)}) async-start(bf16[8,48,768]{2,1,0:T(8,128)(2,1)} %bitcast.62), calls=%async_computation.4 | async-start | bytes 1179648 | tf_op jit(solution)/shard_map/all_to_all | solution.py:780
  292.8 6.2 %block_out.1 = bf16[384,768]{1,0:T(8,128)(2,1)S(1)} custom-call(s32[33]{0:T(128)S(1)} %pad_add_fusion.1.refs_0_.refs_9_, bf16[4,192,384]{2,1,0:T(8,128)(2,1)} %pad_maximum_fusion.3.refs_10_.refs_1_, bf16[4,192,384]{2,1,0:T(8,128)(2,1)} %collective-permute-done.36.refs_11_.refs_2_, bf16[4,192,384]{2,1,0:T(8,128)(2,1)} %collective-permute-done.37.refs_12_.refs_3_, ...), custom_call_target="tpu_custom_call" | custom-call | flops 1811939328 | bytes 8945796 | tf_op jit(solution)/shard_map/block_out/pallas_call | solution.py:283
  305.9 8.2 %temporal_proj_back.1 = (bf16[8,48,768]{2,1,0:T(8,128)(2,1)S(1)}, bf16[8,48,768]{2,1,0:T(8,128)(2,1)S(1)}, bf16[8,48,768]{2,1,0:T(8,128)(2,1)S(1)}, bf16[8,48,76...) custom-call(s32[33]{0:T(128)S(1)} %pad_add_fusion.1.refs_0_.refs_9_, ...), custom_call_target="tpu_custom_call" | custom-call | flops 1811939328 | bytes 11034756 | tf_op jit(solution)/shard_map/temporal_proj_back/pallas_call | solution.py:283
  320.2 3.5 collective-permute-done.59
  323.7 6.8 %collective-permute-done.60 = bf16[48,1536]{1,0:T(8,128)(2,1)S(1)} collective-permute-done((bf16[48,1536]{1,0:T(8,128)(2,1)S(1)}, bf16[48,1536]{1,0:T(8,128)(2,1)S(1)}, u32[]{:S(2)}, u32[]{:S(2)}) %collective-permute-start.60) | collective-permute-done | bytes 147488 | tf_op jit(solution)/shard_map/ppermute | solution.py:24
  342.0 4.6 %all-to-all-start.5 = ((bf16[8,48,768]{2,1,0:T(8,128)(2,1)}), bf16[8,48,768]{2,1,0:T(8,128)(2,1)}, u32[]{:S(2)}, u32[]{:S(2)}) async-start(bf16[8,48,768]{2,1,0:T(8,128)(2,1)} %bitcast.122), calls=%async_computation.5 | async-start | bytes 1179648 | tf_op jit(solution)/shard_map/all_to_all | solution.py:780
  349.8 19.2 %temporal_attention_back.1 = (bf16[8,48,1280]{2,1,0:T(8,128)(2,1)S(1)}, bf16[8,48,1280]{2,1,0:T(8,128)(2,1)S(1)}, bf16[8,48,1280]{2,1,0:T(8,128)(2,1)S(1)}, bf16...) custom-call(s32[33]{0:T(128)S(1)} %pad_add_fusion.1.refs_0_.refs_9_, bf16[4,48,2048]{2,1,0:T(8,128)(2,1)S(1)} %pad_maximum_fusion.refs_1_, ...), custom_call_target="tpu_custom_call" | custom-call | flops 4982833152 | bytes 14564484 | tf_op jit(solution)/shard_map/temporal_attention_back/pallas_call | solution.py:283
  387.0 3.5 all-to-all-start.6
  398.7 4.6 %all-to-all-done.6 = bf16[4,96,768]{2,1,0:T(8,128)(2,1)S(1)} async-done(((bf16[4,96,768]{2,1,0:T(8,128)(2,1)}), bf16[4,96,768]{2,1,0:T(8,128)(2,1)S(1)}, u32[]{:S(2)}, u32[]{:S(2)}) %all-to-all-start.6) | async-done | bytes 589856 | tf_op jit(solution)/shard_map/all_to_all | solution.py:776
  422.1 3.5 all-to-all-start.7
  425.7 8.8 %all-to-all-done.7 = bf16[4,96,768]{2,1,0:T(8,128)(2,1)S(1)} async-done(((bf16[4,96,768]{2,1,0:T(8,128)(2,1)}), bf16[4,96,768]{2,1,0:T(8,128)(2,1)S(1)}, u32[]{:S(2)}, u32[]{:S(2)}) %all-to-all-start.7) | async-done | bytes 589856 | tf_op jit(solution)/shard_map/all_to_all | solution.py:776
  (579 shorter events, 209.8 us)
Async XLA Ops:
  10.5 23.7 %all-to-all-start = ((bf16[4,96,768]{2,1,0:T(8,128)(2,1)}), bf16[4,96,768]{2,1,0:T(8,128)(2,1)S(1)}, u32[]{:S(2)}, u32[]{:S(2)}) async-start(bf16[4,96,768]{2,1,0:T(8,128)(2,1)} %copy.60), calls=%async_computation | async-start | bytes 1179648 | tf_op jit(solution)/shard_map/all_to_all | solution.py:776
  17.1 17.1 %collective-permute-start.2 = (bf16[48,2048]{1,0:T(8,128)(2,1)S(1)}, bf16[48,2048]{1,0:T(8,128)(2,1)S(1)}, u32[]{:S(2)}, u32[]{:S(2)}) collective-permute-start(bf16[48,2048]{1,0:T(8,128)(2,1)S(1)} %pad_maximum_fusion.8), channel_id=1, source_target_pairs={{0,4},{1,5},{2,6},{3,7},{4,0},{5,1},{6,2},{7,3},{8,12},{9,13},{10,... | collective-permute-start | bytes 589832 | tf_op jit(solution)/shard_map/ppermute | solution.py:24
  35.1 18.4 %collective-permute-start.6 = (bf16[4,48,2048]{2,1,0:T(8,128)(2,1)S(1)}, bf16[4,48,2048]{2,1,0:T(8,128)(2,1)S(1)}, u32[]{:S(2)}, u32[]{:S(2)}) collective-permute-start(bf16[4,48,2048]{2,1,0:T(8,128)(2,1)S(1)} %pad_maximum_fusion.refs_1_), channel_id=1, source_target_pairs={{0,8},{1,17},{2,10},{3,19},{4,12},{5,21},{6,14},{7,23},{8,0},{9,25... | collective-permute-start | bytes 2359304 | tf_op jit(solution)/shard_map/ppermute | solution.py:24
  54.3 19.9 %collective-permute-start.11 = (bf16[4,48,2048]{2,1,0:T(8,128)(2,1)S(1)}, bf16[4,48,2048]{2,1,0:T(8,128)(2,1)}, u32[]{:S(2)}, u32[]{:S(2)}) collective-permute-start(bf16[4,48,2048]{2,1,0:T(8,128)(2,1)S(1)} %collective-permute-done.6.refs_2_), channel_id=1, source_target_pairs={{0,16},{1,9},{2,18},{3,11},{4,20},{5,13},{6,22},{7,15},{8,24},{9,1... | collective-permute-start | bytes 2359304 | tf_op jit(solution)/shard_map/ppermute | solution.py:24
  86.4 32.0 %collective-permute-start.20 = (bf16[4,48,1536]{2,1,0:T(8,128)(2,1)S(1)}, bf16[4,48,1536]{2,1,0:T(8,128)(2,1)}, u32[]{:S(2)}, u32[]{:S(2)}) collective-permute-start(bf16[4,48,1536]{2,1,0:T(8,128)(2,1)S(1)} %pad_maximum_fusion.1.refs_1_), channel_id=1, source_target_pairs={{0,16},{1,9},{2,18},{3,11},{4,20},{5,13},{6,22},{7,15},{8,24},{9,1... | collective-permute-start | bytes 1769480 | tf_op jit(solution)/shard_map/ppermute | solution.py:24
  87.1 32.1 %collective-permute-start.21 = (bf16[4,48,1536]{2,1,0:T(8,128)(2,1)}, bf16[4,48,1536]{2,1,0:T(8,128)(2,1)}, u32[]{:S(2)}, u32[]{:S(2)}) collective-permute-start(bf16[4,48,1536]{2,1,0:T(8,128)(2,1)} %collective-permute-done.19.refs_2_), channel_id=1, source_target_pairs={{0,16},{1,9},{2,18},{3,11},{4,20},{5,13},{6,22},{7,15},{8,24},{9,1... | collective-permute-start | bytes 1769480 | tf_op jit(solution)/shard_map/ppermute | solution.py:24
  90.5 28.8 %all-to-all-start.2 = ((bf16[4,96,768]{2,1,0:T(8,128)(2,1)}), bf16[4,96,768]{2,1,0:T(8,128)(2,1)}, u32[]{:S(2)}, u32[]{:S(2)}) async-start(bf16[4,96,768]{2,1,0:T(8,128)(2,1)} %pad_bitcast_fusion), calls=%async_computation.2 | async-start | bytes 1179648 | tf_op jit(solution)/shard_map/all_to_all | solution.py:776
  94.9 23.4 %collective-permute-start.22 = (bf16[192,384]{1,0:T(8,128)(2,1)S(1)}, bf16[192,384]{1,0:T(8,128)(2,1)S(1)}, u32[]{:S(2)}, u32[]{:S(2)}) collective-permute-start(bf16[192,384]{1,0:T(8,128)(2,1)S(1)} %pad_maximum_fusion.12), channel_id=1, source_target_pairs={{0,2},{1,3},{2,0},{3,1},{4,6},{5,7},{6,4},{7,5},{8,10},{9,11},{10,... | collective-permute-start | bytes 442376 | tf_op jit(solution)/shard_map/ppermute | solution.py:24
  97.1 21.3 %collective-permute-start.23 = (bf16[192,384]{1,0:T(8,128)(2,1)S(1)}, bf16[192,384]{1,0:T(8,128)(2,1)S(1)}, u32[]{:S(2)}, u32[]{:S(2)}) collective-permute-start(bf16[192,384]{1,0:T(8,128)(2,1)S(1)} %pad_maximum_fusion.12), channel_id=1, source_target_pairs={{0,4},{1,5},{2,6},{3,7},{4,0},{5,1},{6,2},{7,3},{8,12},{9,13},{10,... | collective-permute-start | bytes 442376 | tf_op jit(solution)/shard_map/ppermute | solution.py:24
  98.2 20.3 %collective-permute-start.24 = (bf16[192,384]{1,0:T(8,128)(2,1)S(1)}, bf16[192,384]{1,0:T(8,128)(2,1)S(1)}, u32[]{:S(2)}, u32[]{:S(2)}) collective-permute-start(bf16[192,384]{1,0:T(8,128)(2,1)S(1)} %pad_maximum_fusion.12), channel_id=1, source_target_pairs={{0,6},{1,7},{2,4},{3,5},{4,2},{5,3},{6,0},{7,1},{8,14},{9,15},{10,... | collective-permute-start | bytes 442376 | tf_op jit(solution)/shard_map/ppermute | solution.py:24
  119.3 20.4 %all-to-all-start.1 = ((bf16[8,48,768]{2,1,0:T(8,128)(2,1)}), bf16[8,48,768]{2,1,0:T(8,128)(2,1)S(1)}, u32[]{:S(2)}, u32[]{:S(2)}) async-start(bf16[8,48,768]{2,1,0:T(8,128)(2,1)} %bitcast.124), calls=%async_computation.1 | async-start | bytes 1179648 | tf_op jit(solution)/shard_map/all_to_all | solution.py:780
  139.7 29.4 %all-to-all-start.3 = ((bf16[8,48,768]{2,1,0:T(8,128)(2,1)}), bf16[8,48,768]{2,1,0:T(8,128)(2,1)}, u32[]{:S(2)}, u32[]{:S(2)}) async-start(bf16[8,48,768]{2,1,0:T(8,128)(2,1)} %bitcast.51), calls=%async_computation.3 | async-start | bytes 1179648 | tf_op jit(solution)/shard_map/all_to_all | solution.py:780
  144.4 24.8 %collective-permute-start.30 = (bf16[4,48,1536]{2,1,0:T(8,128)(2,1)}, bf16[4,48,1536]{2,1,0:T(8,128)(2,1)}, u32[]{:S(2)}, u32[]{:S(2)}) collective-permute-start(bf16[4,48,1536]{2,1,0:T(8,128)(2,1)} %pad_maximum_fusion.2.refs_1_), channel_id=1, source_target_pairs={{0,16},{1,9},{2,18},{3,11},{4,20},{5,13},{6,22},{7,15},{8,24},{9,1... | collective-permute-start | bytes 1769480 | tf_op jit(solution)/shard_map/ppermute | solution.py:24
  146.4 22.7 %collective-permute-start.31 = (bf16[4,48,1536]{2,1,0:T(8,128)(2,1)}, bf16[4,48,1536]{2,1,0:T(8,128)(2,1)}, u32[]{:S(2)}, u32[]{:S(2)}) collective-permute-start(bf16[4,48,1536]{2,1,0:T(8,128)(2,1)} %collective-permute-done.29.refs_2_), channel_id=1, source_target_pairs={{0,16},{1,9},{2,18},{3,11},{4,20},{5,13},{6,22},{7,15},{8,24},{9,1... | collective-permute-start | bytes 1769480 | tf_op jit(solution)/shard_map/ppermute | solution.py:24
  147.7 22.6 %collective-permute-start.36 = (bf16[4,192,384]{2,1,0:T(8,128)(2,1)}, bf16[4,192,384]{2,1,0:T(8,128)(2,1)}, u32[]{:S(2)}, u32[]{:S(2)}) collective-permute-start(bf16[4,192,384]{2,1,0:T(8,128)(2,1)} %pad_maximum_fusion.3.refs_10_.refs_1_), channel_id=1, source_target_pairs={{0,8},{1,17},{2,10},{3,19},{4,12},{5,21},{6,14},{7,23},{8,0},{9,25... | collective-permute-start | bytes 1769480 | tf_op jit(solution)/shard_map/ppermute | solution.py:24
  174.8 24.8 %collective-permute-start.37 = (bf16[4,192,384]{2,1,0:T(8,128)(2,1)}, bf16[4,192,384]{2,1,0:T(8,128)(2,1)}, u32[]{:S(2)}, u32[]{:S(2)}) collective-permute-start(bf16[4,192,384]{2,1,0:T(8,128)(2,1)} %pad_maximum_fusion.3.refs_10_.refs_1_), channel_id=1, source_target_pairs={{0,16},{1,9},{2,18},{3,11},{4,20},{5,13},{6,22},{7,15},{8,24},{9,1... | collective-permute-start | bytes 1769480 | tf_op jit(solution)/shard_map/ppermute | solution.py:24
  176.3 23.3 %collective-permute-start.38 = (bf16[4,192,384]{2,1,0:T(8,128)(2,1)}, bf16[4,192,384]{2,1,0:T(8,128)(2,1)}, u32[]{:S(2)}, u32[]{:S(2)}) collective-permute-start(bf16[4,192,384]{2,1,0:T(8,128)(2,1)} %collective-permute-done.36.refs_11_.refs_2_), channel_id=1, source_target_pairs={{0,16},{1,9},{2,18},{3,11},{4,20},{5,13},{6,22},{7,15},{8,24},{9,1... | collective-permute-start | bytes 1769480 | tf_op jit(solution)/shard_map/ppermute | solution.py:24
  239.3 19.6 %collective-permute-start.49 = (bf16[8,48,1536]{2,1,0:T(8,128)(2,1)S(1)}, bf16[8,48,1536]{2,1,0:T(8,128)(2,1)S(1)}, u32[]{:S(2)}, u32[]{:S(2)}) collective-permute-start(bf16[8,48,1536]{2,1,0:T(8,128)(2,1)S(1)} %add_convert_fusion.1), channel_id=1, source_target_pairs={{0,16},{1,9},{2,18},{3,11},{4,20},{5,13},{6,22},{7,15},{8,24},{9,1... | collective-permute-start | bytes 3538952 | tf_op jit(solution)/shard_map/ppermute | solution.py:24
  241.3 17.6 %collective-permute-start.50 = (bf16[192,384]{1,0:T(8,128)(2,1)S(1)}, bf16[192,384]{1,0:T(8,128)(2,1)S(1)}, u32[]{:S(2)}, u32[]{:S(2)}) collective-permute-start(bf16[192,384]{1,0:T(8,128)(2,1)S(1)} %get-tuple-element.632), channel_id=1, source_target_pairs={{0,2},{1,3},{2,0},{3,1},{4,6},{5,7},{6,4},{7,5},{8,10},{9,11},{10,... | collective-permute-start | bytes 442376 | tf_op jit(solution)/shard_map/ppermute | solution.py:24
  278.3 22.9 %collective-permute-start.57 = (bf16[8,48,1536]{2,1,0:T(8,128)(2,1)}, bf16[8,48,1536]{2,1,0:T(8,128)(2,1)}, u32[]{:S(2)}, u32[]{:S(2)}) collective-permute-start(bf16[8,48,1536]{2,1,0:T(8,128)(2,1)} %add_convert_fusion), channel_id=1, source_target_pairs={{0,16},{1,9},{2,18},{3,11},{4,20},{5,13},{6,22},{7,15},{8,24},{9,1... | collective-permute-start | bytes 3538952 | tf_op jit(solution)/shard_map/ppermute | solution.py:24
  279.0 22.2 %all-to-all-start.4 = ((bf16[8,48,768]{2,1,0:T(8,128)(2,1)}), bf16[8,48,768]{2,1,0:T(8,128)(2,1)}, u32[]{:S(2)}, u32[]{:S(2)}) async-start(bf16[8,48,768]{2,1,0:T(8,128)(2,1)} %bitcast.62), calls=%async_computation.4 | async-start | bytes 1179648 | tf_op jit(solution)/shard_map/all_to_all | solution.py:780
  302.8 27.6 %collective-permute-start.58 = (bf16[4,48,1536]{2,1,0:T(8,128)(2,1)S(1)}, bf16[4,48,1536]{2,1,0:T(8,128)(2,1)S(1)}, u32[]{:S(2)}, u32[]{:S(2)}) collective-permute-start(bf16[4,48,1536]{2,1,0:T(8,128)(2,1)S(1)} %add_convert_fusion.5), channel_id=1, source_target_pairs={{0,8},{1,17},{2,10},{3,19},{4,12},{5,21},{6,14},{7,23},{8,0},{9,25... | collective-permute-start | bytes 1769480 | tf_op jit(solution)/shard_map/ppermute | solution.py:24
  335.2 37.7 %collective-permute-start.63 = (bf16[48,1536]{1,0:T(8,128)(2,1)}, bf16[48,1536]{1,0:T(8,128)(2,1)}, u32[]{:S(2)}, u32[]{:S(2)}) collective-permute-start(bf16[48,1536]{1,0:T(8,128)(2,1)} %get-tuple-element.626), channel_id=1, source_target_pairs={{0,2},{1,3},{2,0},{3,1},{4,6},{5,7},{6,4},{7,5},{8,10},{9,11},{10,... | collective-permute-start | bytes 442376 | tf_op jit(solution)/shard_map/ppermute | solution.py:24
  335.2 37.7 %collective-permute-start.64 = (bf16[48,1536]{1,0:T(8,128)(2,1)}, bf16[48,1536]{1,0:T(8,128)(2,1)}, u32[]{:S(2)}, u32[]{:S(2)}) collective-permute-start(bf16[48,1536]{1,0:T(8,128)(2,1)} %get-tuple-element.625), channel_id=1, source_target_pairs={{0,4},{1,5},{2,6},{3,7},{4,0},{5,1},{6,2},{7,3},{8,12},{9,13},{10,... | collective-permute-start | bytes 442376 | tf_op jit(solution)/shard_map/ppermute | solution.py:24
  338.1 34.8 %collective-permute-start.65 = (bf16[48,1536]{1,0:T(8,128)(2,1)}, bf16[48,1536]{1,0:T(8,128)(2,1)}, u32[]{:S(2)}, u32[]{:S(2)}) collective-permute-start(bf16[48,1536]{1,0:T(8,128)(2,1)} %get-tuple-element.624), channel_id=1, source_target_pairs={{0,6},{1,7},{2,4},{3,5},{4,2},{5,3},{6,0},{7,1},{8,14},{9,15},{10,... | collective-permute-start | bytes 442376 | tf_op jit(solution)/shard_map/ppermute | solution.py:24
  340.6 32.3 %collective-permute-start.69 = (bf16[8,48,768]{2,1,0:T(8,128)(2,1)}, bf16[8,48,768]{2,1,0:T(8,128)(2,1)}, u32[]{:S(2)}, u32[]{:S(2)}) collective-permute-start(bf16[8,48,768]{2,1,0:T(8,128)(2,1)} %add_convert_fusion.4), channel_id=1, source_target_pairs={{0,16},{1,9},{2,18},{3,11},{4,20},{5,13},{6,22},{7,15},{8,24},{9,1... | collective-permute-start | bytes 1769480 | tf_op jit(solution)/shard_map/ppermute | solution.py:24
  342.0 31.0 %all-to-all-start.5 = ((bf16[8,48,768]{2,1,0:T(8,128)(2,1)}), bf16[8,48,768]{2,1,0:T(8,128)(2,1)}, u32[]{:S(2)}, u32[]{:S(2)}) async-start(bf16[8,48,768]{2,1,0:T(8,128)(2,1)} %bitcast.122), calls=%async_computation.5 | async-start | bytes 1179648 | tf_op jit(solution)/shard_map/all_to_all | solution.py:780
  347.8 25.1 %collective-permute-start.68 = (f32[24,1536]{1,0:T(8,128)S(1)}, f32[24,1536]{1,0:T(8,128)}, u32[]{:S(2)}, u32[]{:S(2)}) collective-permute-start(f32[24,1536]{1,0:T(8,128)S(1)} %get-tuple-element.647), channel_id=1, source_target_pairs={{0,1},{1,0},{2,3},{3,2},{4,5},{5,4},{6,7},{7,6},{8,9},{9,8},{10,11... | collective-permute-start | bytes 442376 | tf_op jit(solution)/shard_map/ppermute | solution.py:24
  379.9 24.5 %collective-permute-start.76 = (f32[24,1536]{1,0:T(8,128)}, f32[24,1536]{1,0:T(8,128)}, u32[]{:S(2)}, u32[]{:S(2)}) collective-permute-start(f32[24,1536]{1,0:T(8,128)} %get-tuple-element.645), channel_id=1, source_target_pairs={{0,1},{1,0},{2,3},{3,2},{4,5},{5,4},{6,7},{7,6},{8,9},{9,8},{10,11... | collective-permute-start | bytes 442376 | tf_op jit(solution)/shard_map/ppermute | solution.py:24
  383.7 20.9 %collective-permute-start.75 = (bf16[8,48,1280]{2,1,0:T(8,128)(2,1)S(1)}, bf16[8,48,1280]{2,1,0:T(8,128)(2,1)}, u32[]{:S(2)}, u32[]{:S(2)}) collective-permute-start(bf16[8,48,1280]{2,1,0:T(8,128)(2,1)S(1)} %add_convert_fusion.3), channel_id=1, source_target_pairs={{0,16},{1,9},{2,18},{3,11},{4,20},{5,13},{6,22},{7,15},{8,24},{9,1... | collective-permute-start | bytes 2949128 | tf_op jit(solution)/shard_map/ppermute | solution.py:24
  417.6 18.4 %collective-permute-start.84 = (bf16[48,1280]{1,0:T(8,128)(2,1)S(1)}, bf16[48,1280]{1,0:T(8,128)(2,1)S(1)}, u32[]{:S(2)}, u32[]{:S(2)}) collective-permute-start(bf16[48,1280]{1,0:T(8,128)(2,1)S(1)} %get-tuple-element.635), channel_id=1, source_target_pairs={{0,2},{1,3},{2,0},{3,1},{4,6},{5,7},{6,4},{7,5},{8,10},{9,11},{10,... | collective-permute-start | bytes 368648 | tf_op jit(solution)/shard_map/ppermute | solution.py:24
  418.0 18.0 %collective-permute-start.85 = (bf16[48,1280]{1,0:T(8,128)(2,1)S(1)}, bf16[48,1280]{1,0:T(8,128)(2,1)S(1)}, u32[]{:S(2)}, u32[]{:S(2)}) collective-permute-start(bf16[48,1280]{1,0:T(8,128)(2,1)S(1)} %get-tuple-element.634), channel_id=1, source_target_pairs={{0,4},{1,5},{2,6},{3,7},{4,0},{5,1},{6,2},{7,3},{8,12},{9,13},{10,... | collective-permute-start | bytes 368648 | tf_op jit(solution)/shard_map/ppermute | solution.py:24
  (198 other events, 1686.3 us)
